TPU v7x, 1024 devices: a whole 8x8x8 slice. The times are simulated.
1024 devices in a mesh: dp: 32 (over x, y_lo, core), tensor: 32 (over z, y_hi).
Axes of the slice: x: 8, y: 8 (y_hi: 4, y_lo: 2; y = y_hi * 2 + y_lo), z: 8, core: 2. Of those that a mesh axis runs over, the one named last changes fastest.
Arguments:
- activations: bfloat16 [4096, 8192], P('dp', 'tensor'), may hold values from -56 to 56
- w_query: bfloat16 [8192, 8192], P(None, 'tensor'), may hold values from -0.0625 to 0.0625
- w_keyval: bfloat16 [8192, 2048], P(None, 'tensor'), may hold values from -0.0625 to 0.0625
- w_out: bfloat16 [8192, 8192], P('tensor'), may hold values from -0.0625 to 0.0625
- targets: int32 [1024], replicated, may hold values from 0 to 2047, as said below
- segments: int32 [5120], P('dp'), may hold values from -64 to 100003, as said below
Outputs:
- mixed: bfloat16 [5120, 8192], P('dp', 'tensor')
Inputs may be any that keep to these rules, and one draw needn't show every extreme that they name: All entries differ. targets // 64 is a destination block, never the source block s of entry s * 32 + m, and targets % 64 is a slot below 64; each source's tail is a run of four documents, each going whole to its own destination and landing in consecutive slots in order; every slot of some destination blocks, the last block among them, is used. In every block the arriving documents fill slots from 0 without gaps. `segments`: labels of the first 96 rows of a block are small positive numbers, those of arriving documents 100000 and up, and every unused arriving slot t carries -(t + 1); labels match the documents that targets places.
All inputs are finite; a program needn't handle non-finite values.
Results may differ from a plain program's by a relative error of at most 0.02.
Values may be sent and summed in bfloat16 or wider, within the bound.
No kernel may reach another device: no remote copies, remote signals or barrier semaphores. Data moves between devices by JAX's collectives and lax.ppermute only.
A program may use at most 32 MiB of HBM per device.

v0:
```python
import math

import jax
import jax.numpy as jnp
from jax import lax
from jax.sharding import PartitionSpec as P

HQ = 64
KVH = 8
HD = 128
KEEP = 96
RECV = 64
ROWS_BAL = 160


rope_base = 500000.0


def rotation_tables(positions):
    half = HD // 2
    freqs = rope_base ** (-(jnp.arange(half, dtype=jnp.float32) * 2.0 / HD))
    angles = positions.astype(jnp.float32)[:, None] * freqs[None, :]
    return (jnp.cos(angles), jnp.sin(angles))


def rotate(values, cosine, sine):
    half = HD // 2
    first = values[..., :half]
    second = values[..., half:]
    cosine = cosine[:, None, :]
    sine = sine[:, None, :]
    return jnp.concatenate(
        [first * cosine - second * sine, second * cosine + first * sine], axis=-1
    )


def doc_layout(segment):
    same = segment[:, None] == segment[None, :]
    indices = jnp.arange(segment.shape[0])
    earlier = indices[None, :] < indices[:, None]
    positions = jnp.sum(jnp.logical_and(same, earlier), axis=1)
    visible = jnp.logical_and(same, indices[None, :] <= indices[:, None])
    return (positions, visible)


def attend(query_rot, key_rot, value_rows, visible):
    count = query_rot.shape[0]
    scores = jnp.einsum(
        "rkgd,ckd->kgrc", query_rot, key_rot, preferred_element_type=jnp.float32
    ) / math.sqrt(HD)
    scores = jnp.where(visible[None, None], scores, -1e30)
    top = jnp.max(scores, axis=-1, keepdims=True)
    expd = jnp.exp(scores - top)
    weights = (expd / jnp.sum(expd, axis=-1, keepdims=True)).astype(jnp.bfloat16)
    result = jnp.einsum("kgrc,ckd->rkgd", weights, value_rows, preferred_element_type=jnp.float32)
    return result.astype(jnp.bfloat16).reshape(count, -1)


def shards(activations, w_query, w_keyval, w_out, targets, segments):
    query_cols = w_query.shape[1]
    block_index = lax.axis_index("dp")
    slot_ids = lax.iota(jnp.int32, RECV)
    kept_rows = activations[:KEEP]
    tail_rows = activations[KEEP:]
    wanted = targets - block_index * RECV
    select = (slot_ids[:, None] == wanted[None, :]).astype(jnp.bfloat16)
    arrived = jnp.dot(
        select,
        lax.all_gather(tail_rows, "dp", axis=0, tiled=True),
        preferred_element_type=jnp.float32,
    ).astype(jnp.bfloat16)
    balanced = jnp.concatenate([kept_rows, arrived], axis=0)
    piece = lax.all_gather(balanced, "tensor", axis=1, tiled=True)
    query_acc = jnp.dot(piece, w_query, preferred_element_type=jnp.float32)
    keyval_acc = jnp.dot(piece, w_keyval, preferred_element_type=jnp.float32)
    keyval_part = keyval_acc.astype(jnp.bfloat16)
    keyval_all = lax.all_gather(keyval_part, "tensor", axis=1, tiled=True)
    positions, visible = doc_layout(segments)
    cosine, sine = rotation_tables(positions)
    heads_local = query_cols // HD
    group = HQ // KVH
    kv_local = max(1, heads_local // group)
    kv_first = lax.axis_index("tensor") * heads_local // group
    query_rot = rotate(query_acc.reshape(ROWS_BAL, heads_local, HD), cosine, sine).astype(
        jnp.bfloat16
    )
    query_rot = query_rot.reshape(ROWS_BAL, kv_local, heads_local // kv_local, HD)
    key_raw = keyval_all[:, : KVH * HD].reshape(ROWS_BAL, KVH, HD)
    value_all = keyval_all[:, KVH * HD :].reshape(ROWS_BAL, KVH, HD)
    key_chosen = lax.dynamic_slice_in_dim(key_raw, kv_first, kv_local, 1)
    value_chosen = lax.dynamic_slice_in_dim(value_all, kv_first, kv_local, 1)
    key_rot = rotate(key_chosen.astype(jnp.float32), cosine, sine).astype(jnp.bfloat16)
    attended = attend(query_rot, key_rot, value_chosen, visible)
    summed = lax.psum_scatter(
        lax.dot_general(
            w_out, attended, (((0,), (1,)), ((), ())), preferred_element_type=jnp.float32
        ).astype(jnp.bfloat16),
        "tensor",
        scatter_dimension=0,
        tiled=True,
    ).astype(jnp.float32)
    return summed.T.astype(jnp.bfloat16)


def solution(mesh):
    placed = (
        P("dp", "tensor"),
        P(None, "tensor"),
        P(None, "tensor"),
        P("tensor", None),
        P(),
        P("dp"),
    )
    return jax.shard_map(
        shards, mesh=mesh, in_specs=placed, out_specs=P("dp", "tensor"), check_vma=False
    )
```

profile of v0, /device:TPU:1, one launch (start us, length us, event | category | flops | bytes accessed | tf_op | source)
XLA Modules:
  0.0 481.6 jit_solution(2094344096674784927)
XLA Ops:
  6.5 0.0 copy-start
  6.5 0.0 all-gather.2.cloned.1.call-start
  6.5 0.8 slice.25
  7.3 0.8 slice.24
  8.1 45.8 %all_gather.9 = bf16[1024,256]{1,0:T(8,128)(2,1)S(1)} all-gather(bf16[32,256]{1,0:T(8,128)(2,1)S(1)} %slice.25), channel_id=1, replica_groups=mesh['dp'=32,'tensor'=32] {'dp'}, dimensions={0}, use_global_device_ids=true | all-gather | bytes 540672 | tf_op jit(solution)/shard_map/all_gather | solution.py:69
  53.9 0.7 broadcast_subtract_fusion
  54.6 0.2 convolution_convert_fusion.3
  54.8 0.6 pad_maximum_fusion
  55.5 0.0 all-gather.2.cloned.1.call-update
  55.5 0.0 reduce-scatter.2.cloned.1.call-start
  55.6 0.9 convert_reduce_fusion
  56.4 0.8 compare_and_fusion.1
  57.3 0.4 multiply_cosine_fusion
  57.7 91.1 %all-gather.2.cloned.1.call-done = bf16[160,8192]{1,0:T(8,128)(2,1)} async-done(((bf16[160,256]{1,0:T(8,128)(2,1)}), bf16[160,8192]{1,0:T(8,128)(2,1)}) %all-gather.2.cloned.1.call-update) | async-done | bytes 2621456 | tf_op jit(solution)/shard_map/all_gather | solution.py:73
  148.7 3.8 fusion.31
  152.6 0.1 reshape.203
  152.7 0.2 fusion.29
  152.9 0.0 copy-done
  152.9 2.7 convolution_convert_fusion.2
  155.6 72.6 %all_gather.11 = bf16[160,2048]{0,1:T(8,128)(2,1)S(1)} all-gather(bf16[160,64]{0,1:T(8,128)(2,1)S(1)} %convolution_convert_fusion.2), channel_id=1, replica_groups=mesh['dp'=32,'tensor'=32] {'tensor'}, dimensions={1}, use_global_device_ids=true | all-gather | bytes 675840 | tf_op jit(solution)/shard_map/all_gather | solution.py:77
  228.2 0.1 fusion.28
  228.3 0.1 copy.19
  228.4 0.4 fusion.25
  228.9 0.3 fusion.30
  229.2 0.1 fusion.4
  229.3 0.3 fusion.3
  229.5 0.1 copy.17
  229.6 4.6 fusion
  234.2 0.0 reduce-scatter.2.cloned.1.call-update
  234.2 240.5 %reduce-scatter.2.cloned.1.call-done = bf16[256,160]{0,1:T(8,128)(2,1)} async-done(((bf16[8192,160]{0,1:T(8,128)(2,1)}), bf16[256,160]{0,1:T(8,128)(2,1)}) %reduce-scatter.2.cloned.1.call-update) | async-done | bytes 81936 | tf_op jit(solution)/shard_map/reduce_scatter | solution.py:94
  (5 shorter events, 0.1 us)
Async XLA Ops:
  6.5 146.4 %copy-start = (bf16[8192,64]{0,1:T(8,128)(2,1)S(1)}, bf16[8192,64]{0,1:T(8,128)(2,1)}, u32[]{:S(2)}) copy-start(bf16[8192,64]{0,1:T(8,128)(2,1)} %param.8) | copy-start | bytes 3145732
  6.5 142.2 %all-gather.2.cloned.1.call-start = ((), (), s32[]{:S(2)}) async-start(), calls=%async_computation.1 | async-start | bytes 2703360 | tf_op jit(solution)/shard_map/all_gather | solution.py:73
  55.5 419.2 %reduce-scatter.2.cloned.1.call-start = ((), (), s32[]{:S(2)}) async-start(), calls=%async_computation.2 | async-start | bytes 2703360 | tf_op jit(solution)/shard_map/reduce_scatter | solution.py:94
Sparse Core Ops, SparseCore 0:
  55.6 93.0 all-gather.1
  234.3 240.3 reduce-scatter.1
where the time goes:
time: 486 us; the launch traced here: 482 us
  waiting for transfers between devices  332 us (68%)
  blocking collectives  118 us (24%)
  between operations  13.5 us (3%)
  matrix products  11.9 us (2%)
    reduce_scatter x1, waiting for transfers between devices, shards(): lax.psum_scatter(lax.dot_general(w_out, attended, (((0,), (1,)), ((), ())...  241 us
    all_gather x1, waiting for transfers between devices, shards(): piece = lax.all_gather(balanced, 'tensor', axis=1, tiled=True)  91.1 us
    all_gather x1, blocking collectives, shards(): keyval_all = lax.all_gather(keyval_part, 'tensor', axis=1, tiled=True)  72.6 us
    all_gather x1, blocking collectives, shards(): lax.all_gather(tail_rows, 'dp', axis=0, tiled=True)  45.8 us
  transfers between devices with their start and end apart: 2, of which 2 were waited for; matrix products, arithmetic and copies ran while one was open for 0% of the time, Pallas kernels for 0%

commit v1 on v0

v1 whole, which is shorter than its diff:
```python
import math

import jax
import jax.numpy as jnp
from jax import lax
from jax.sharding import Mesh
from jax.sharding import PartitionSpec as P

HQ = 64
KVH = 8
HD = 128
KEEP = 96
MOVE = 32
RECV = 64
SEQ = 128

N_Z = 8
N_Y = 4
DP = ("x", "yl", "core")
TENSOR = ("z", "yh")

rope_base = 500000.0


def rotation_tables(positions):
    half = HD // 2
    freqs = rope_base ** (-(jnp.arange(half, dtype=jnp.float32) * 2.0 / HD))
    angles = positions.astype(jnp.float32)[:, None] * freqs[None, :]
    return (jnp.cos(angles), jnp.sin(angles))


def rotate(values, cosine, sine):
    half = HD // 2
    first = values[..., :half]
    second = values[..., half:]
    cosine = cosine[:, None, :]
    sine = sine[:, None, :]
    return jnp.concatenate(
        [first * cosine - second * sine, second * cosine + first * sine], axis=-1
    )


def doc_layout(segment):
    same = segment[:, None] == segment[None, :]
    indices = jnp.arange(segment.shape[0])
    earlier = indices[None, :] < indices[:, None]
    positions = jnp.sum(jnp.logical_and(same, earlier), axis=1)
    visible = jnp.logical_and(same, indices[None, :] <= indices[:, None])
    return (positions, visible)


def attend(query_rot, key_rot, value_rows, visible):
    count = query_rot.shape[0]
    scores = jnp.einsum(
        "rkgd,ckd->kgrc", query_rot, key_rot, preferred_element_type=jnp.float32
    ) / math.sqrt(HD)
    scores = jnp.where(visible[None, None], scores, -1e30)
    top = jnp.max(scores, axis=-1, keepdims=True)
    expd = jnp.exp(scores - top)
    weights = (expd / jnp.sum(expd, axis=-1, keepdims=True)).astype(jnp.bfloat16)
    result = jnp.einsum("kgrc,ckd->rkgd", weights, value_rows, preferred_element_type=jnp.float32)
    return result.astype(jnp.bfloat16).reshape(count, -1)


def keyval_routes():
    half = N_Z * N_Y // 2
    return [(s, N_Y * ((s % half) // 2) + (s % 2) + 2 * (s // half)) for s in range(2 * half)]


def sum_over_y(rows):
    me = lax.axis_index("yh")
    width = rows.shape[1] // N_Y
    total = lax.dynamic_slice_in_dim(rows, me * width, width, 1).astype(jnp.float32)
    for k in range(1, N_Y):
        piece = lax.dynamic_slice_in_dim(rows, lax.rem(me + k, N_Y) * width, width, 1)
        piece = lax.ppermute(piece, "yh", [(i, (i + k) % N_Y) for i in range(N_Y)])
        total = total + piece.astype(jnp.float32)
    return total.astype(jnp.bfloat16)


def shards(activations, w_query, w_keyval, w_out, targets, segments):
    block = lax.axis_index(DP)
    tail_docs = lax.dynamic_slice_in_dim(targets, block * MOVE, MOVE) // RECV
    labels = jnp.concatenate([segments[:KEEP], -1 - tail_docs])
    positions, visible = doc_layout(labels)
    cosine, sine = rotation_tables(positions)

    piece = lax.all_gather(activations, "yh", axis=1, tiled=True)
    piece = lax.all_gather(piece, "z", axis=1, tiled=True)
    query = jnp.dot(piece, w_query, preferred_element_type=jnp.float32)
    keyval = jnp.dot(piece, w_keyval, preferred_element_type=jnp.float32).astype(jnp.bfloat16)
    keyval = lax.ppermute(keyval, TENSOR, keyval_routes())
    keyval = lax.all_gather(keyval, "yh", axis=1, tiled=True)
    key = keyval[:, :HD].reshape(SEQ, 1, HD)
    value = keyval[:, HD:].reshape(SEQ, 1, HD)
    query_rot = rotate(query.reshape(SEQ, 2, HD), cosine, sine).astype(jnp.bfloat16)
    key_rot = rotate(key.astype(jnp.float32), cosine, sine).astype(jnp.bfloat16)
    attended = attend(query_rot.reshape(SEQ, 1, 2, HD), key_rot, value, visible)

    partial = lax.dot_general(
        w_out, attended, (((0,), (1,)), ((), ())), preferred_element_type=jnp.float32
    ).astype(jnp.bfloat16)
    summed = lax.psum_scatter(partial, "z", scatter_dimension=0, tiled=True)
    mixed = sum_over_y(summed.T)

    slots = lax.iota(jnp.int32, RECV)
    wanted = targets - block * RECV
    select = (slots[:, None] == wanted[None, :]).astype(jnp.bfloat16)
    tails = lax.all_gather(mixed[KEEP:], DP, axis=0, tiled=True)
    arrived = jnp.dot(select, tails, preferred_element_type=jnp.float32).astype(jnp.bfloat16)
    return jnp.concatenate([mixed[:KEEP], arrived], axis=0)


def solution(mesh):
    fine = Mesh(
        mesh.devices.reshape(8, 2, 2, N_Z, N_Y), ("x", "yl", "core", "z", "yh")
    )
    placed = (
        P(DP, TENSOR),
        P(None, TENSOR),
        P(None, TENSOR),
        P(TENSOR, None),
        P(),
        P(DP),
    )
    return jax.shard_map(
        shards, mesh=fine, in_specs=placed, out_specs=P(DP, TENSOR), check_vma=False
    )
```

time: 486 us -> 228 us (0.47)
  waiting for transfers between devices: 332 us -> 102 us
  blocking collectives: 118 us -> 83.7 us
  starting transfers between devices: 0.04 us -> 15.5 us
    reduce_scatter x1, waiting for transfers between devices: 241 us -> 46.8 us  [shards(): summed = lax.psum_scatter(partial, 'z', scatter_dimension=0, tiled=True)]
    all_gather x1, waiting for transfers between devices: 91.1 us -> 53.2 us  [shards(): piece = lax.all_gather(piece, 'z', axis=1, tiled=True)]
    all_gather x2 -> x3, blocking collectives: 118 us -> 83.7 us  [the longest x1 41.9 us: shards(): tails = lax.all_gather(mixed[KEEP:], DP, axis=0, tiled=True)]
    ppermute x0 -> x4, starting transfers between devices: none -> 15.5 us  [the longest x3 14.7 us: sum_over_y(): piece = lax.ppermute(piece, 'yh', [(i, (i + k) % N_Y) for i in range(N_Y)])]
  transfers between devices with their start and end apart: 2 -> 6, of which waited for: 2 -> 3; matrix products, arithmetic and copies ran while one was open for 0% -> 1% of each run, Pallas kernels for 0% -> 0%
where the time goes in v1:
time: 228 us
  waiting for transfers between devices  102 us (45%)
  blocking collectives  83.7 us (37%)
  starting transfers between devices  15.5 us (7%)
  between operations  13.7 us (6%)
  matrix products  7.22 us (3%)
  other arithmetic  3.17 us (1%)
  local copies, waits for them, and re-layouts  2.33 us (1%)
    all_gather x1, waiting for transfers between devices, shards(): piece = lax.all_gather(piece, 'z', axis=1, tiled=True)  53.2 us
    reduce_scatter x1, waiting for transfers between devices, shards(): summed = lax.psum_scatter(partial, 'z', scatter_dimension=0, tiled=True)  46.8 us
    all_gather x1, blocking collectives, shards(): tails = lax.all_gather(mixed[KEEP:], DP, axis=0, tiled=True)  41.9 us
    all_gather x1, blocking collectives, shards(): keyval = lax.all_gather(keyval, 'yh', axis=1, tiled=True)  25.3 us
    all_gather x1, blocking collectives, shards(): piece = lax.all_gather(activations, 'yh', axis=1, tiled=True)  16.5 us
    ppermute x3, starting transfers between devices, sum_over_y(): piece = lax.ppermute(piece, 'yh', [(i, (i + k) % N_Y) for i in range(N_Y)])  14.7 us
  transfers between devices with their start and end apart: 6, of which 3 were waited for; matrix products, arithmetic and copies ran while one was open for 1% of the time, Pallas kernels for 0%

profile of v1, /device:TPU:1, one launch (start us, length us, event | category | flops | bytes accessed | tf_op | source)
XLA Modules:
  0.0 227.5 jit_solution(16884949143760023742)
XLA Ops:
  6.5 0.0 copy-start
  6.5 0.0 all-gather.2.cloned.1.call-start
  6.5 16.5 %all_gather.12 = bf16[128,1024]{1,0:T(8,128)(2,1)} all-gather(bf16[128,256]{1,0:T(8,128)(2,1)} %param.6), channel_id=1, replica_groups=mesh['x'=8,'yl'=2,'core'=2,'z'=8,'yh'=4] {'yh'}, dimensions={1}, use_global_device_ids=true | all-gather | bytes 327680 | tf_op jit(solution)/shard_map/all_gather | solution.py:88
  23.0 0.0 all-gather.2.cloned.1.call-update
  23.1 0.0 reduce-scatter.2.cloned.1.call-start
  23.1 0.7 slice.28
  23.8 0.8 fusion.25
  24.6 0.1 pad_add_fusion
  24.6 0.1 convert_reduce_fusion
  24.7 0.0 copy-start.4
  24.8 0.0 copy-start.6
  24.8 0.1 compare_and_fusion.1
  24.9 0.4 copy-done.4
  25.3 0.0 copy-done.6
  25.3 0.3 multiply_cosine_fusion
  25.6 53.2 %all-gather.2.cloned.1.call-done = bf16[128,8192]{1,0:T(8,128)(2,1)} async-done(((bf16[128,1024]{1,0:T(8,128)(2,1)}), bf16[128,8192]{1,0:T(8,128)(2,1)}) %all-gather.2.cloned.1.call-update) | async-done | bytes 2097168 | tf_op jit(solution)/shard_map/all_gather | solution.py:89
  78.8 3.7 %fusion.29 = f32[128,256]{1,0:T(8,128)S(1)} fusion(bf16[128,8192]{1,0:T(8,128)(2,1)} %all-gather.2.cloned.1.call-done, bf16[8192,256]{1,0:T(8,128)(2,1)} %param.7), kind=kOutput, calls=%fused_computation.63 | convolution fusion | flops 536870912 | bytes 6422528 | tf_op jit(solution)/shard_map/dot_general | solution.py:90
  82.4 0.1 reshape.197
  82.5 0.0 copy-done
  82.5 0.0 copy-done.1
  82.5 0.0 copy-start.5
  82.5 0.0 copy-start.7
  82.6 0.0 copy-start.2
  82.6 0.8 convolution_convert_fusion.3
  83.4 0.8 collective-permute-start
  84.2 0.2 fusion.27
  84.5 0.0 collective-permute-done
  84.5 25.3 %all_gather.14 = bf16[128,256]{0,1:T(8,128)(2,1)S(1)} all-gather(bf16[128,64]{0,1:T(8,128)(2,1)S(1)} %collective-permute-done), channel_id=1, replica_groups=mesh['x'=8,'yl'=2,'core'=2,'z'=8,'yh'=4] {'yh'}, dimensions={1}, use_global_device_ids=true | all-gather | bytes 81920 | tf_op jit(solution)/shard_map/all_gather | solution.py:93
  109.8 0.0 copy-done.5
  109.8 0.0 copy-done.7
  109.8 0.2 fusion.24
  110.0 0.3 fusion.28
  110.4 0.2 convolution_convert_fusion.1
  110.5 0.0 copy-start.3
  110.5 2.1 fusion
  112.6 0.0 reduce-scatter.2.cloned.1.call-update
  112.7 46.8 %reduce-scatter.2.cloned.1.call-done = bf16[1024,128]{0,1:T(8,128)(2,1)} async-done(((bf16[8192,128]{0,1:T(8,128)(2,1)}), bf16[1024,128]{0,1:T(8,128)(2,1)}) %reduce-scatter.2.cloned.1.call-update) | async-done | bytes 262160 | tf_op jit(solution)/shard_map/reduce_scatter | solution.py:103
  159.5 0.9 dynamic-slice_bitcast_fusion.2
  160.4 4.0 %collective-permute-start.1 = (bf16[128,256]{1,0:T(8,128)(2,1)S(1)}, bf16[128,256]{1,0:T(8,128)(2,1)S(1)}, u32[]{:S(2)}, u32[]{:S(2)}) collective-permute-start(bf16[128,256]{1,0:T(8,128)(2,1)S(1)} %get-tuple-element.7), channel_id=1, source_target_pairs={{0,1},{1,2},{2,3},{3,0},{4,5},{5,6},{6,7},{7,4},{8,9},{9,10},{10,1... | collective-permute-start | bytes 196616 | tf_op jit(solution)/shard_map/ppermute | solution.py:76
  164.4 3.5 %collective-permute-start.3 = (bf16[128,256]{1,0:T(8,128)(2,1)S(1)}, bf16[128,256]{1,0:T(8,128)(2,1)S(1)}, u32[]{:S(2)}, u32[]{:S(2)}) collective-permute-start(bf16[128,256]{1,0:T(8,128)(2,1)S(1)} %get-tuple-element.8), channel_id=1, source_target_pairs={{0,3},{1,0},{2,1},{3,2},{4,7},{5,4},{6,5},{7,6},{8,11},{9,8},{10,9... | collective-permute-start | bytes 196616 | tf_op jit(solution)/shard_map/ppermute | solution.py:76
  168.0 7.1 %collective-permute-start.2 = (bf16[128,256]{1,0:T(8,128)(2,1)S(1)}, bf16[128,256]{1,0:T(8,128)(2,1)S(1)}, u32[]{:S(2)}, u32[]{:S(2)}) collective-permute-start(bf16[128,256]{1,0:T(8,128)(2,1)S(1)} %get-tuple-element.9), channel_id=1, source_target_pairs={{0,2},{1,3},{2,0},{3,1},{4,6},{5,7},{6,4},{7,5},{8,10},{9,11},{10,... | collective-permute-start | bytes 196616 | tf_op jit(solution)/shard_map/ppermute | solution.py:76
  175.1 0.0 collective-permute-done.1
  175.1 0.0 collective-permute-done.3
  175.1 1.9 collective-permute-done.2
  177.0 0.9 fusion.5
  177.9 41.9 %all_gather.15 = bf16[1024,256]{1,0:T(8,128)(2,1)S(1)} all-gather(bf16[32,256]{1,0:T(8,128)(2,1)S(1)} %slice.43), channel_id=1, replica_groups=mesh['x'=8,'yl'=2,'core'=2,'z'=8,'yh'=4] {'x','yl','core'}, dimensions={0}, use_global_device_ids=true | all-gather | bytes 540672 | tf_op jit(solution)/shard_map/all_gather | solution.py:109
  219.8 0.2 convolution_convert_fusion.2
  220.0 0.6 pad_maximum_fusion
  (11 shorter events, 0.1 us)
Async XLA Ops:
  6.5 76.0 %copy-start = (bf16[8192,64]{0,1:T(8,128)(2,1)S(1)}, bf16[8192,64]{0,1:T(8,128)(2,1)}, u32[]{:S(2)}) copy-start(bf16[8192,64]{0,1:T(8,128)(2,1)} %param.8) | copy-start | bytes 3145732
  6.5 72.2 %all-gather.2.cloned.1.call-start = ((), (), s32[]{:S(2)}) async-start(), calls=%async_computation.1 | async-start | bytes 2359296 | tf_op jit(solution)/shard_map/all_gather | solution.py:89
  23.1 136.4 %reduce-scatter.2.cloned.1.call-start = ((), (), s32[]{:S(2)}) async-start(), calls=%async_computation.2 | async-start | bytes 2359296 | tf_op jit(solution)/shard_map/reduce_scatter | solution.py:103
  24.7 0.5 copy-start.4
  24.8 0.5 copy-start.6
  78.8 3.8 %copy-start.1 = (bf16[128,8192]{1,0:T(8,128)(2,1)S(1)}, bf16[128,8192]{1,0:T(8,128)(2,1)}, u32[]{:S(2)}) copy-start(bf16[128,8192]{1,0:T(8,128)(2,1)} %all-gather.2.cloned.1.call-done) | copy-start | bytes 6291460
  82.5 27.3 %copy-start.5 = (f32[128]{0:T(128)S(1)}, f32[128]{0:T(128)}, u32[]{:S(2)}) copy-start(f32[128]{0:T(128)} %copy-done.4) | copy-start | bytes 1540
  82.5 27.3 %copy-start.7 = (f32[64]{0:T(128)S(1)}, f32[64]{0:T(128)}, u32[]{:S(2)}) copy-start(f32[64]{0:T(128)} %copy-done.6) | copy-start | bytes 772
  82.6 28.0 %copy-start.2 = (bf16[256,8192]{1,0:T(8,128)(2,1)S(1)}, bf16[256,8192]{1,0:T(8,128)(2,1)}, u32[]{:S(2)}) copy-start(bf16[256,8192]{1,0:T(8,128)(2,1)} %param.9) | copy-start | bytes 12582916
  83.4 1.1 collective-permute-start
  110.5 64.5 %copy-start.3 = (s32[1024]{0:T(1024)S(1)}, s32[1024]{0:T(1024)}, u32[]{:S(2)}) copy-start(s32[1024]{0:T(1024)} %param.10) | copy-start | bytes 12292
  160.4 14.7 %collective-permute-start.1 = (bf16[128,256]{1,0:T(8,128)(2,1)S(1)}, bf16[128,256]{1,0:T(8,128)(2,1)S(1)}, u32[]{:S(2)}, u32[]{:S(2)}) collective-permute-start(bf16[128,256]{1,0:T(8,128)(2,1)S(1)} %get-tuple-element.7), channel_id=1, source_target_pairs={{0,1},{1,2},{2,3},{3,0},{4,5},{5,6},{6,7},{7,4},{8,9},{9,10},{10,1... | collective-permute-start | bytes 196616 | tf_op jit(solution)/shard_map/ppermute | solution.py:76
  164.4 10.7 %collective-permute-start.3 = (bf16[128,256]{1,0:T(8,128)(2,1)S(1)}, bf16[128,256]{1,0:T(8,128)(2,1)S(1)}, u32[]{:S(2)}, u32[]{:S(2)}) collective-permute-start(bf16[128,256]{1,0:T(8,128)(2,1)S(1)} %get-tuple-element.8), channel_id=1, source_target_pairs={{0,3},{1,0},{2,1},{3,2},{4,7},{5,4},{6,5},{7,6},{8,11},{9,8},{10,9... | collective-permute-start | bytes 196616 | tf_op jit(solution)/shard_map/ppermute | solution.py:76
  168.0 9.0 %collective-permute-start.2 = (bf16[128,256]{1,0:T(8,128)(2,1)S(1)}, bf16[128,256]{1,0:T(8,128)(2,1)S(1)}, u32[]{:S(2)}, u32[]{:S(2)}) collective-permute-start(bf16[128,256]{1,0:T(8,128)(2,1)S(1)} %get-tuple-element.9), channel_id=1, source_target_pairs={{0,2},{1,3},{2,0},{3,1},{4,6},{5,7},{6,4},{7,5},{8,10},{9,11},{10,... | collective-permute-start | bytes 196616 | tf_op jit(solution)/shard_map/ppermute | solution.py:76
Sparse Core Ops, SparseCore 0:
  23.2 55.5 all-gather.1
  112.8 46.6 reduce-scatter.1

commit v2 on v1

--- a/solution.py
+++ b/solution.py
@@ -62,9 +62,39 @@
     return result.astype(jnp.bfloat16).reshape(count, -1)
 
 
-def keyval_routes():
+def ring(n, k):
+    return [(i, (i + k) % n) for i in range(n)]
+
+
+def keyval_routes(k):
     half = N_Z * N_Y // 2
-    return [(s, N_Y * ((s % half) // 2) + (s % 2) + 2 * (s // half)) for s in range(2 * half)]
+    return [
+        (s, N_Y * ((s % half) // 2) + (s % 2 + 2 * (s // half) + k) % N_Y) for s in range(2 * half)
+    ]
+
+
+def gather_y(rows):
+    me = lax.axis_index("yh")
+    pieces = [rows] + [lax.ppermute(rows, "yh", ring(N_Y, k)) for k in range(1, N_Y)]
+    stack = jnp.stack(pieces)
+    return jnp.concatenate(
+        [lax.dynamic_index_in_dim(stack, (me - j) % N_Y, 0, False) for j in range(N_Y)], axis=1
+    )
+
+
+def sum_pieces(pieces):
+    return jnp.sum(pieces.astype(jnp.float32), axis=0).astype(jnp.bfloat16)
+
+
+def scatter_sum(attended, w_out):
+    n = N_Z * N_Y
+    partial = jnp.einsum(
+        "rk,kdn->drn",
+        attended,
+        w_out.reshape(w_out.shape[0], n, -1),
+        preferred_element_type=jnp.float32,
+    ).astype(jnp.bfloat16)
+    return sum_pieces(lax.all_to_all(partial, TENSOR, 0, 0, tiled=True))
 
 
 def sum_over_y(rows):
@@ -85,30 +115,53 @@
     positions, visible = doc_layout(labels)
     cosine, sine = rotation_tables(positions)
 
-    piece = lax.all_gather(activations, "yh", axis=1, tiled=True)
-    piece = lax.all_gather(piece, "z", axis=1, tiled=True)
-    query = jnp.dot(piece, w_query, preferred_element_type=jnp.float32)
-    keyval = jnp.dot(piece, w_keyval, preferred_element_type=jnp.float32).astype(jnp.bfloat16)
-    keyval = lax.ppermute(keyval, TENSOR, keyval_routes())
-    keyval = lax.all_gather(keyval, "yh", axis=1, tiled=True)
-    key = keyval[:, :HD].reshape(SEQ, 1, HD)
-    value = keyval[:, HD:].reshape(SEQ, 1, HD)
+    z_me = lax.axis_index("z")
+    y_me = lax.axis_index("yh")
+    own = gather_y(activations)
+    depth = own.shape[1]
+
+    def times(weight, chunk, k):
+        rows = lax.dynamic_slice_in_dim(weight, ((z_me + k) % N_Z) * depth, depth, 0)
+        return jnp.dot(chunk, rows, preferred_element_type=jnp.float32)
+
+    query = times(w_query, own, 0)
+    keyval = times(w_keyval, own, 0)
+    up, down = own, own
+    for step in range(1, N_Z // 2):
+        up = lax.ppermute(up, "z", ring(N_Z, 1))
+        down = lax.ppermute(down, "z", ring(N_Z, -1))
+        query = query + times(w_query, up, -step) + times(w_query, down, step)
+        keyval = keyval + times(w_keyval, up, -step) + times(w_keyval, down, step)
+    half = SEQ // 2
+    up = lax.ppermute(up[:half], "z", ring(N_Z, 1))
+    down = lax.ppermute(down[half:], "z", ring(N_Z, -1))
+    last = jnp.concatenate([up, down], axis=0)
+    keyval = (keyval + times(w_keyval, last, N_Z // 2)).astype(jnp.bfloat16)
+    pieces = [lax.ppermute(keyval, TENSOR, keyval_routes(k)) for k in range(N_Y)]
+    query = query + times(w_query, last, N_Z // 2)
+
+    stack = jnp.stack(pieces)
+    roles = [lax.dynamic_index_in_dim(stack, (y_me - r) % N_Y, 0, False) for r in range(N_Y)]
+    key = jnp.concatenate(roles[:2], axis=1).reshape(SEQ, 1, HD)
+    value = jnp.concatenate(roles[2:], axis=1).reshape(SEQ, 1, HD)
     query_rot = rotate(query.reshape(SEQ, 2, HD), cosine, sine).astype(jnp.bfloat16)
     key_rot = rotate(key.astype(jnp.float32), cosine, sine).astype(jnp.bfloat16)
     attended = attend(query_rot.reshape(SEQ, 1, 2, HD), key_rot, value, visible)
 
     partial = lax.dot_general(
-        w_out, attended, (((0,), (1,)), ((), ())), preferred_element_type=jnp.float32
+        w_out, attended[:KEEP], (((0,), (1,)), ((), ())), preferred_element_type=jnp.float32
     ).astype(jnp.bfloat16)
-    summed = lax.psum_scatter(partial, "z", scatter_dimension=0, tiled=True)
-    mixed = sum_over_y(summed.T)
+    kept = lax.psum_scatter(partial, "z", scatter_dimension=0, tiled=True)
+    moving = scatter_sum(attended[KEEP:], w_out)
+    kept = sum_over_y(kept.T)
 
     slots = lax.iota(jnp.int32, RECV)
     wanted = targets - block * RECV
     select = (slots[:, None] == wanted[None, :]).astype(jnp.bfloat16)
-    tails = lax.all_gather(mixed[KEEP:], DP, axis=0, tiled=True)
+    tails = jnp.broadcast_to(moving[None], (targets.shape[0] // MOVE,) + moving.shape)
+    tails = lax.all_to_all(tails, DP, 0, 0, tiled=True).reshape(targets.shape[0], -1)
     arrived = jnp.dot(select, tails, preferred_element_type=jnp.float32).astype(jnp.bfloat16)
-    return jnp.concatenate([mixed[:KEEP], arrived], axis=0)
+    return jnp.concatenate([kept, arrived], axis=0)
 
 
 def solution(mesh):

time: 228 us -> 191 us (0.84)
  the two profiles are of different devices: /device:TPU:1 before, /device:TPU:2 now
where the time goes in v2:
time: 191 us; the launch traced here: 190 us
  starting transfers between devices  91.1 us (48%)
  waiting for transfers between devices  33.3 us (17%)
  blocking collectives  29.9 us (16%)
  between operations  14.2 us (7%)
  matrix products  13.6 us (7%)
  other arithmetic  4.67 us (2%)
  local copies, waits for them, and re-layouts  3.35 us (2%)
    all_to_all x1, blocking collectives, scatter_sum(): return sum_pieces(lax.all_to_all(partial, TENSOR, 0, 0, tiled=True))  29.9 us
    ppermute x3, starting transfers between devices, shards(): down = lax.ppermute(down, 'z', ring(N_Z, -1))  28.4 us
    ppermute x3, starting transfers between devices, gather_y(): lax.ppermute(rows, 'yh', ring(N_Y, k))  16.3 us
    ppermute x3, starting transfers between devices, sum_over_y(): piece = lax.ppermute(piece, 'yh', [(i, (i + k) % N_Y) for i in range(N_Y)])  14.2 us
    reduce_scatter x1, waiting for transfers between devices, shards(): kept = lax.psum_scatter(partial, 'z', scatter_dimension=0, tiled=True)  13.2 us
    ppermute x4, starting transfers between devices, shards(): lax.ppermute(keyval, TENSOR, keyval_routes(k))  11.5 us
    ppermute x4, waiting for transfers between devices, shards(): lax.ppermute(keyval, TENSOR, keyval_routes(k))  8.15 us
    all_to_all x1, starting transfers between devices, shards(): lax.all_to_all(tails, DP, 0, 0, tiled=True).reshape(targets.shape[0], -1)  7.45 us
  transfers between devices with their start and end apart: 20, of which 9 were waited for; matrix products, arithmetic and copies ran while one was open for 7% of the time, Pallas kernels for 0%

profile of v2, /device:TPU:2, one launch (start us, length us, event | category | flops | bytes accessed | tf_op | source)
XLA Modules:
  0.0 190.1 jit_solution(15165715392862040307)
XLA Ops:
  6.5 4.8 %collective-permute-start = (bf16[128,256]{1,0:T(8,128)(2,1)}, bf16[128,256]{1,0:T(8,128)(2,1)S(1)}, u32[]{:S(2)}, u32[]{:S(2)}) collective-permute-start(bf16[128,256]{1,0:T(8,128)(2,1)} %param.6), channel_id=1, source_target_pairs={{0,1},{1,2},{2,3},{3,0},{4,5},{5,6},{6,7},{7,4},{8,9},{9,10},{10,1... | collective-permute-start | bytes 196616 | tf_op jit(solution)/shard_map/ppermute | solution.py:78
  11.4 4.0 %collective-permute-start.2 = (bf16[128,256]{1,0:T(8,128)(2,1)}, bf16[128,256]{1,0:T(8,128)(2,1)S(1)}, u32[]{:S(2)}, u32[]{:S(2)}) collective-permute-start(bf16[128,256]{1,0:T(8,128)(2,1)} %param.6), channel_id=1, source_target_pairs={{0,3},{1,0},{2,1},{3,2},{4,7},{5,4},{6,5},{7,6},{8,11},{9,8},{10,9... | collective-permute-start | bytes 196616 | tf_op jit(solution)/shard_map/ppermute | solution.py:78
  15.4 7.4 %collective-permute-start.1 = (bf16[128,256]{1,0:T(8,128)(2,1)}, bf16[128,256]{1,0:T(8,128)(2,1)S(1)}, u32[]{:S(2)}, u32[]{:S(2)}) collective-permute-start(bf16[128,256]{1,0:T(8,128)(2,1)} %param.6), channel_id=1, source_target_pairs={{0,2},{1,3},{2,0},{3,1},{4,6},{5,7},{6,4},{7,5},{8,10},{9,11},{10,... | collective-permute-start | bytes 196616 | tf_op jit(solution)/shard_map/ppermute | solution.py:78
  22.9 0.7 slice.35
  23.5 0.8 fusion.85
  24.5 0.3 multiply_cosine_fusion
  25.1 0.7 collective-permute-done.1
  25.8 1.2 pad_maximum_fusion
  27.1 17.3 %collective-permute-start.4 = (bf16[128,1024]{1,0:T(8,128)(2,1)S(1)}, bf16[128,1024]{1,0:T(8,128)(2,1)S(1)}, u32[]{:S(2)}, u32[]{:S(2)}) collective-permute-start(bf16[128,1024]{1,0:T(8,128)(2,1)S(1)} %pad_maximum_fusion.1), channel_id=1, source_target_pairs={{0,28},{4,0},{8,4},{12,8},{16,12},{20,16},{24,20},{28,24},{1,29},{... | collective-permute-start | bytes 786440 | tf_op jit(solution)/shard_map/ppermute | solution.py:132
  44.4 1.9 %collective-permute-start.3 = (bf16[128,1024]{1,0:T(8,128)(2,1)S(1)}, bf16[128,1024]{1,0:T(8,128)(2,1)S(1)}, u32[]{:S(2)}, u32[]{:S(2)}) collective-permute-start(bf16[128,1024]{1,0:T(8,128)(2,1)S(1)} %pad_maximum_fusion.1), channel_id=1, source_target_pairs={{0,4},{4,8},{8,12},{12,16},{16,20},{20,24},{24,28},{28,0},{1,5},{5... | collective-permute-start | bytes 786440 | tf_op jit(solution)/shard_map/ppermute | solution.py:131
  46.6 1.3 fusion.30
  47.9 0.6 collective-permute-done.4
  48.5 5.6 %collective-permute-start.6 = (bf16[128,1024]{1,0:T(8,128)(2,1)S(1)}, bf16[128,1024]{1,0:T(8,128)(2,1)S(1)}, u32[]{:S(2)}, u32[]{:S(2)}) collective-permute-start(bf16[128,1024]{1,0:T(8,128)(2,1)S(1)} %collective-permute-done.4), channel_id=1, source_target_pairs={{0,28},{4,0},{8,4},{12,8},{16,12},{20,16},{24,20},{28,24},{1,29},{... | collective-permute-start | bytes 786440 | tf_op jit(solution)/shard_map/ppermute | solution.py:132
  54.1 1.9 %collective-permute-start.5 = (bf16[128,1024]{1,0:T(8,128)(2,1)S(1)}, bf16[128,1024]{1,0:T(8,128)(2,1)S(1)}, u32[]{:S(2)}, u32[]{:S(2)}) collective-permute-start(bf16[128,1024]{1,0:T(8,128)(2,1)S(1)} %collective-permute-done.3), channel_id=1, source_target_pairs={{0,4},{4,8},{8,12},{12,16},{16,20},{20,24},{24,28},{28,0},{1,5},{5... | collective-permute-start | bytes 786440 | tf_op jit(solution)/shard_map/ppermute | solution.py:131
  56.0 1.3 convolution_add_fusion.3
  57.7 0.2 convolution_add_fusion.2
  58.0 5.5 %collective-permute-start.8 = (bf16[128,1024]{1,0:T(8,128)(2,1)S(1)}, bf16[128,1024]{1,0:T(8,128)(2,1)S(1)}, u32[]{:S(2)}, u32[]{:S(2)}) collective-permute-start(bf16[128,1024]{1,0:T(8,128)(2,1)S(1)} %collective-permute-done.6), channel_id=1, source_target_pairs={{0,28},{4,0},{8,4},{12,8},{16,12},{20,16},{24,20},{28,24},{1,29},{... | collective-permute-start | bytes 786440 | tf_op jit(solution)/shard_map/ppermute | solution.py:132
  63.8 0.2 fusion.25
  64.0 1.9 %collective-permute-start.7 = (bf16[128,1024]{1,0:T(8,128)(2,1)S(1)}, bf16[128,1024]{1,0:T(8,128)(2,1)S(1)}, u32[]{:S(2)}, u32[]{:S(2)}) collective-permute-start(bf16[128,1024]{1,0:T(8,128)(2,1)S(1)} %collective-permute-done.5), channel_id=1, source_target_pairs={{0,4},{4,8},{8,12},{12,16},{16,20},{20,24},{24,28},{28,0},{1,5},{5... | collective-permute-start | bytes 786440 | tf_op jit(solution)/shard_map/ppermute | solution.py:131
  66.2 0.2 fusion.11
  66.4 1.0 collective-permute-done.8
  67.4 5.6 %collective-permute-start.10 = (bf16[64,1024]{1,0:T(8,128)(2,1)S(1)}, bf16[64,1024]{1,0:T(8,128)(2,1)S(1)}, u32[]{:S(2)}, u32[]{:S(2)}) collective-permute-start(bf16[64,1024]{1,0:T(8,128)(2,1)S(1)} %slice.45), channel_id=1, source_target_pairs={{0,28},{4,0},{8,4},{12,8},{16,12},{20,16},{24,20},{28,24},{1,29},{... | collective-permute-start | bytes 393224 | tf_op jit(solution)/shard_map/ppermute | solution.py:137
  73.0 0.5 collective-permute-done.7
  73.5 1.9 %collective-permute-start.9 = (bf16[64,1024]{1,0:T(8,128)(2,1)S(1)}, bf16[64,1024]{1,0:T(8,128)(2,1)S(1)}, u32[]{:S(2)}, u32[]{:S(2)}) collective-permute-start(bf16[64,1024]{1,0:T(8,128)(2,1)S(1)} %slice.44), channel_id=1, source_target_pairs={{0,4},{4,8},{8,12},{12,16},{16,20},{20,24},{24,28},{28,0},{1,5},{5... | collective-permute-start | bytes 393224 | tf_op jit(solution)/shard_map/ppermute | solution.py:136
  75.9 5.7 %collective-permute-done.9 = bf16[64,1024]{1,0:T(8,128)(2,1)S(1)} collective-permute-done((bf16[64,1024]{1,0:T(8,128)(2,1)S(1)}, bf16[64,1024]{1,0:T(8,128)(2,1)S(1)}, u32[]{:S(2)}, u32[]{:S(2)}) %collective-permute-start.9) | collective-permute-done | bytes 131104 | tf_op jit(solution)/shard_map/ppermute | solution.py:136
  81.8 0.2 fusion.20
  82.3 4.2 %collective-permute-start.14 = (bf16[128,64]{0,1:T(8,128)(2,1)S(1)}, bf16[128,64]{0,1:T(8,128)(2,1)S(1)}, u32[]{:S(2)}, u32[]{:S(2)}) collective-permute-start(bf16[128,64]{0,1:T(8,128)(2,1)S(1)} %fusion.19), channel_id=1, source_target_pairs={{0,3},{1,0},{2,7},{3,4},{4,11},{5,8},{6,15},{7,12},{8,19},{9,16},{... | collective-permute-start | bytes 49160 | tf_op jit(solution)/shard_map/ppermute | solution.py:140
  86.5 4.7 %collective-permute-start.13 = (bf16[128,64]{0,1:T(8,128)(2,1)S(1)}, bf16[128,64]{0,1:T(8,128)(2,1)S(1)}, u32[]{:S(2)}, u32[]{:S(2)}) collective-permute-start(bf16[128,64]{0,1:T(8,128)(2,1)S(1)} %fusion.19), channel_id=1, source_target_pairs={{0,2},{1,3},{2,6},{3,7},{4,10},{5,11},{6,14},{7,15},{8,18},{9,19},... | collective-permute-start | bytes 49160 | tf_op jit(solution)/shard_map/ppermute | solution.py:140
  91.2 1.9 %collective-permute-start.12 = (bf16[128,64]{0,1:T(8,128)(2,1)S(1)}, bf16[128,64]{0,1:T(8,128)(2,1)S(1)}, u32[]{:S(2)}, u32[]{:S(2)}) collective-permute-start(bf16[128,64]{0,1:T(8,128)(2,1)S(1)} %fusion.19), channel_id=1, source_target_pairs={{0,1},{1,2},{2,5},{3,6},{4,9},{5,10},{6,13},{7,14},{8,17},{9,18},{... | collective-permute-start | bytes 49160 | tf_op jit(solution)/shard_map/ppermute | solution.py:140
  93.2 0.7 collective-permute-start.11
  93.8 0.2 fusion.12
  94.4 1.6 collective-permute-done.13
  96.1 6.5 %collective-permute-done.12 = bf16[128,64]{0,1:T(8,128)(2,1)S(1)} collective-permute-done((bf16[128,64]{0,1:T(8,128)(2,1)S(1)}, bf16[128,64]{0,1:T(8,128)(2,1)S(1)}, u32[]{:S(2)}, u32[]{:S(2)}) %collective-permute-start.12) | collective-permute-done | bytes 16416 | tf_op jit(solution)/shard_map/ppermute | solution.py:140
  103.1 0.3 fusion.68
  103.5 0.3 fusion.89
  104.2 4.2 %fusion = bf16[8192,96]{0,1:T(8,128)(2,1)} fusion(bf16[256,8192]{1,0:T(8,128)(2,1)} %param.9, bf16[12,8,2,128]{3,2,1,0:T(2,128)(2,1)S(1)} %bitcast.105), kind=kOutput, calls=%fused_computation.1 | convolution fusion | flops 403439616 | bytes 5816320 | tf_op jit(solution)/shard_map/dot_general | solution.py:151
  108.4 3.0 %fusion.7 = bf16[32,32,256]{2,1,0:T(8,128)(2,1)S(1)} fusion(bf16[32,256,1]{1,0,2:T(8,128)(2,1)S(1)} %reshape.240, bf16[32,32,8,256]{3,2,1,0:T(8,128)(2,1)} %bitcast.103), kind=kOutput, calls=%fused_computation.6 | convolution fusion | flops 134479872 | bytes 4734976 | tf_op jit(solution)/shard_map/rk,kdn->drn/dot_general | solution.py:91
  111.4 29.9 %all_to_all.10 = bf16[32,32,256]{2,1,0:T(8,128)(2,1)S(1)} all-to-all(bf16[32,32,256]{2,1,0:T(8,128)(2,1)S(1)} %fusion.7), channel_id=1, replica_groups=mesh['x'=8,'yl'=2,'core'=2,'z'=8,'yh'=4] {'z','yh'}, dimensions={0} | all-to-all | bytes 1048576 | tf_op jit(solution)/shard_map/all_to_all | solution.py:97
  141.4 0.9 broadcast_in_dim.12
  142.3 7.4 %all-to-all-start.1 = ((bf16[32,32,256]{2,1,0:T(8,128)(2,1)}), bf16[32,32,256]{2,1,0:T(8,128)(2,1)S(1)}, u32[]{:S(2)}, u32[]{:S(2)}) async-start(bf16[32,32,256]{2,1,0:T(8,128)(2,1)} %broadcast_in_dim.12), calls=%async_computation.2 | async-start | bytes 1048576 | tf_op jit(solution)/shard_map/all_to_all | solution.py:162
  149.8 13.2 %reduce-scatter.2.cloned.1.call-done = bf16[1024,96]{0,1:T(8,128)(2,1)} async-done(((bf16[8192,96]{0,1:T(8,128)(2,1)}), bf16[1024,96]{0,1:T(8,128)(2,1)}) %reduce-scatter.2.cloned.1.call-update) | async-done | bytes 196624 | tf_op jit(solution)/shard_map/reduce_scatter | solution.py:154
  163.1 0.9 dynamic-slice_bitcast_fusion.6
  163.9 3.9 %collective-permute-start.15 = (bf16[96,256]{1,0:T(8,128)(2,1)S(1)}, bf16[96,256]{1,0:T(8,128)(2,1)S(1)}, u32[]{:S(2)}, u32[]{:S(2)}) collective-permute-start(bf16[96,256]{1,0:T(8,128)(2,1)S(1)} %get-tuple-element.11), channel_id=1, source_target_pairs={{0,1},{1,2},{2,3},{3,0},{4,5},{5,6},{6,7},{7,4},{8,9},{9,10},{10,1... | collective-permute-start | bytes 147464 | tf_op jit(solution)/shard_map/ppermute | solution.py:106
  167.8 4.1 %collective-permute-start.17 = (bf16[96,256]{1,0:T(8,128)(2,1)S(1)}, bf16[96,256]{1,0:T(8,128)(2,1)S(1)}, u32[]{:S(2)}, u32[]{:S(2)}) collective-permute-start(bf16[96,256]{1,0:T(8,128)(2,1)S(1)} %get-tuple-element.12), channel_id=1, source_target_pairs={{0,3},{1,0},{2,1},{3,2},{4,7},{5,4},{6,5},{7,6},{8,11},{9,8},{10,9... | collective-permute-start | bytes 147464 | tf_op jit(solution)/shard_map/ppermute | solution.py:106
  171.9 6.2 %collective-permute-start.16 = (bf16[96,256]{1,0:T(8,128)(2,1)S(1)}, bf16[96,256]{1,0:T(8,128)(2,1)S(1)}, u32[]{:S(2)}, u32[]{:S(2)}) collective-permute-start(bf16[96,256]{1,0:T(8,128)(2,1)S(1)} %get-tuple-element.13), channel_id=1, source_target_pairs={{0,2},{1,3},{2,0},{3,1},{4,6},{5,7},{6,4},{7,5},{8,10},{9,11},{10,... | collective-permute-start | bytes 147464 | tf_op jit(solution)/shard_map/ppermute | solution.py:106
  178.4 3.4 %collective-permute-done.16 = bf16[96,256]{1,0:T(8,128)(2,1)S(1)} collective-permute-done((bf16[96,256]{1,0:T(8,128)(2,1)S(1)}, bf16[96,256]{1,0:T(8,128)(2,1)S(1)}, u32[]{:S(2)}, u32[]{:S(2)}) %collective-permute-start.16) | collective-permute-done | bytes 49184 | tf_op jit(solution)/shard_map/ppermute | solution.py:106
  181.8 0.8 fusion.48
  182.6 0.6 pad_maximum_fusion.2
  (59 shorter events, 3.9 us)
Async XLA Ops:
  6.5 39.8 %copy-start = (bf16[8192,64]{0,1:T(8,128)(2,1)S(1)}, bf16[8192,64]{0,1:T(8,128)(2,1)}, u32[]{:S(2)}) copy-start(bf16[8192,64]{0,1:T(8,128)(2,1)} %param.8) | copy-start | bytes 3145732
  6.5 156.5 %reduce-scatter.2.cloned.1.call-start = ((), (), s32[]{:S(2)}) async-start(), calls=%async_computation.3 | async-start | bytes 1769472 | tf_op jit(solution)/shard_map/reduce_scatter | solution.py:154
  6.5 18.6 %collective-permute-start = (bf16[128,256]{1,0:T(8,128)(2,1)}, bf16[128,256]{1,0:T(8,128)(2,1)S(1)}, u32[]{:S(2)}, u32[]{:S(2)}) collective-permute-start(bf16[128,256]{1,0:T(8,128)(2,1)} %param.6), channel_id=1, source_target_pairs={{0,1},{1,2},{2,3},{3,0},{4,5},{5,6},{6,7},{7,4},{8,9},{9,10},{10,1... | collective-permute-start | bytes 196616 | tf_op jit(solution)/shard_map/ppermute | solution.py:78
  11.4 13.7 %collective-permute-start.2 = (bf16[128,256]{1,0:T(8,128)(2,1)}, bf16[128,256]{1,0:T(8,128)(2,1)S(1)}, u32[]{:S(2)}, u32[]{:S(2)}) collective-permute-start(bf16[128,256]{1,0:T(8,128)(2,1)} %param.6), channel_id=1, source_target_pairs={{0,3},{1,0},{2,1},{3,2},{4,7},{5,4},{6,5},{7,6},{8,11},{9,8},{10,9... | collective-permute-start | bytes 196616 | tf_op jit(solution)/shard_map/ppermute | solution.py:78
  15.4 10.4 %collective-permute-start.1 = (bf16[128,256]{1,0:T(8,128)(2,1)}, bf16[128,256]{1,0:T(8,128)(2,1)S(1)}, u32[]{:S(2)}, u32[]{:S(2)}) collective-permute-start(bf16[128,256]{1,0:T(8,128)(2,1)} %param.6), channel_id=1, source_target_pairs={{0,2},{1,3},{2,0},{3,1},{4,6},{5,7},{6,4},{7,5},{8,10},{9,11},{10,... | collective-permute-start | bytes 196616 | tf_op jit(solution)/shard_map/ppermute | solution.py:78
  25.1 32.6 %copy-start.1 = (bf16[8192,256]{1,0:T(8,128)(2,1)S(1)}, bf16[8192,256]{1,0:T(8,128)(2,1)}, u32[]{:S(2)}) copy-start(bf16[8192,256]{1,0:T(8,128)(2,1)} %param.7) | copy-start | bytes 12582916
  27.1 21.4 %collective-permute-start.4 = (bf16[128,1024]{1,0:T(8,128)(2,1)S(1)}, bf16[128,1024]{1,0:T(8,128)(2,1)S(1)}, u32[]{:S(2)}, u32[]{:S(2)}) collective-permute-start(bf16[128,1024]{1,0:T(8,128)(2,1)S(1)} %pad_maximum_fusion.1), channel_id=1, source_target_pairs={{0,28},{4,0},{8,4},{12,8},{16,12},{20,16},{24,20},{28,24},{1,29},{... | collective-permute-start | bytes 786440 | tf_op jit(solution)/shard_map/ppermute | solution.py:132
  44.4 9.6 %collective-permute-start.3 = (bf16[128,1024]{1,0:T(8,128)(2,1)S(1)}, bf16[128,1024]{1,0:T(8,128)(2,1)S(1)}, u32[]{:S(2)}, u32[]{:S(2)}) collective-permute-start(bf16[128,1024]{1,0:T(8,128)(2,1)S(1)} %pad_maximum_fusion.1), channel_id=1, source_target_pairs={{0,4},{4,8},{8,12},{12,16},{16,20},{20,24},{24,28},{28,0},{1,5},{5... | collective-permute-start | bytes 786440 | tf_op jit(solution)/shard_map/ppermute | solution.py:131
  48.5 9.5 %collective-permute-start.6 = (bf16[128,1024]{1,0:T(8,128)(2,1)S(1)}, bf16[128,1024]{1,0:T(8,128)(2,1)S(1)}, u32[]{:S(2)}, u32[]{:S(2)}) collective-permute-start(bf16[128,1024]{1,0:T(8,128)(2,1)S(1)} %collective-permute-done.4), channel_id=1, source_target_pairs={{0,28},{4,0},{8,4},{12,8},{16,12},{20,16},{24,20},{28,24},{1,29},{... | collective-permute-start | bytes 786440 | tf_op jit(solution)/shard_map/ppermute | solution.py:132
  54.1 9.9 %collective-permute-start.5 = (bf16[128,1024]{1,0:T(8,128)(2,1)S(1)}, bf16[128,1024]{1,0:T(8,128)(2,1)S(1)}, u32[]{:S(2)}, u32[]{:S(2)}) collective-permute-start(bf16[128,1024]{1,0:T(8,128)(2,1)S(1)} %collective-permute-done.3), channel_id=1, source_target_pairs={{0,4},{4,8},{8,12},{12,16},{16,20},{20,24},{24,28},{28,0},{1,5},{5... | collective-permute-start | bytes 786440 | tf_op jit(solution)/shard_map/ppermute | solution.py:131
  58.0 9.4 %collective-permute-start.8 = (bf16[128,1024]{1,0:T(8,128)(2,1)S(1)}, bf16[128,1024]{1,0:T(8,128)(2,1)S(1)}, u32[]{:S(2)}, u32[]{:S(2)}) collective-permute-start(bf16[128,1024]{1,0:T(8,128)(2,1)S(1)} %collective-permute-done.6), channel_id=1, source_target_pairs={{0,28},{4,0},{8,4},{12,8},{16,12},{20,16},{24,20},{28,24},{1,29},{... | collective-permute-start | bytes 786440 | tf_op jit(solution)/shard_map/ppermute | solution.py:132
  64.0 9.5 %collective-permute-start.7 = (bf16[128,1024]{1,0:T(8,128)(2,1)S(1)}, bf16[128,1024]{1,0:T(8,128)(2,1)S(1)}, u32[]{:S(2)}, u32[]{:S(2)}) collective-permute-start(bf16[128,1024]{1,0:T(8,128)(2,1)S(1)} %collective-permute-done.5), channel_id=1, source_target_pairs={{0,4},{4,8},{8,12},{12,16},{16,20},{20,24},{24,28},{28,0},{1,5},{5... | collective-permute-start | bytes 786440 | tf_op jit(solution)/shard_map/ppermute | solution.py:131
  67.4 14.2 %collective-permute-start.10 = (bf16[64,1024]{1,0:T(8,128)(2,1)S(1)}, bf16[64,1024]{1,0:T(8,128)(2,1)S(1)}, u32[]{:S(2)}, u32[]{:S(2)}) collective-permute-start(bf16[64,1024]{1,0:T(8,128)(2,1)S(1)} %slice.45), channel_id=1, source_target_pairs={{0,28},{4,0},{8,4},{12,8},{16,12},{20,16},{24,20},{28,24},{1,29},{... | collective-permute-start | bytes 393224 | tf_op jit(solution)/shard_map/ppermute | solution.py:137
  73.5 8.1 %collective-permute-start.9 = (bf16[64,1024]{1,0:T(8,128)(2,1)S(1)}, bf16[64,1024]{1,0:T(8,128)(2,1)S(1)}, u32[]{:S(2)}, u32[]{:S(2)}) collective-permute-start(bf16[64,1024]{1,0:T(8,128)(2,1)S(1)} %slice.44), channel_id=1, source_target_pairs={{0,4},{4,8},{8,12},{12,16},{16,20},{20,24},{24,28},{28,0},{1,5},{5... | collective-permute-start | bytes 393224 | tf_op jit(solution)/shard_map/ppermute | solution.py:136
  82.3 12.1 %collective-permute-start.14 = (bf16[128,64]{0,1:T(8,128)(2,1)S(1)}, bf16[128,64]{0,1:T(8,128)(2,1)S(1)}, u32[]{:S(2)}, u32[]{:S(2)}) collective-permute-start(bf16[128,64]{0,1:T(8,128)(2,1)S(1)} %fusion.19), channel_id=1, source_target_pairs={{0,3},{1,0},{2,7},{3,4},{4,11},{5,8},{6,15},{7,12},{8,19},{9,16},{... | collective-permute-start | bytes 49160 | tf_op jit(solution)/shard_map/ppermute | solution.py:140
  86.5 9.5 %collective-permute-start.13 = (bf16[128,64]{0,1:T(8,128)(2,1)S(1)}, bf16[128,64]{0,1:T(8,128)(2,1)S(1)}, u32[]{:S(2)}, u32[]{:S(2)}) collective-permute-start(bf16[128,64]{0,1:T(8,128)(2,1)S(1)} %fusion.19), channel_id=1, source_target_pairs={{0,2},{1,3},{2,6},{3,7},{4,10},{5,11},{6,14},{7,15},{8,18},{9,19},... | collective-permute-start | bytes 49160 | tf_op jit(solution)/shard_map/ppermute | solution.py:140
  91.2 11.3 %collective-permute-start.12 = (bf16[128,64]{0,1:T(8,128)(2,1)S(1)}, bf16[128,64]{0,1:T(8,128)(2,1)S(1)}, u32[]{:S(2)}, u32[]{:S(2)}) collective-permute-start(bf16[128,64]{0,1:T(8,128)(2,1)S(1)} %fusion.19), channel_id=1, source_target_pairs={{0,1},{1,2},{2,5},{3,6},{4,9},{5,10},{6,13},{7,14},{8,17},{9,18},{... | collective-permute-start | bytes 49160 | tf_op jit(solution)/shard_map/ppermute | solution.py:140
  93.2 9.4 %collective-permute-start.11 = (bf16[128,64]{0,1:T(8,128)(2,1)S(1)}, bf16[128,64]{0,1:T(8,128)(2,1)S(1)}, u32[]{:S(2)}, u32[]{:S(2)}) collective-permute-start(bf16[128,64]{0,1:T(8,128)(2,1)S(1)} %fusion.19), channel_id=1, source_target_pairs={{0,0},{1,1},{2,4},{3,5},{4,8},{5,9},{6,12},{7,13},{8,16},{9,17},{1... | collective-permute-start | bytes 49160 | tf_op jit(solution)/shard_map/ppermute | solution.py:140
  108.4 41.5 %copy-start.2 = (s32[1024]{0:T(1024)S(1)}, s32[1024]{0:T(1024)}, u32[]{:S(2)}) copy-start(s32[1024]{0:T(1024)} %param.10) | copy-start | bytes 12292
  142.3 35.8 %all-to-all-start.1 = ((bf16[32,32,256]{2,1,0:T(8,128)(2,1)}), bf16[32,32,256]{2,1,0:T(8,128)(2,1)S(1)}, u32[]{:S(2)}, u32[]{:S(2)}) async-start(bf16[32,32,256]{2,1,0:T(8,128)(2,1)} %broadcast_in_dim.12), calls=%async_computation.2 | async-start | bytes 1048576 | tf_op jit(solution)/shard_map/all_to_all | solution.py:162
  163.9 14.4 %collective-permute-start.15 = (bf16[96,256]{1,0:T(8,128)(2,1)S(1)}, bf16[96,256]{1,0:T(8,128)(2,1)S(1)}, u32[]{:S(2)}, u32[]{:S(2)}) collective-permute-start(bf16[96,256]{1,0:T(8,128)(2,1)S(1)} %get-tuple-element.11), channel_id=1, source_target_pairs={{0,1},{1,2},{2,3},{3,0},{4,5},{5,6},{6,7},{7,4},{8,9},{9,10},{10,1... | collective-permute-start | bytes 147464 | tf_op jit(solution)/shard_map/ppermute | solution.py:106
  167.8 10.5 %collective-permute-start.17 = (bf16[96,256]{1,0:T(8,128)(2,1)S(1)}, bf16[96,256]{1,0:T(8,128)(2,1)S(1)}, u32[]{:S(2)}, u32[]{:S(2)}) collective-permute-start(bf16[96,256]{1,0:T(8,128)(2,1)S(1)} %get-tuple-element.12), channel_id=1, source_target_pairs={{0,3},{1,0},{2,1},{3,2},{4,7},{5,4},{6,5},{7,6},{8,11},{9,8},{10,9... | collective-permute-start | bytes 147464 | tf_op jit(solution)/shard_map/ppermute | solution.py:106
  171.9 9.9 %collective-permute-start.16 = (bf16[96,256]{1,0:T(8,128)(2,1)S(1)}, bf16[96,256]{1,0:T(8,128)(2,1)S(1)}, u32[]{:S(2)}, u32[]{:S(2)}) collective-permute-start(bf16[96,256]{1,0:T(8,128)(2,1)S(1)} %get-tuple-element.13), channel_id=1, source_target_pairs={{0,2},{1,3},{2,0},{3,1},{4,6},{5,7},{6,4},{7,5},{8,10},{9,11},{10,... | collective-permute-start | bytes 147464 | tf_op jit(solution)/shard_map/ppermute | solution.py:106
Sparse Core Ops, SparseCore 0:
  108.5 54.5 reduce-scatter.1

commit v3 on v1

v3 whole, which is shorter than its diff:
```python
import math

import jax
import jax.numpy as jnp
from jax import lax
from jax.sharding import Mesh
from jax.sharding import PartitionSpec as P

HQ = 64
KVH = 8
HD = 128
KEEP = 96
MOVE = 32
RECV = 64

N_Z = 8
N_Y = 4
DP = ("x", "yl", "core")
TENSOR = ("z", "yh")

rope_base = 500000.0


def rotation_tables(positions):
    half = HD // 2
    freqs = rope_base ** (-(jnp.arange(half, dtype=jnp.float32) * 2.0 / HD))
    angles = positions.astype(jnp.float32)[:, None] * freqs[None, :]
    return (jnp.cos(angles), jnp.sin(angles))


def rotate(values, cosine, sine):
    half = HD // 2
    first = values[..., :half]
    second = values[..., half:]
    cosine = cosine[:, None, :]
    sine = sine[:, None, :]
    return jnp.concatenate(
        [first * cosine - second * sine, second * cosine + first * sine], axis=-1
    )


def doc_layout(segment):
    same = segment[:, None] == segment[None, :]
    indices = jnp.arange(segment.shape[0])
    earlier = indices[None, :] < indices[:, None]
    positions = jnp.sum(jnp.logical_and(same, earlier), axis=1)
    visible = jnp.logical_and(same, indices[None, :] <= indices[:, None])
    return (positions, visible)


def attend(query_rot, key_rot, value_rows, visible):
    count = query_rot.shape[0]
    scores = jnp.einsum(
        "rkgd,ckd->kgrc", query_rot, key_rot, preferred_element_type=jnp.float32
    ) / math.sqrt(HD)
    scores = jnp.where(visible[None, None], scores, -1e30)
    top = jnp.max(scores, axis=-1, keepdims=True)
    expd = jnp.exp(scores - top)
    weights = (expd / jnp.sum(expd, axis=-1, keepdims=True)).astype(jnp.bfloat16)
    result = jnp.einsum("kgrc,ckd->rkgd", weights, value_rows, preferred_element_type=jnp.float32)
    return result.astype(jnp.bfloat16).reshape(count, -1)


def ring(n, k):
    return [(i, (i + k) % n) for i in range(n)]


def keyval_routes(k):
    half = N_Z * N_Y // 2
    return [
        (s, N_Y * ((s % half) // 2) + (s % 2 + 2 * (s // half) + k) % N_Y) for s in range(2 * half)
    ]


def sum_pieces(pieces):
    return jnp.sum(pieces.astype(jnp.float32), axis=0).astype(jnp.bfloat16)


def scatter_sum(attended, w_out):
    n = N_Z * N_Y
    partial = jnp.einsum(
        "rk,kdn->drn",
        attended,
        w_out.reshape(w_out.shape[0], n, -1),
        preferred_element_type=jnp.float32,
    ).astype(jnp.bfloat16)
    return sum_pieces(lax.all_to_all(partial, TENSOR, 0, 0, tiled=True))


def move_keyval(keyval):
    rows = keyval.shape[0]
    y_me = lax.axis_index("yh")
    pieces = [lax.ppermute(keyval, TENSOR, keyval_routes(k)) for k in range(N_Y)]
    stack = jnp.stack(pieces)
    roles = [lax.dynamic_index_in_dim(stack, (y_me - r) % N_Y, 0, False) for r in range(N_Y)]
    key = jnp.concatenate(roles[:2], axis=1).reshape(rows, 1, HD)
    value = jnp.concatenate(roles[2:], axis=1).reshape(rows, 1, HD)
    return key, value


def heads_of(features, labels, w_query, w_keyval):
    rows = features.shape[0]
    keyval = jnp.dot(features, w_keyval, preferred_element_type=jnp.float32).astype(jnp.bfloat16)
    key, value = move_keyval(keyval)
    query = jnp.dot(features, w_query, preferred_element_type=jnp.float32)
    positions, visible = doc_layout(labels)
    cosine, sine = rotation_tables(positions)
    query_rot = rotate(query.reshape(rows, 2, HD), cosine, sine).astype(jnp.bfloat16)
    key_rot = rotate(key.astype(jnp.float32), cosine, sine).astype(jnp.bfloat16)
    return attend(query_rot.reshape(rows, 1, 2, HD), key_rot, value, visible)


def to_all(rows, axes, n):
    sent = jnp.broadcast_to(rows[None], (n,) + rows.shape)
    return lax.all_to_all(sent, axes, 0, 0, tiled=True)


def shards(activations, w_query, w_keyval, w_out, targets, segments):
    block = lax.axis_index(DP)
    n_tensor = N_Z * N_Y

    kept = lax.all_gather(activations[:KEEP], "yh", axis=1, tiled=True)
    kept = lax.all_gather(kept, "z", axis=1, tiled=True)

    tails = to_all(activations[KEEP:], TENSOR, n_tensor)
    tails = tails.transpose(1, 0, 2).reshape(MOVE, -1)
    tail_docs = lax.dynamic_slice_in_dim(targets, block * MOVE, MOVE) // RECV
    tails = heads_of(tails, tail_docs, w_query, w_keyval)
    tails = scatter_sum(tails, w_out)

    slots = lax.iota(jnp.int32, RECV)
    wanted = targets - block * RECV
    select = (slots[:, None] == wanted[None, :]).astype(jnp.bfloat16)
    n_dp = targets.shape[0] // MOVE
    tails = to_all(tails, DP, n_dp).reshape(targets.shape[0], -1)
    arrived = jnp.dot(select, tails, preferred_element_type=jnp.float32).astype(jnp.bfloat16)

    kept = heads_of(kept, segments[:KEEP], w_query, w_keyval)
    kept = scatter_sum(kept, w_out)
    return jnp.concatenate([kept, arrived], axis=0)


def solution(mesh):
    fine = Mesh(
        mesh.devices.reshape(8, 2, 2, N_Z, N_Y), ("x", "yl", "core", "z", "yh")
    )
    placed = (
        P(DP, TENSOR),
        P(None, TENSOR),
        P(None, TENSOR),
        P(TENSOR, None),
        P(),
        P(DP),
    )
    return jax.shard_map(
        shards, mesh=fine, in_specs=placed, out_specs=P(DP, TENSOR), check_vma=False
    )
```

time: 228 us -> 221 us (0.969)
  starting transfers between devices: 15.5 us -> 95.2 us
  blocking collectives: 83.7 us -> 21 us
  waiting for transfers between devices: 102 us -> 57.3 us
  matrix products: 7.22 us -> 18.7 us
  local copies, waits for them, and re-layouts: 2.33 us -> 11 us
    all_gather x3 -> x1, blocking collectives: 83.7 us -> 21 us  [shards(): kept = lax.all_gather(activations[:KEEP], 'yh', axis=1, tiled=True)]
    all_to_all x0 -> x4, starting transfers between devices: none -> 60.2 us  [the longest x2 37.4 us: to_all(): return lax.all_to_all(sent, axes, 0, 0, tiled=True)]
    all_to_all x0 -> x4, waiting for transfers between devices: none -> 57.3 us  [the longest x2 57.2 us: scatter_sum(): return sum_pieces(lax.all_to_all(partial, TENSOR, 0, 0, tiled=True))]
    all_gather x1, waiting for transfers between devices: 53.2 us -> 0.02 us  [shards(): kept = lax.all_gather(kept, 'z', axis=1, tiled=True)]
    reduce_scatter x1 -> x0, waiting for transfers between devices: 46.8 us -> none  [shards(): summed = lax.psum_scatter(partial, 'z', scatter_dimension=0, tiled=True)]
    ppermute x4 -> x8, starting transfers between devices: 15.5 us -> 34.9 us  [move_keyval(): lax.ppermute(keyval, TENSOR, keyval_routes(k))]
    dot_general x3 -> x6, matrix products: 6.59 us -> 17.5 us  [the longest x2 8 us: scatter_sum(): jnp.einsum('rk,kdn->drn', attended, w_out.reshape(w_out.shape[0], n, -1),...]
    dot_general x0 -> x1, local copies, waits for them, and re-layouts: none -> 6.34 us  [heads_of(): query = jnp.dot(features, w_query, preferred_element_type=jnp.float32)]
  transfers between devices with their start and end apart: 6 -> 13, of which waited for: 3 -> 2; matrix products, arithmetic and copies ran while one was open for 1% -> 14% of each run, Pallas kernels for 0% -> 0%
where the time goes in v3:
time: 221 us; the launch traced here: 220 us
  starting transfers between devices  95.2 us (43%)
  waiting for transfers between devices  57.3 us (26%)
  blocking collectives  21 us (10%)
  matrix products  18.7 us (8%)
  between operations  13.9 us (6%)
  local copies, waits for them, and re-layouts  11 us (5%)
  other arithmetic  3.27 us (1%)
    all_to_all x2, waiting for transfers between devices, scatter_sum(): return sum_pieces(lax.all_to_all(partial, TENSOR, 0, 0, tiled=True))  57.2 us
    all_to_all x2, starting transfers between devices, to_all(): return lax.all_to_all(sent, axes, 0, 0, tiled=True)  37.4 us
    ppermute x8, starting transfers between devices, move_keyval(): lax.ppermute(keyval, TENSOR, keyval_routes(k))  34.9 us
    all_to_all x2, starting transfers between devices, scatter_sum(): return sum_pieces(lax.all_to_all(partial, TENSOR, 0, 0, tiled=True))  22.9 us
    all_gather x1, blocking collectives, shards(): kept = lax.all_gather(activations[:KEEP], 'yh', axis=1, tiled=True)  21 us
    dot_general x2, matrix products, scatter_sum(): jnp.einsum('rk,kdn->drn', attended, w_out.reshape(w_out.shape[0], n, -1),...  8 us
    dot_general x2, matrix products, heads_of(): query = jnp.dot(features, w_query, preferred_element_type=jnp.float32)  7.02 us
    dot_general x1, local copies, waits for them, and re-layouts, heads_of(): query = jnp.dot(features, w_query, preferred_element_type=jnp.float32)  6.34 us
  transfers between devices with their start and end apart: 13, of which 2 were waited for; matrix products, arithmetic and copies ran while one was open for 14% of the time, Pallas kernels for 0%

profile of v3, /device:TPU:1, one launch (start us, length us, event | category | flops | bytes accessed | tf_op | source)
XLA Modules:
  0.0 220.4 jit_solution(11332997228011686193)
XLA Ops:
  6.5 0.8 slice.39
  7.3 0.8 broadcast_in_dim.26
  8.2 23.3 %all-to-all-start.1 = ((bf16[32,32,256]{2,1,0:T(8,128)(2,1)}), bf16[32,32,256]{2,1,0:T(8,128)(2,1)S(1)}, u32[]{:S(2)}, u32[]{:S(2)}) async-start(bf16[32,32,256]{2,1,0:T(8,128)(2,1)} %broadcast_in_dim.26), calls=%async_computation.1 | async-start | bytes 1048576 | tf_op jit(solution)/shard_map/all_to_all | solution.py:115
  31.6 0.8 slice.33
  32.4 21.0 %all_gather.6 = bf16[96,1024]{1,0:T(8,128)(2,1)} all-gather(bf16[96,256]{1,0:T(8,128)(2,1)S(1)} %slice.33), channel_id=1, replica_groups=mesh['x'=8,'yl'=2,'core'=2,'z'=8,'yh'=4] {'yh'}, dimensions={1}, use_global_device_ids=true | all-gather | bytes 245760 | tf_op jit(solution)/shard_map/all_gather | solution.py:122
  53.5 0.8 and_select_fusion
  54.3 0.1 convert_reduce_fusion.1
  54.4 6.3 %copy.43 = bf16[256,8192]{1,0:T(8,128)(2,1)} copy(bf16[256,8192]{0,1:T(8,128)(2,1)} %bitcast.113) | data formatting | bytes 8388608 | tf_op jit(solution)/shard_map/dot_general | solution.py:105
  60.8 0.1 multiply_cosine_fusion.2
  61.0 0.4 convolution_convert_fusion.4
  61.4 0.7 collective-permute-start.4
  62.1 5.0 %collective-permute-start.5 = (bf16[32,64]{1,0:T(8,128)(2,1)S(1)}, bf16[32,64]{1,0:T(8,128)(2,1)S(1)}, u32[]{:S(2)}, u32[]{:S(2)}) collective-permute-start(bf16[32,64]{1,0:T(8,128)(2,1)S(1)} %convolution_convert_fusion.4), channel_id=1, source_target_pairs={{0,1},{1,2},{2,5},{3,6},{4,9},{5,10},{6,13},{7,14},{8,17},{9,18},{... | collective-permute-start | bytes 12296 | tf_op jit(solution)/shard_map/ppermute | solution.py:93
  67.1 8.7 %collective-permute-start.6 = (bf16[32,64]{1,0:T(8,128)(2,1)S(1)}, bf16[32,64]{1,0:T(8,128)(2,1)S(1)}, u32[]{:S(2)}, u32[]{:S(2)}) collective-permute-start(bf16[32,64]{1,0:T(8,128)(2,1)S(1)} %convolution_convert_fusion.4), channel_id=1, source_target_pairs={{0,2},{1,3},{2,6},{3,7},{4,10},{5,11},{6,14},{7,15},{8,18},{9,19},... | collective-permute-start | bytes 12296 | tf_op jit(solution)/shard_map/ppermute | solution.py:93
  75.8 4.2 %collective-permute-start.7 = (bf16[32,64]{1,0:T(8,128)(2,1)S(1)}, bf16[32,64]{1,0:T(8,128)(2,1)S(1)}, u32[]{:S(2)}, u32[]{:S(2)}) collective-permute-start(bf16[32,64]{1,0:T(8,128)(2,1)S(1)} %convolution_convert_fusion.4), channel_id=1, source_target_pairs={{0,3},{1,0},{2,7},{3,4},{4,11},{5,8},{6,15},{7,12},{8,19},{9,16},{... | collective-permute-start | bytes 12296 | tf_op jit(solution)/shard_map/ppermute | solution.py:93
  80.0 0.3 copy.36
  80.3 0.2 reshape.469
  80.6 3.6 %fusion.71 = f32[32,2,128]{2,0,1:T(8,128)S(1)} fusion(bf16[32,8192,1]{1,0,2:T(8,128)(2,1)S(1)} %reshape.469, bf16[2,128,8192]{2,1,0:T(8,128)(2,1)} %bitcast.116), kind=kOutput, calls=%fused_computation.120 | convolution fusion | flops 134217728 | bytes 4751360 | tf_op jit(solution)/shard_map/dot_general | solution.py:105
  84.4 0.1 fusion.62
  84.5 0.3 fusion.68
  84.8 0.2 fusion.23
  85.1 3.9 %fusion.15 = bf16[32,32,256]{2,1,0:T(8,128)(2,1)} fusion(bf16[32,256,1]{1,0,2:T(8,128)(2,1)S(1)} %reshape.472, bf16[32,32,8,256]{3,2,1,0:T(8,128)(2,1)} %bitcast.114), kind=kOutput, calls=%fused_computation.9 | convolution fusion | flops 134479872 | bytes 4734976 | tf_op jit(solution)/shard_map/rk,kdn->drn/dot_general | solution.py:81
  88.9 11.8 %all-to-all-start.2 = ((bf16[32,32,256]{2,1,0:T(8,128)(2,1)}), bf16[32,32,256]{2,1,0:T(8,128)(2,1)S(1)}, u32[]{:S(2)}, u32[]{:S(2)}) async-start(bf16[32,32,256]{2,1,0:T(8,128)(2,1)} %fusion.15), calls=%async_computation.2 | async-start | bytes 1048576 | tf_op jit(solution)/shard_map/all_to_all | solution.py:87
  100.8 0.1 convert_reduce_fusion
  101.0 0.2 multiply_cosine_fusion
  101.2 13.6 %all-to-all-done.2 = bf16[32,32,256]{2,1,0:T(8,128)(2,1)S(1)} async-done(((bf16[32,32,256]{2,1,0:T(8,128)(2,1)}), bf16[32,32,256]{2,1,0:T(8,128)(2,1)S(1)}, u32[]{:S(2)}, u32[]{:S(2)}) %all-to-all-start.2) | async-done | bytes 524320 | tf_op jit(solution)/shard_map/all_to_all | solution.py:87
  115.0 0.8 broadcast_in_dim.29
  115.8 14.0 %all-to-all-start.3 = ((bf16[32,32,256]{2,1,0:T(8,128)(2,1)}), bf16[32,32,256]{2,1,0:T(8,128)(2,1)S(1)}, u32[]{:S(2)}, u32[]{:S(2)}) async-start(bf16[32,32,256]{2,1,0:T(8,128)(2,1)} %broadcast_in_dim.29), calls=%async_computation.3 | async-start | bytes 1048576 | tf_op jit(solution)/shard_map/all_to_all | solution.py:115
  129.9 2.1 convolution_convert_fusion.3
  132.0 0.7 collective-permute-start
  132.6 2.4 %collective-permute-start.1 = (bf16[96,64]{0,1:T(8,128)(2,1)S(1)}, bf16[96,64]{0,1:T(8,128)(2,1)S(1)}, u32[]{:S(2)}, u32[]{:S(2)}) collective-permute-start(bf16[96,64]{0,1:T(8,128)(2,1)S(1)} %convolution_convert_fusion.3), channel_id=1, source_target_pairs={{0,1},{1,2},{2,5},{3,6},{4,9},{5,10},{6,13},{7,14},{8,17},{9,18},{... | collective-permute-start | bytes 36872 | tf_op jit(solution)/shard_map/ppermute | solution.py:93
  135.1 8.7 %collective-permute-start.2 = (bf16[96,64]{0,1:T(8,128)(2,1)S(1)}, bf16[96,64]{0,1:T(8,128)(2,1)S(1)}, u32[]{:S(2)}, u32[]{:S(2)}) collective-permute-start(bf16[96,64]{0,1:T(8,128)(2,1)S(1)} %convolution_convert_fusion.3), channel_id=1, source_target_pairs={{0,2},{1,3},{2,6},{3,7},{4,10},{5,11},{6,14},{7,15},{8,18},{9,19},... | collective-permute-start | bytes 36872 | tf_op jit(solution)/shard_map/ppermute | solution.py:93
  143.7 4.6 %collective-permute-start.3 = (bf16[96,64]{0,1:T(8,128)(2,1)S(1)}, bf16[96,64]{0,1:T(8,128)(2,1)S(1)}, u32[]{:S(2)}, u32[]{:S(2)}) collective-permute-start(bf16[96,64]{0,1:T(8,128)(2,1)S(1)} %convolution_convert_fusion.3), channel_id=1, source_target_pairs={{0,3},{1,0},{2,7},{3,4},{4,11},{5,8},{6,15},{7,12},{8,19},{9,16},{... | collective-permute-start | bytes 36872 | tf_op jit(solution)/shard_map/ppermute | solution.py:93
  148.3 3.5 %fusion.70 = f32[96,256]{1,0:T(8,128)S(1)} fusion(bf16[96,8192]{1,0:T(8,128)(2,1)} %all-gather.2.cloned.1.call-done, bf16[8192,256]{1,0:T(8,128)(2,1)} %param.7), kind=kOutput, calls=%fused_computation.119 | convolution fusion | flops 402653184 | bytes 5865472 | tf_op jit(solution)/shard_map/dot_general | solution.py:105
  151.9 0.2 fusion.67
  152.2 0.1 copy.29
  152.3 0.1 copy.30
  152.4 0.1 copy.27
  152.5 0.1 copy.28
  152.6 0.1 maximum_convert_fusion
  152.7 0.3 fusion.44
  153.0 0.3 fusion.69
  153.3 0.2 fusion.20
  153.6 4.1 %fusion.9 = bf16[32,96,256]{2,1,0:T(8,128)(2,1)} fusion(bf16[96,256,1]{1,0,2:T(8,128)(2,1)S(1)} %reshape.468, bf16[32,32,8,256]{3,2,1,0:T(8,128)(2,1)} %bitcast.115), kind=kOutput, calls=%fused_computation.7 | convolution fusion | flops 403439616 | bytes 5816320 | tf_op jit(solution)/shard_map/rk,kdn->drn/dot_general | solution.py:81
  157.8 11.0 %all-to-all-start = ((bf16[32,96,256]{2,1,0:T(8,128)(2,1)}), bf16[32,96,256]{2,1,0:T(8,128)(2,1)S(1)}, u32[]{:S(2)}, u32[]{:S(2)}) async-start(bf16[32,96,256]{2,1,0:T(8,128)(2,1)} %fusion.9), calls=%async_computation | async-start | bytes 3145728 | tf_op jit(solution)/shard_map/all_to_all | solution.py:87
  168.9 0.2 convolution_convert_fusion.1
  169.1 43.6 %all-to-all-done = bf16[32,96,256]{2,1,0:T(8,128)(2,1)S(1)} async-done(((bf16[32,96,256]{2,1,0:T(8,128)(2,1)}), bf16[32,96,256]{2,1,0:T(8,128)(2,1)S(1)}, u32[]{:S(2)}, u32[]{:S(2)}) %all-to-all-start) | async-done | bytes 1572896 | tf_op jit(solution)/shard_map/all_to_all | solution.py:87
  212.7 0.2 reduce_sum.62
  212.9 0.6 pad_maximum_fusion
  (42 shorter events, 0.9 us)
Async XLA Ops:
  6.5 54.5 %copy-start = (bf16[8192,64]{0,1:T(8,128)(2,1)S(1)}, bf16[8192,64]{0,1:T(8,128)(2,1)}, u32[]{:S(2)}) copy-start(bf16[8192,64]{0,1:T(8,128)(2,1)} %param.8) | copy-start | bytes 3145732
  8.2 52.8 %all-to-all-start.1 = ((bf16[32,32,256]{2,1,0:T(8,128)(2,1)}), bf16[32,32,256]{2,1,0:T(8,128)(2,1)S(1)}, u32[]{:S(2)}, u32[]{:S(2)}) async-start(bf16[32,32,256]{2,1,0:T(8,128)(2,1)} %broadcast_in_dim.26), calls=%async_computation.1 | async-start | bytes 1048576 | tf_op jit(solution)/shard_map/all_to_all | solution.py:115
  31.5 98.3 %all-gather.2.cloned.1.call-start = ((), (), s32[]{:S(2)}) async-start(), calls=%async_computation.4 | async-start | bytes 1769472 | tf_op jit(solution)/shard_map/all_gather | solution.py:123
  61.4 22.8 %collective-permute-start.4 = (bf16[32,64]{1,0:T(8,128)(2,1)S(1)}, bf16[32,64]{1,0:T(8,128)(2,1)S(1)}, u32[]{:S(2)}, u32[]{:S(2)}) collective-permute-start(bf16[32,64]{1,0:T(8,128)(2,1)S(1)} %convolution_convert_fusion.4), channel_id=1, source_target_pairs={{0,0},{1,1},{2,4},{3,5},{4,8},{5,9},{6,12},{7,13},{8,16},{9,17},{1... | collective-permute-start | bytes 12296 | tf_op jit(solution)/shard_map/ppermute | solution.py:93
  62.1 22.1 %collective-permute-start.5 = (bf16[32,64]{1,0:T(8,128)(2,1)S(1)}, bf16[32,64]{1,0:T(8,128)(2,1)S(1)}, u32[]{:S(2)}, u32[]{:S(2)}) collective-permute-start(bf16[32,64]{1,0:T(8,128)(2,1)S(1)} %convolution_convert_fusion.4), channel_id=1, source_target_pairs={{0,1},{1,2},{2,5},{3,6},{4,9},{5,10},{6,13},{7,14},{8,17},{9,18},{... | collective-permute-start | bytes 12296 | tf_op jit(solution)/shard_map/ppermute | solution.py:93
  67.1 17.1 %collective-permute-start.6 = (bf16[32,64]{1,0:T(8,128)(2,1)S(1)}, bf16[32,64]{1,0:T(8,128)(2,1)S(1)}, u32[]{:S(2)}, u32[]{:S(2)}) collective-permute-start(bf16[32,64]{1,0:T(8,128)(2,1)S(1)} %convolution_convert_fusion.4), channel_id=1, source_target_pairs={{0,2},{1,3},{2,6},{3,7},{4,10},{5,11},{6,14},{7,15},{8,18},{9,19},... | collective-permute-start | bytes 12296 | tf_op jit(solution)/shard_map/ppermute | solution.py:93
  75.8 8.4 %collective-permute-start.7 = (bf16[32,64]{1,0:T(8,128)(2,1)S(1)}, bf16[32,64]{1,0:T(8,128)(2,1)S(1)}, u32[]{:S(2)}, u32[]{:S(2)}) collective-permute-start(bf16[32,64]{1,0:T(8,128)(2,1)S(1)} %convolution_convert_fusion.4), channel_id=1, source_target_pairs={{0,3},{1,0},{2,7},{3,4},{4,11},{5,8},{6,15},{7,12},{8,19},{9,16},{... | collective-permute-start | bytes 12296 | tf_op jit(solution)/shard_map/ppermute | solution.py:93
  84.1 16.6 %copy-start.2 = (s32[160]{0:T(256)S(1)}, s32[160]{0:T(256)}, u32[]{:S(2)}) copy-start(s32[160]{0:T(256)} %param.11) | copy-start | bytes 1924
  88.9 25.9 %all-to-all-start.2 = ((bf16[32,32,256]{2,1,0:T(8,128)(2,1)}), bf16[32,32,256]{2,1,0:T(8,128)(2,1)S(1)}, u32[]{:S(2)}, u32[]{:S(2)}) async-start(bf16[32,32,256]{2,1,0:T(8,128)(2,1)} %fusion.15), calls=%async_computation.2 | async-start | bytes 1048576 | tf_op jit(solution)/shard_map/all_to_all | solution.py:87
  115.8 42.0 %all-to-all-start.3 = ((bf16[32,32,256]{2,1,0:T(8,128)(2,1)}), bf16[32,32,256]{2,1,0:T(8,128)(2,1)S(1)}, u32[]{:S(2)}, u32[]{:S(2)}) async-start(bf16[32,32,256]{2,1,0:T(8,128)(2,1)} %broadcast_in_dim.29), calls=%async_computation.3 | async-start | bytes 1048576 | tf_op jit(solution)/shard_map/all_to_all | solution.py:115
  132.0 20.1 %collective-permute-start = (bf16[96,64]{0,1:T(8,128)(2,1)S(1)}, bf16[96,64]{0,1:T(8,128)(2,1)S(1)}, u32[]{:S(2)}, u32[]{:S(2)}) collective-permute-start(bf16[96,64]{0,1:T(8,128)(2,1)S(1)} %convolution_convert_fusion.3), channel_id=1, source_target_pairs={{0,0},{1,1},{2,4},{3,5},{4,8},{5,9},{6,12},{7,13},{8,16},{9,17},{1... | collective-permute-start | bytes 36872 | tf_op jit(solution)/shard_map/ppermute | solution.py:93
  132.6 19.5 %collective-permute-start.1 = (bf16[96,64]{0,1:T(8,128)(2,1)S(1)}, bf16[96,64]{0,1:T(8,128)(2,1)S(1)}, u32[]{:S(2)}, u32[]{:S(2)}) collective-permute-start(bf16[96,64]{0,1:T(8,128)(2,1)S(1)} %convolution_convert_fusion.3), channel_id=1, source_target_pairs={{0,1},{1,2},{2,5},{3,6},{4,9},{5,10},{6,13},{7,14},{8,17},{9,18},{... | collective-permute-start | bytes 36872 | tf_op jit(solution)/shard_map/ppermute | solution.py:93
  135.1 17.0 %collective-permute-start.2 = (bf16[96,64]{0,1:T(8,128)(2,1)S(1)}, bf16[96,64]{0,1:T(8,128)(2,1)S(1)}, u32[]{:S(2)}, u32[]{:S(2)}) collective-permute-start(bf16[96,64]{0,1:T(8,128)(2,1)S(1)} %convolution_convert_fusion.3), channel_id=1, source_target_pairs={{0,2},{1,3},{2,6},{3,7},{4,10},{5,11},{6,14},{7,15},{8,18},{9,19},... | collective-permute-start | bytes 36872 | tf_op jit(solution)/shard_map/ppermute | solution.py:93
  143.7 8.4 %collective-permute-start.3 = (bf16[96,64]{0,1:T(8,128)(2,1)S(1)}, bf16[96,64]{0,1:T(8,128)(2,1)S(1)}, u32[]{:S(2)}, u32[]{:S(2)}) collective-permute-start(bf16[96,64]{0,1:T(8,128)(2,1)S(1)} %convolution_convert_fusion.3), channel_id=1, source_target_pairs={{0,3},{1,0},{2,7},{3,4},{4,11},{5,8},{6,15},{7,12},{8,19},{9,16},{... | collective-permute-start | bytes 36872 | tf_op jit(solution)/shard_map/ppermute | solution.py:93
  153.6 15.2 %copy-start.1 = (s32[1024]{0:T(1024)S(1)}, s32[1024]{0:T(1024)}, u32[]{:S(2)}) copy-start(s32[1024]{0:T(1024)} %param.10) | copy-start | bytes 12292
  157.8 54.9 %all-to-all-start = ((bf16[32,96,256]{2,1,0:T(8,128)(2,1)}), bf16[32,96,256]{2,1,0:T(8,128)(2,1)S(1)}, u32[]{:S(2)}, u32[]{:S(2)}) async-start(bf16[32,96,256]{2,1,0:T(8,128)(2,1)} %fusion.9), calls=%async_computation | async-start | bytes 3145728 | tf_op jit(solution)/shard_map/all_to_all | solution.py:87
Sparse Core Ops, SparseCore 0:
  53.6 43.8 all-gather.1

commit v4 on v2

--- a/solution.py
+++ b/solution.py
@@ -3,6 +3,8 @@
 import jax
 import jax.numpy as jnp
 from jax import lax
+from jax.experimental import pallas as pl
+from jax.experimental.pallas import tpu as pltpu
 from jax.sharding import Mesh
 from jax.sharding import PartitionSpec as P
 
@@ -66,46 +68,80 @@
     return [(i, (i + k) % n) for i in range(n)]
 
 
-def keyval_routes(k):
+def move_keyval(keyval):
+    rows = keyval.shape[0]
+    y_me = lax.axis_index("yh")
+    other = lax.ppermute(keyval, "yh", [(i, i ^ 1) for i in range(N_Y)])
+    low = y_me % 2 == 0
+    whole = jnp.concatenate(
+        [jnp.where(low, keyval, other), jnp.where(low, other, keyval)], axis=1
+    )
     half = N_Z * N_Y // 2
-    return [
-        (s, N_Y * ((s % half) // 2) + (s % 2 + 2 * (s // half) + k) % N_Y) for s in range(2 * half)
-    ]
-
-
-def gather_y(rows):
-    me = lax.axis_index("yh")
-    pieces = [rows] + [lax.ppermute(rows, "yh", ring(N_Y, k)) for k in range(1, N_Y)]
-    stack = jnp.stack(pieces)
-    return jnp.concatenate(
-        [lax.dynamic_index_in_dim(stack, (me - j) % N_Y, 0, False) for j in range(N_Y)], axis=1
-    )
+
+    def routes(flip):
+        return [
+            (s, N_Y * ((s % half) // 2) + s % 2 + 2 * ((s // half) ^ flip)) for s in range(2 * half)
+        ]
+
+    straight = lax.ppermute(whole, TENSOR, routes(0))
+    crossed = lax.ppermute(whole, TENSOR, routes(1))
+    first = y_me < 2
+    key = jnp.where(first, straight, crossed)
+    value = jnp.where(first, crossed, straight)
+    return key.reshape(rows, 1, HD), value.reshape(rows, 1, HD)
 
 
 def sum_pieces(pieces):
     return jnp.sum(pieces.astype(jnp.float32), axis=0).astype(jnp.bfloat16)
 
 
-def scatter_sum(attended, w_out):
+def output_kernel(attended_ref, w_ref, kept_ref, tail_ref):
+    rows = jnp.dot(attended_ref[...], w_ref[...], preferred_element_type=jnp.float32)
+    rows = rows.astype(jnp.bfloat16)
+    kept_ref[...] = rows[:KEEP]
+    width = tail_ref.shape[2]
+    for d in range(tail_ref.shape[0]):
+        tail_ref[d] = rows[KEEP:, d * width : (d + 1) * width]
+
+
+def output_partials(attended, w_out):
+    depth, wide = w_out.shape
     n = N_Z * N_Y
-    partial = jnp.einsum(
-        "rk,kdn->drn",
-        attended,
-        w_out.reshape(w_out.shape[0], n, -1),
-        preferred_element_type=jnp.float32,
-    ).astype(jnp.bfloat16)
-    return sum_pieces(lax.all_to_all(partial, TENSOR, 0, 0, tiled=True))
+    return pl.pallas_call(
+        output_kernel,
+        grid=(N_Z,),
+        in_specs=[
+            pl.BlockSpec((KEEP + MOVE, depth), lambda i: (0, 0)),
+            pl.BlockSpec((depth, wide // N_Z), lambda i: (0, i)),
+        ],
+        out_specs=[
+            pl.BlockSpec((KEEP, wide // N_Z), lambda i: (0, i)),
+            pl.BlockSpec((N_Y, MOVE, wide // n), lambda i: (i, 0, 0)),
+        ],
+        out_shape=[
+            jax.ShapeDtypeStruct((KEEP, wide), jnp.bfloat16),
+            jax.ShapeDtypeStruct((n, MOVE, wide // n), jnp.bfloat16),
+        ],
+        compiler_params=pltpu.CompilerParams(vmem_limit_bytes=16 * 1024 * 1024),
+    )(attended, w_out)
 
 
 def sum_over_y(rows):
     me = lax.axis_index("yh")
     width = rows.shape[1] // N_Y
-    total = lax.dynamic_slice_in_dim(rows, me * width, width, 1).astype(jnp.float32)
-    for k in range(1, N_Y):
-        piece = lax.dynamic_slice_in_dim(rows, lax.rem(me + k, N_Y) * width, width, 1)
-        piece = lax.ppermute(piece, "yh", [(i, (i + k) % N_Y) for i in range(N_Y)])
-        total = total + piece.astype(jnp.float32)
-    return total.astype(jnp.bfloat16)
+
+    def part(y):
+        return lax.dynamic_slice_in_dim(rows, y * width, width, 1)
+
+    near, far = me ^ 1, me ^ 2
+    sent = jnp.concatenate([part(near), part(near ^ 2)], axis=1)
+    held = jnp.concatenate([part(me), part(far)], axis=1)
+    got = lax.ppermute(sent, "yh", [(i, i ^ 1) for i in range(N_Y)])
+    held = held.astype(jnp.float32) + got.astype(jnp.float32)
+    got = lax.ppermute(
+        held[:, width:].astype(jnp.bfloat16), "yh", [(i, i ^ 2) for i in range(N_Y)]
+    )
+    return (held[:, :width] + got.astype(jnp.float32)).astype(jnp.bfloat16)
 
 
 def shards(activations, w_query, w_keyval, w_out, targets, segments):
@@ -116,8 +152,7 @@
     cosine, sine = rotation_tables(positions)
 
     z_me = lax.axis_index("z")
-    y_me = lax.axis_index("yh")
-    own = gather_y(activations)
+    own = lax.all_gather(activations, "yh", axis=1, tiled=True)
     depth = own.shape[1]
 
     def times(weight, chunk, k):
@@ -137,22 +172,16 @@
     down = lax.ppermute(down[half:], "z", ring(N_Z, -1))
     last = jnp.concatenate([up, down], axis=0)
     keyval = (keyval + times(w_keyval, last, N_Z // 2)).astype(jnp.bfloat16)
-    pieces = [lax.ppermute(keyval, TENSOR, keyval_routes(k)) for k in range(N_Y)]
+    key, value = move_keyval(keyval)
     query = query + times(w_query, last, N_Z // 2)
 
-    stack = jnp.stack(pieces)
-    roles = [lax.dynamic_index_in_dim(stack, (y_me - r) % N_Y, 0, False) for r in range(N_Y)]
-    key = jnp.concatenate(roles[:2], axis=1).reshape(SEQ, 1, HD)
-    value = jnp.concatenate(roles[2:], axis=1).reshape(SEQ, 1, HD)
     query_rot = rotate(query.reshape(SEQ, 2, HD), cosine, sine).astype(jnp.bfloat16)
     key_rot = rotate(key.astype(jnp.float32), cosine, sine).astype(jnp.bfloat16)
     attended = attend(query_rot.reshape(SEQ, 1, 2, HD), key_rot, value, visible)
 
-    partial = lax.dot_general(
-        w_out, attended[:KEEP], (((0,), (1,)), ((), ())), preferred_element_type=jnp.float32
-    ).astype(jnp.bfloat16)
-    kept = lax.psum_scatter(partial, "z", scatter_dimension=0, tiled=True)
-    moving = scatter_sum(attended[KEEP:], w_out)
+    kept, moving = output_partials(attended, w_out)
+    kept = lax.psum_scatter(kept.T, "z", scatter_dimension=0, tiled=True)
+    moving = sum_pieces(lax.all_to_all(moving, TENSOR, 0, 0, tiled=True))
     kept = sum_over_y(kept.T)
 
     slots = lax.iota(jnp.int32, RECV)

time: 191 us -> 183 us (0.958)
  the two profiles are of different devices: /device:TPU:2 before, /device:TPU:16 now
where the time goes in v4:
time: 183 us; the launch traced here: 182 us
  starting transfers between devices  69.4 us (38%)
  blocking collectives  40.6 us (22%)
  waiting for transfers between devices  38.2 us (21%)
  between operations  14 us (8%)
  matrix products  8.34 us (5%)
  local copies, waits for them, and re-layouts  5 us (3%)
  Pallas kernels  4.18 us (2%)
  other arithmetic  2.44 us (1%)
    ppermute x3, starting transfers between devices, shards(): down = lax.ppermute(down, 'z', ring(N_Z, -1))  27.6 us
    all_to_all x1, blocking collectives, shards(): moving = sum_pieces(lax.all_to_all(moving, TENSOR, 0, 0, tiled=True))  23.9 us
    all_gather x1, blocking collectives, shards(): own = lax.all_gather(activations, 'yh', axis=1, tiled=True)  16.6 us
    reduce_scatter x1, waiting for transfers between devices, shards(): kept = lax.psum_scatter(kept.T, 'z', scatter_dimension=0, tiled=True)  13.5 us
    all_to_all x1, starting transfers between devices, shards(): lax.all_to_all(tails, DP, 0, 0, tiled=True).reshape(targets.shape[0], -1)  8.41 us
    dot_general x16, matrix products, times(): return jnp.dot(chunk, rows, preferred_element_type=jnp.float32)  7.71 us
    ppermute x1, starting transfers between devices, move_keyval(): crossed = lax.ppermute(whole, TENSOR, routes(1))  7.34 us
    ppermute x1, waiting for transfers between devices, move_keyval(): crossed = lax.ppermute(whole, TENSOR, routes(1))  6.79 us
  transfers between devices with their start and end apart: 15, of which 8 were waited for; matrix products, arithmetic and copies ran while one was open for 6% of the time, Pallas kernels for 0%

profile of v4, /device:TPU:16, one launch (start us, length us, event | category | flops | bytes accessed | tf_op | source)
XLA Modules:
  0.0 182.2 jit_solution(242534974791228031)
XLA Ops:
  6.5 16.6 %all_gather.3 = bf16[128,1024]{1,0:T(8,128)(2,1)S(1)} all-gather(bf16[128,256]{1,0:T(8,128)(2,1)} %param.6), channel_id=1, replica_groups=mesh['x'=8,'yl'=2,'core'=2,'z'=8,'yh'=4] {'yh'}, dimensions={1}, use_global_device_ids=true | all-gather | bytes 327680 | tf_op jit(solution)/shard_map/all_gather | solution.py:155
  23.2 17.4 %collective-permute-start.1 = (bf16[128,1024]{1,0:T(8,128)(2,1)S(1)}, bf16[128,1024]{1,0:T(8,128)(2,1)S(1)}, u32[]{:S(2)}, u32[]{:S(2)}) collective-permute-start(bf16[128,1024]{1,0:T(8,128)(2,1)S(1)} %all_gather.3), channel_id=1, source_target_pairs={{0,28},{4,0},{8,4},{12,8},{16,12},{20,16},{24,20},{28,24},{1,29},{... | collective-permute-start | bytes 786440 | tf_op jit(solution)/shard_map/ppermute | solution.py:167
  40.6 1.9 %collective-permute-start = (bf16[128,1024]{1,0:T(8,128)(2,1)S(1)}, bf16[128,1024]{1,0:T(8,128)(2,1)S(1)}, u32[]{:S(2)}, u32[]{:S(2)}) collective-permute-start(bf16[128,1024]{1,0:T(8,128)(2,1)S(1)} %all_gather.3), channel_id=1, source_target_pairs={{0,4},{4,8},{8,12},{12,16},{16,20},{20,24},{24,28},{28,0},{1,5},{5... | collective-permute-start | bytes 786440 | tf_op jit(solution)/shard_map/ppermute | solution.py:166
  42.5 0.7 slice.30
  43.2 0.8 fusion.73
  44.2 0.3 multiply_cosine_fusion
  45.0 1.5 fusion.21
  46.5 5.1 %collective-permute-start.3 = (bf16[128,1024]{1,0:T(8,128)(2,1)S(1)}, bf16[128,1024]{1,0:T(8,128)(2,1)S(1)}, u32[]{:S(2)}, u32[]{:S(2)}) collective-permute-start(bf16[128,1024]{1,0:T(8,128)(2,1)S(1)} %collective-permute-done.1), channel_id=1, source_target_pairs={{0,28},{4,0},{8,4},{12,8},{16,12},{20,16},{24,20},{28,24},{1,29},{... | collective-permute-start | bytes 786440 | tf_op jit(solution)/shard_map/ppermute | solution.py:167
  51.7 1.9 %collective-permute-start.2 = (bf16[128,1024]{1,0:T(8,128)(2,1)S(1)}, bf16[128,1024]{1,0:T(8,128)(2,1)S(1)}, u32[]{:S(2)}, u32[]{:S(2)}) collective-permute-start(bf16[128,1024]{1,0:T(8,128)(2,1)S(1)} %collective-permute-done), channel_id=1, source_target_pairs={{0,4},{4,8},{8,12},{12,16},{16,20},{20,24},{24,28},{28,0},{1,5},{5... | collective-permute-start | bytes 786440 | tf_op jit(solution)/shard_map/ppermute | solution.py:166
  53.6 1.4 convolution_add_fusion.3
  55.0 0.2 convolution_add_fusion.7
  55.2 0.2 convolution_add_fusion.6
  55.4 1.4 convolution_add_fusion.2
  56.8 5.1 %collective-permute-start.5 = (bf16[128,1024]{1,0:T(8,128)(2,1)S(1)}, bf16[128,1024]{1,0:T(8,128)(2,1)S(1)}, u32[]{:S(2)}, u32[]{:S(2)}) collective-permute-start(bf16[128,1024]{1,0:T(8,128)(2,1)S(1)} %collective-permute-done.3), channel_id=1, source_target_pairs={{0,28},{4,0},{8,4},{12,8},{16,12},{20,16},{24,20},{28,24},{1,29},{... | collective-permute-start | bytes 786440 | tf_op jit(solution)/shard_map/ppermute | solution.py:167
  61.9 0.2 fusion.29
  62.2 0.3 fusion.16
  62.5 1.9 %collective-permute-start.4 = (bf16[128,1024]{1,0:T(8,128)(2,1)S(1)}, bf16[128,1024]{1,0:T(8,128)(2,1)S(1)}, u32[]{:S(2)}, u32[]{:S(2)}) collective-permute-start(bf16[128,1024]{1,0:T(8,128)(2,1)S(1)} %collective-permute-done.2), channel_id=1, source_target_pairs={{0,4},{4,8},{8,12},{12,16},{16,20},{20,24},{24,28},{28,0},{1,5},{5... | collective-permute-start | bytes 786440 | tf_op jit(solution)/shard_map/ppermute | solution.py:166
  64.5 0.2 fusion.9
  64.7 0.3 fusion.2
  65.0 0.8 collective-permute-done.5
  65.8 5.6 %collective-permute-start.7 = (bf16[64,1024]{1,0:T(8,128)(2,1)S(1)}, bf16[64,1024]{1,0:T(8,128)(2,1)S(1)}, u32[]{:S(2)}, u32[]{:S(2)}) collective-permute-start(bf16[64,1024]{1,0:T(8,128)(2,1)S(1)} %slice.38), channel_id=1, source_target_pairs={{0,28},{4,0},{8,4},{12,8},{16,12},{20,16},{24,20},{28,24},{1,29},{... | collective-permute-start | bytes 393224 | tf_op jit(solution)/shard_map/ppermute | solution.py:172
  71.4 0.6 collective-permute-done.4
  72.0 1.9 %collective-permute-start.6 = (bf16[64,1024]{1,0:T(8,128)(2,1)S(1)}, bf16[64,1024]{1,0:T(8,128)(2,1)S(1)}, u32[]{:S(2)}, u32[]{:S(2)}) collective-permute-start(bf16[64,1024]{1,0:T(8,128)(2,1)S(1)} %slice.37), channel_id=1, source_target_pairs={{0,4},{4,8},{8,12},{12,16},{16,20},{20,24},{24,28},{28,0},{1,5},{5... | collective-permute-start | bytes 393224 | tf_op jit(solution)/shard_map/ppermute | solution.py:171
  73.9 0.3 fusion.13
  74.3 0.2 fusion.26
  74.5 5.6 %collective-permute-done.6 = bf16[64,1024]{1,0:T(8,128)(2,1)S(1)} collective-permute-done((bf16[64,1024]{1,0:T(8,128)(2,1)S(1)}, bf16[64,1024]{1,0:T(8,128)(2,1)S(1)}, u32[]{:S(2)}, u32[]{:S(2)}) %collective-permute-start.6) | collective-permute-done | bytes 131104 | tf_op jit(solution)/shard_map/ppermute | solution.py:171
  80.1 0.2 fusion.24
  80.3 0.4 fusion.11
  80.7 0.2 fusion.10
  80.9 2.9 %collective-permute-start.8 = (bf16[128,64]{0,1:T(8,128)(2,1)S(1)}, bf16[128,64]{0,1:T(8,128)(2,1)S(1)}, u32[]{:S(2)}, u32[]{:S(2)}) collective-permute-start(bf16[128,64]{0,1:T(8,128)(2,1)S(1)} %fusion.10), channel_id=1, source_target_pairs={{0,1},{1,0},{2,3},{3,2},{4,5},{5,4},{6,7},{7,6},{8,9},{9,8},{10,11... | collective-permute-start | bytes 49160 | tf_op jit(solution)/shard_map/ppermute | solution.py:74
  83.8 0.4 fusion.3
  84.4 3.1 %collective-permute-done.8 = bf16[128,64]{0,1:T(8,128)(2,1)S(1)} collective-permute-done((bf16[128,64]{0,1:T(8,128)(2,1)S(1)}, bf16[128,64]{0,1:T(8,128)(2,1)S(1)}, u32[]{:S(2)}, u32[]{:S(2)}) %collective-permute-start.8) | collective-permute-done | bytes 16416 | tf_op jit(solution)/shard_map/ppermute | solution.py:74
  87.5 0.7 collective-permute-start.10
  88.2 7.3 %collective-permute-start.9 = (bf16[128,128]{0,1:T(8,128)(2,1)S(1)}, bf16[128,128]{0,1:T(8,128)(2,1)S(1)}, u32[]{:S(2)}, u32[]{:S(2)}) collective-permute-start(bf16[128,128]{0,1:T(8,128)(2,1)S(1)} %pad_maximum_fusion.2), channel_id=1, source_target_pairs={{0,2},{1,3},{2,6},{3,7},{4,10},{5,11},{6,14},{7,15},{8,18},{9,19},... | collective-permute-start | bytes 98312 | tf_op jit(solution)/shard_map/ppermute | solution.py:87
  95.6 6.8 %collective-permute-done.9 = bf16[128,128]{0,1:T(8,128)(2,1)S(1)} collective-permute-done((bf16[128,128]{0,1:T(8,128)(2,1)S(1)}, bf16[128,128]{0,1:T(8,128)(2,1)S(1)}, u32[]{:S(2)}, u32[]{:S(2)}) %collective-permute-start.9) | collective-permute-done | bytes 32800 | tf_op jit(solution)/shard_map/ppermute | solution.py:87
  102.6 0.3 fusion.76
  103.2 2.2 %copy-done.1 = bf16[256,8192]{1,0:T(8,128)(2,1)S(1)} copy-done((bf16[256,8192]{1,0:T(8,128)(2,1)S(1)}, bf16[256,8192]{1,0:T(8,128)(2,1)}, u32[]{:S(2)}) %copy-start.1) | copy-done | bytes 4194328
  105.4 4.2 %shard_map.64 = (bf16[96,8192]{1,0:T(8,128)(2,1)}, bf16[32,32,256]{2,1,0:T(8,128)(2,1)S(1)}) custom-call(bf16[128,256]{1,0:T(8,128)(2,1)S(1)} %copy.17.attended_ref, bf16[256,8192]{1,0:T(8,128)(2,1)S(1)} %copy-done.1), custom_call_target="tpu_custom_call" | custom-call | tf_op jit(solution)/shard_map/pallas_call | solution.py:110
  109.6 23.9 %all_to_all.10 = bf16[32,32,256]{2,1,0:T(8,128)(2,1)S(1)} all-to-all(bf16[32,32,256]{2,1,0:T(8,128)(2,1)S(1)} %get-tuple-element.8), channel_id=1, replica_groups=mesh['x'=8,'yl'=2,'core'=2,'z'=8,'yh'=4] {'z','yh'}, dimensions={0} | all-to-all | bytes 1048576 | tf_op jit(solution)/shard_map/all_to_all | solution.py:184
  133.6 0.9 broadcast_in_dim.12
  134.5 8.4 %all-to-all-start.1 = ((bf16[32,32,256]{2,1,0:T(8,128)(2,1)}), bf16[32,32,256]{2,1,0:T(8,128)(2,1)S(1)}, u32[]{:S(2)}, u32[]{:S(2)}) async-start(bf16[32,32,256]{2,1,0:T(8,128)(2,1)} %broadcast_in_dim.12), calls=%async_computation.2 | async-start | bytes 1048576 | tf_op jit(solution)/shard_map/all_to_all | solution.py:191
  142.9 13.5 %reduce-scatter.2.cloned.1.call-done = bf16[1024,96]{0,1:T(8,128)(2,1)} async-done(((bf16[8192,96]{0,1:T(8,128)(2,1)}), bf16[1024,96]{0,1:T(8,128)(2,1)}) %reduce-scatter.2.cloned.1.call-update) | async-done | bytes 196624 | tf_op jit(solution)/shard_map/reduce_scatter | solution.py:183
  156.4 0.9 dynamic-slice_bitcast_fusion.3
  157.3 3.7 %collective-permute-start.11 = (bf16[96,512]{1,0:T(8,128)(2,1)S(1)}, bf16[96,512]{1,0:T(8,128)(2,1)S(1)}, u32[]{:S(2)}, u32[]{:S(2)}) collective-permute-start(bf16[96,512]{1,0:T(8,128)(2,1)S(1)} %pad_maximum_fusion), channel_id=1, source_target_pairs={{0,1},{1,0},{2,3},{3,2},{4,5},{5,4},{6,7},{7,6},{8,9},{9,8},{10,11... | collective-permute-start | bytes 294920 | tf_op jit(solution)/shard_map/ppermute | solution.py:139
  160.9 3.7 %collective-permute-done.11 = bf16[96,512]{1,0:T(8,128)(2,1)S(1)} collective-permute-done((bf16[96,512]{1,0:T(8,128)(2,1)S(1)}, bf16[96,512]{1,0:T(8,128)(2,1)S(1)}, u32[]{:S(2)}, u32[]{:S(2)}) %collective-permute-start.11) | collective-permute-done | bytes 98336 | tf_op jit(solution)/shard_map/ppermute | solution.py:139
  164.7 5.6 %collective-permute-start.12 = (bf16[96,256]{1,0:T(8,128)(2,1)S(1)}, bf16[96,256]{1,0:T(8,128)(2,1)S(1)}, u32[]{:S(2)}, u32[]{:S(2)}) collective-permute-start(bf16[96,256]{1,0:T(8,128)(2,1)S(1)} %slice.61), channel_id=1, source_target_pairs={{0,2},{1,3},{2,0},{3,1},{4,6},{5,7},{6,4},{7,5},{8,10},{9,11},{10,... | collective-permute-start | bytes 147464 | tf_op jit(solution)/shard_map/ppermute | solution.py:141
  170.5 4.2 %collective-permute-done.12 = bf16[96,256]{1,0:T(8,128)(2,1)S(1)} collective-permute-done((bf16[96,256]{1,0:T(8,128)(2,1)S(1)}, bf16[96,256]{1,0:T(8,128)(2,1)S(1)}, u32[]{:S(2)}, u32[]{:S(2)}) %collective-permute-start.12) | collective-permute-done | bytes 49184 | tf_op jit(solution)/shard_map/ppermute | solution.py:141
  174.7 0.6 pad_maximum_fusion.1
  (44 shorter events, 1.7 us)
Async XLA Ops:
  6.5 38.0 %copy-start = (bf16[8192,64]{0,1:T(8,128)(2,1)S(1)}, bf16[8192,64]{0,1:T(8,128)(2,1)}, u32[]{:S(2)}) copy-start(bf16[8192,64]{0,1:T(8,128)(2,1)} %param.8) | copy-start | bytes 3145732
  6.5 149.8 %reduce-scatter.2.cloned.1.call-start = ((), (), s32[]{:S(2)}) async-start(), calls=%async_computation.3 | async-start | bytes 1769472 | tf_op jit(solution)/shard_map/reduce_scatter | solution.py:183
  23.2 23.3 %collective-permute-start.1 = (bf16[128,1024]{1,0:T(8,128)(2,1)S(1)}, bf16[128,1024]{1,0:T(8,128)(2,1)S(1)}, u32[]{:S(2)}, u32[]{:S(2)}) collective-permute-start(bf16[128,1024]{1,0:T(8,128)(2,1)S(1)} %all_gather.3), channel_id=1, source_target_pairs={{0,28},{4,0},{8,4},{12,8},{16,12},{20,16},{24,20},{28,24},{1,29},{... | collective-permute-start | bytes 786440 | tf_op jit(solution)/shard_map/ppermute | solution.py:167
  40.6 11.1 %collective-permute-start = (bf16[128,1024]{1,0:T(8,128)(2,1)S(1)}, bf16[128,1024]{1,0:T(8,128)(2,1)S(1)}, u32[]{:S(2)}, u32[]{:S(2)}) collective-permute-start(bf16[128,1024]{1,0:T(8,128)(2,1)S(1)} %all_gather.3), channel_id=1, source_target_pairs={{0,4},{4,8},{8,12},{12,16},{16,20},{20,24},{24,28},{28,0},{1,5},{5... | collective-permute-start | bytes 786440 | tf_op jit(solution)/shard_map/ppermute | solution.py:166
  44.9 17.2 %copy-start.2 = (bf16[8192,256]{1,0:T(8,128)(2,1)S(1)}, bf16[8192,256]{1,0:T(8,128)(2,1)}, u32[]{:S(2)}) copy-start(bf16[8192,256]{1,0:T(8,128)(2,1)} %param.7) | copy-start | bytes 12582916
  46.5 10.3 %collective-permute-start.3 = (bf16[128,1024]{1,0:T(8,128)(2,1)S(1)}, bf16[128,1024]{1,0:T(8,128)(2,1)S(1)}, u32[]{:S(2)}, u32[]{:S(2)}) collective-permute-start(bf16[128,1024]{1,0:T(8,128)(2,1)S(1)} %collective-permute-done.1), channel_id=1, source_target_pairs={{0,28},{4,0},{8,4},{12,8},{16,12},{20,16},{24,20},{28,24},{1,29},{... | collective-permute-start | bytes 786440 | tf_op jit(solution)/shard_map/ppermute | solution.py:167
  51.7 10.9 %collective-permute-start.2 = (bf16[128,1024]{1,0:T(8,128)(2,1)S(1)}, bf16[128,1024]{1,0:T(8,128)(2,1)S(1)}, u32[]{:S(2)}, u32[]{:S(2)}) collective-permute-start(bf16[128,1024]{1,0:T(8,128)(2,1)S(1)} %collective-permute-done), channel_id=1, source_target_pairs={{0,4},{4,8},{8,12},{12,16},{16,20},{20,24},{24,28},{28,0},{1,5},{5... | collective-permute-start | bytes 786440 | tf_op jit(solution)/shard_map/ppermute | solution.py:166
  56.8 9.0 %collective-permute-start.5 = (bf16[128,1024]{1,0:T(8,128)(2,1)S(1)}, bf16[128,1024]{1,0:T(8,128)(2,1)S(1)}, u32[]{:S(2)}, u32[]{:S(2)}) collective-permute-start(bf16[128,1024]{1,0:T(8,128)(2,1)S(1)} %collective-permute-done.3), channel_id=1, source_target_pairs={{0,28},{4,0},{8,4},{12,8},{16,12},{20,16},{24,20},{28,24},{1,29},{... | collective-permute-start | bytes 786440 | tf_op jit(solution)/shard_map/ppermute | solution.py:167
  62.5 9.5 %collective-permute-start.4 = (bf16[128,1024]{1,0:T(8,128)(2,1)S(1)}, bf16[128,1024]{1,0:T(8,128)(2,1)S(1)}, u32[]{:S(2)}, u32[]{:S(2)}) collective-permute-start(bf16[128,1024]{1,0:T(8,128)(2,1)S(1)} %collective-permute-done.2), channel_id=1, source_target_pairs={{0,4},{4,8},{8,12},{12,16},{16,20},{20,24},{24,28},{28,0},{1,5},{5... | collective-permute-start | bytes 786440 | tf_op jit(solution)/shard_map/ppermute | solution.py:166
  65.8 14.3 %collective-permute-start.7 = (bf16[64,1024]{1,0:T(8,128)(2,1)S(1)}, bf16[64,1024]{1,0:T(8,128)(2,1)S(1)}, u32[]{:S(2)}, u32[]{:S(2)}) collective-permute-start(bf16[64,1024]{1,0:T(8,128)(2,1)S(1)} %slice.38), channel_id=1, source_target_pairs={{0,28},{4,0},{8,4},{12,8},{16,12},{20,16},{24,20},{28,24},{1,29},{... | collective-permute-start | bytes 393224 | tf_op jit(solution)/shard_map/ppermute | solution.py:172
  72.0 8.1 %collective-permute-start.6 = (bf16[64,1024]{1,0:T(8,128)(2,1)S(1)}, bf16[64,1024]{1,0:T(8,128)(2,1)S(1)}, u32[]{:S(2)}, u32[]{:S(2)}) collective-permute-start(bf16[64,1024]{1,0:T(8,128)(2,1)S(1)} %slice.37), channel_id=1, source_target_pairs={{0,4},{4,8},{8,12},{12,16},{16,20},{20,24},{24,28},{28,0},{1,5},{5... | collective-permute-start | bytes 393224 | tf_op jit(solution)/shard_map/ppermute | solution.py:171
  80.9 6.6 %collective-permute-start.8 = (bf16[128,64]{0,1:T(8,128)(2,1)S(1)}, bf16[128,64]{0,1:T(8,128)(2,1)S(1)}, u32[]{:S(2)}, u32[]{:S(2)}) collective-permute-start(bf16[128,64]{0,1:T(8,128)(2,1)S(1)} %fusion.10), channel_id=1, source_target_pairs={{0,1},{1,0},{2,3},{3,2},{4,5},{5,4},{6,7},{7,6},{8,9},{9,8},{10,11... | collective-permute-start | bytes 49160 | tf_op jit(solution)/shard_map/ppermute | solution.py:74
  87.5 8.1 %collective-permute-start.10 = (bf16[128,128]{0,1:T(8,128)(2,1)S(1)}, bf16[128,128]{0,1:T(8,128)(2,1)S(1)}, u32[]{:S(2)}, u32[]{:S(2)}) collective-permute-start(bf16[128,128]{0,1:T(8,128)(2,1)S(1)} %pad_maximum_fusion.2), channel_id=1, source_target_pairs={{0,0},{1,1},{2,4},{3,5},{4,8},{5,9},{6,12},{7,13},{8,16},{9,17},{1... | collective-permute-start | bytes 98312 | tf_op jit(solution)/shard_map/ppermute | solution.py:86
  88.2 14.2 %collective-permute-start.9 = (bf16[128,128]{0,1:T(8,128)(2,1)S(1)}, bf16[128,128]{0,1:T(8,128)(2,1)S(1)}, u32[]{:S(2)}, u32[]{:S(2)}) collective-permute-start(bf16[128,128]{0,1:T(8,128)(2,1)S(1)} %pad_maximum_fusion.2), channel_id=1, source_target_pairs={{0,2},{1,3},{2,6},{3,7},{4,10},{5,11},{6,14},{7,15},{8,18},{9,19},... | collective-permute-start | bytes 98312 | tf_op jit(solution)/shard_map/ppermute | solution.py:87
  103.2 2.2 %copy-start.1 = (bf16[256,8192]{1,0:T(8,128)(2,1)S(1)}, bf16[256,8192]{1,0:T(8,128)(2,1)}, u32[]{:S(2)}) copy-start(bf16[256,8192]{1,0:T(8,128)(2,1)} %w_ref.1) | copy-start | bytes 12582916
  105.4 55.5 %copy-start.3 = (s32[1024]{0:T(1024)S(1)}, s32[1024]{0:T(1024)}, u32[]{:S(2)}) copy-start(s32[1024]{0:T(1024)} %param.10) | copy-start | bytes 12292
  134.5 35.9 %all-to-all-start.1 = ((bf16[32,32,256]{2,1,0:T(8,128)(2,1)}), bf16[32,32,256]{2,1,0:T(8,128)(2,1)S(1)}, u32[]{:S(2)}, u32[]{:S(2)}) async-start(bf16[32,32,256]{2,1,0:T(8,128)(2,1)} %broadcast_in_dim.12), calls=%async_computation.2 | async-start | bytes 1048576 | tf_op jit(solution)/shard_map/all_to_all | solution.py:191
  157.3 7.4 %collective-permute-start.11 = (bf16[96,512]{1,0:T(8,128)(2,1)S(1)}, bf16[96,512]{1,0:T(8,128)(2,1)S(1)}, u32[]{:S(2)}, u32[]{:S(2)}) collective-permute-start(bf16[96,512]{1,0:T(8,128)(2,1)S(1)} %pad_maximum_fusion), channel_id=1, source_target_pairs={{0,1},{1,0},{2,3},{3,2},{4,5},{5,4},{6,7},{7,6},{8,9},{9,8},{10,11... | collective-permute-start | bytes 294920 | tf_op jit(solution)/shard_map/ppermute | solution.py:139
  164.7 10.0 %collective-permute-start.12 = (bf16[96,256]{1,0:T(8,128)(2,1)S(1)}, bf16[96,256]{1,0:T(8,128)(2,1)S(1)}, u32[]{:S(2)}, u32[]{:S(2)}) collective-permute-start(bf16[96,256]{1,0:T(8,128)(2,1)S(1)} %slice.61), channel_id=1, source_target_pairs={{0,2},{1,3},{2,0},{3,1},{4,6},{5,7},{6,4},{7,5},{8,10},{9,11},{10,... | collective-permute-start | bytes 147464 | tf_op jit(solution)/shard_map/ppermute | solution.py:141
Sparse Core Ops, SparseCore 0:
  109.7 46.6 reduce-scatter.1

commit v5 on v4

--- a/solution.py
+++ b/solution.py
@@ -1,3 +1,4 @@
+import functools
 import math
 
 import jax
@@ -18,6 +19,7 @@
 
 N_Z = 8
 N_Y = 4
+DISTANCES = (0, -1, 1, -2, 2, -3, 3)
 DP = ("x", "yl", "core")
 TENSOR = ("z", "yh")
 
@@ -123,7 +125,7 @@
             jax.ShapeDtypeStruct((n, MOVE, wide // n), jnp.bfloat16),
         ],
         compiler_params=pltpu.CompilerParams(vmem_limit_bytes=16 * 1024 * 1024),
-    )(attended, w_out)
+    )(attended, pltpu.with_memory_space_constraint(w_out, pltpu.HBM))
 
 
 def sum_over_y(rows):
@@ -144,6 +146,45 @@
     return (held[:, :width] + got.astype(jnp.float32)).astype(jnp.bfloat16)
 
 
+def product_kernel(transposed, z_ref, *refs):
+    *piece_refs, w_ref, out_ref = refs
+    depth = piece_refs[0].shape[1]
+
+    def times(piece, k):
+        at = pl.multiple_of(lax.rem(z_ref[0] + k + N_Z, N_Z) * depth, depth)
+        if transposed:
+            w = w_ref[:, pl.ds(at, depth)]
+        else:
+            w = w_ref[pl.ds(at, depth), :]
+        return lax.dot_general(
+            piece[...],
+            w,
+            (((1,), (1 if transposed else 0,)), ((), ())),
+            preferred_element_type=jnp.float32,
+        )
+
+    total = jnp.concatenate(
+        [times(piece_refs[-2], N_Z // 2), times(piece_refs[-1], N_Z // 2)], axis=0
+    )
+    for piece, k in zip(piece_refs[:-2], DISTANCES, strict=True):
+        total = total + times(piece, k)
+    out_ref[...] = total.astype(out_ref.dtype)
+
+
+def product(pieces, weight, transposed, dtype):
+    rows = pieces[0].shape[0]
+    columns = weight.shape[0] if transposed else weight.shape[1]
+    z_me = lax.axis_index("z").reshape(1)
+    return pl.pallas_call(
+        functools.partial(product_kernel, transposed),
+        in_specs=[pl.BlockSpec(memory_space=pltpu.SMEM)]
+        + [pl.BlockSpec(memory_space=pltpu.VMEM)] * (len(pieces) + 1),
+        out_specs=pl.BlockSpec(memory_space=pltpu.VMEM),
+        out_shape=jax.ShapeDtypeStruct((rows, columns), dtype),
+        compiler_params=pltpu.CompilerParams(vmem_limit_bytes=24 * 1024 * 1024),
+    )(z_me, *pieces, weight)
+
+
 def shards(activations, w_query, w_keyval, w_out, targets, segments):
     block = lax.axis_index(DP)
     tail_docs = lax.dynamic_slice_in_dim(targets, block * MOVE, MOVE) // RECV
@@ -151,29 +192,19 @@
     positions, visible = doc_layout(labels)
     cosine, sine = rotation_tables(positions)
 
-    z_me = lax.axis_index("z")
     own = lax.all_gather(activations, "yh", axis=1, tiled=True)
-    depth = own.shape[1]
-
-    def times(weight, chunk, k):
-        rows = lax.dynamic_slice_in_dim(weight, ((z_me + k) % N_Z) * depth, depth, 0)
-        return jnp.dot(chunk, rows, preferred_element_type=jnp.float32)
-
-    query = times(w_query, own, 0)
-    keyval = times(w_keyval, own, 0)
+    pieces = [own]
     up, down = own, own
-    for step in range(1, N_Z // 2):
+    for _ in range(1, N_Z // 2):
         up = lax.ppermute(up, "z", ring(N_Z, 1))
         down = lax.ppermute(down, "z", ring(N_Z, -1))
-        query = query + times(w_query, up, -step) + times(w_query, down, step)
-        keyval = keyval + times(w_keyval, up, -step) + times(w_keyval, down, step)
+        pieces += [up, down]
     half = SEQ // 2
-    up = lax.ppermute(up[:half], "z", ring(N_Z, 1))
-    down = lax.ppermute(down[half:], "z", ring(N_Z, -1))
-    last = jnp.concatenate([up, down], axis=0)
-    keyval = (keyval + times(w_keyval, last, N_Z // 2)).astype(jnp.bfloat16)
+    pieces.append(lax.ppermute(up[:half], "z", ring(N_Z, 1)))
+    pieces.append(lax.ppermute(down[half:], "z", ring(N_Z, -1)))
+    keyval = product(pieces, w_keyval.T, True, jnp.bfloat16)
     key, value = move_keyval(keyval)
-    query = query + times(w_query, last, N_Z // 2)
+    query = product(pieces, w_query, False, jnp.float32)
 
     query_rot = rotate(query.reshape(SEQ, 2, HD), cosine, sine).astype(jnp.bfloat16)
     key_rot = rotate(key.astype(jnp.float32), cosine, sine).astype(jnp.bfloat16)

time: 183 us -> 180 us (0.984)
  the two profiles are of different devices: /device:TPU:16 before, /device:TPU:4 now
where the time goes in v5:
time: 180 us; the launch traced here: 179 us
  starting transfers between devices  66.3 us (37%)
  waiting for transfers between devices  41.5 us (23%)
  blocking collectives  39.9 us (22%)
  between operations  13.8 us (8%)
  Pallas kernels  8.25 us (5%)
  local copies, waits for them, and re-layouts  6.25 us (3%)
  other arithmetic  2.65 us (1%)
    ppermute x3, starting transfers between devices, shards(): down = lax.ppermute(down, 'z', ring(N_Z, -1))  24.3 us
    all_to_all x1, blocking collectives, shards(): moving = sum_pieces(lax.all_to_all(moving, TENSOR, 0, 0, tiled=True))  22.3 us
    all_gather x1, blocking collectives, shards(): own = lax.all_gather(activations, 'yh', axis=1, tiled=True)  17.6 us
    reduce_scatter x1, waiting for transfers between devices, shards(): kept = lax.psum_scatter(kept.T, 'z', scatter_dimension=0, tiled=True)  15.1 us
    ppermute x3, starting transfers between devices, shards(): up = lax.ppermute(up, 'z', ring(N_Z, 1))  9 us
    all_to_all x1, starting transfers between devices, shards(): lax.all_to_all(tails, DP, 0, 0, tiled=True).reshape(targets.shape[0], -1)  7.8 us
    ppermute x1, starting transfers between devices, move_keyval(): crossed = lax.ppermute(whole, TENSOR, routes(1))  7.08 us
    ppermute x1, waiting for transfers between devices, move_keyval(): crossed = lax.ppermute(whole, TENSOR, routes(1))  6.82 us
  transfers between devices with their start and end apart: 15, of which 10 were waited for; matrix products, arithmetic and copies ran while one was open for 2% of the time, Pallas kernels for 0%

profile of v5, /device:TPU:4, one launch (start us, length us, event | category | flops | bytes accessed | tf_op | source)
XLA Modules:
  0.0 179.2 jit_solution(383377089472507637)
XLA Ops:
  6.5 17.6 %all_gather.3.refs_0_ = bf16[128,1024]{1,0:T(8,128)(2,1)S(1)} all-gather(bf16[128,256]{1,0:T(8,128)(2,1)} %param.6), channel_id=1, replica_groups=mesh['x'=8,'yl'=2,'core'=2,'z'=8,'yh'=4] {'yh'}, dimensions={1}, use_global_device_ids=true | all-gather | bytes 327680 | tf_op jit(solution)/shard_map/all_gather | solution.py:195
  24.1 5.2 %collective-permute-start = (bf16[128,1024]{1,0:T(8,128)(2,1)S(1)}, bf16[128,1024]{1,0:T(8,128)(2,1)S(1)}, u32[]{:S(2)}, u32[]{:S(2)}) collective-permute-start(bf16[128,1024]{1,0:T(8,128)(2,1)S(1)} %all_gather.3.refs_0_), channel_id=1, source_target_pairs={{0,4},{4,8},{8,12},{12,16},{16,20},{20,24},{24,28},{28,0},{1,5},{5... | collective-permute-start | bytes 786440 | tf_op jit(solution)/shard_map/ppermute | solution.py:199
  29.3 14.0 %collective-permute-start.1 = (bf16[128,1024]{1,0:T(8,128)(2,1)S(1)}, bf16[128,1024]{1,0:T(8,128)(2,1)S(1)}, u32[]{:S(2)}, u32[]{:S(2)}) collective-permute-start(bf16[128,1024]{1,0:T(8,128)(2,1)S(1)} %all_gather.3.refs_0_), channel_id=1, source_target_pairs={{0,28},{4,0},{8,4},{12,8},{16,12},{20,16},{24,20},{28,24},{1,29},{... | collective-permute-start | bytes 786440 | tf_op jit(solution)/shard_map/ppermute | solution.py:200
  43.4 2.4 %collective-permute-done.refs_1_ = bf16[128,1024]{1,0:T(8,128)(2,1)S(1)} collective-permute-done((bf16[128,1024]{1,0:T(8,128)(2,1)S(1)}, bf16[128,1024]{1,0:T(8,128)(2,1)S(1)}, u32[]{:S(2)}, u32[]{:S(2)}) %collective-permute-start) | collective-permute-done | bytes 262176 | tf_op jit(solution)/shard_map/ppermute | solution.py:199
  45.8 1.9 %collective-permute-start.2 = (bf16[128,1024]{1,0:T(8,128)(2,1)S(1)}, bf16[128,1024]{1,0:T(8,128)(2,1)S(1)}, u32[]{:S(2)}, u32[]{:S(2)}) collective-permute-start(bf16[128,1024]{1,0:T(8,128)(2,1)S(1)} %collective-permute-done.refs_1_), channel_id=1, source_target_pairs={{0,4},{4,8},{8,12},{12,16},{16,20},{20,24},{24,28},{28,0},{1,5},{5... | collective-permute-start | bytes 786440 | tf_op jit(solution)/shard_map/ppermute | solution.py:199
  47.7 5.1 %collective-permute-start.3 = (bf16[128,1024]{1,0:T(8,128)(2,1)S(1)}, bf16[128,1024]{1,0:T(8,128)(2,1)S(1)}, u32[]{:S(2)}, u32[]{:S(2)}) collective-permute-start(bf16[128,1024]{1,0:T(8,128)(2,1)S(1)} %collective-permute-done.1.refs_2_), channel_id=1, source_target_pairs={{0,28},{4,0},{8,4},{12,8},{16,12},{20,16},{24,20},{28,24},{1,29},{... | collective-permute-start | bytes 786440 | tf_op jit(solution)/shard_map/ppermute | solution.py:200
  52.8 0.8 fusion.24
  53.6 0.7 slice.30
  54.3 0.1 pad_add_fusion
  54.3 0.1 convert_reduce_fusion
  54.4 0.8 collective-permute-done.2.refs_3_
  55.2 1.9 %collective-permute-start.4 = (bf16[128,1024]{1,0:T(8,128)(2,1)S(1)}, bf16[128,1024]{1,0:T(8,128)(2,1)S(1)}, u32[]{:S(2)}, u32[]{:S(2)}) collective-permute-start(bf16[128,1024]{1,0:T(8,128)(2,1)S(1)} %collective-permute-done.2.refs_3_), channel_id=1, source_target_pairs={{0,4},{4,8},{8,12},{12,16},{16,20},{20,24},{24,28},{28,0},{1,5},{5... | collective-permute-start | bytes 786440 | tf_op jit(solution)/shard_map/ppermute | solution.py:199
  57.1 5.1 %collective-permute-start.5 = (bf16[128,1024]{1,0:T(8,128)(2,1)S(1)}, bf16[128,1024]{1,0:T(8,128)(2,1)S(1)}, u32[]{:S(2)}, u32[]{:S(2)}) collective-permute-start(bf16[128,1024]{1,0:T(8,128)(2,1)S(1)} %collective-permute-done.3.refs_4_), channel_id=1, source_target_pairs={{0,28},{4,0},{8,4},{12,8},{16,12},{20,16},{24,20},{28,24},{1,29},{... | collective-permute-start | bytes 786440 | tf_op jit(solution)/shard_map/ppermute | solution.py:200
  62.3 0.3 multiply_cosine_fusion
  62.6 2.4 %collective-permute-done.4.refs_5_ = bf16[128,1024]{1,0:T(8,128)(2,1)S(1)} collective-permute-done((bf16[128,1024]{1,0:T(8,128)(2,1)S(1)}, bf16[128,1024]{1,0:T(8,128)(2,1)S(1)}, u32[]{:S(2)}, u32[]{:S(2)}) %collective-permute-start.4) | collective-permute-done | bytes 262176 | tf_op jit(solution)/shard_map/ppermute | solution.py:199
  65.0 1.9 %collective-permute-start.6 = (bf16[64,1024]{1,0:T(8,128)(2,1)S(1)}, bf16[64,1024]{1,0:T(8,128)(2,1)S(1)}, u32[]{:S(2)}, u32[]{:S(2)}) collective-permute-start(bf16[64,1024]{1,0:T(8,128)(2,1)S(1)} %slice.37), channel_id=1, source_target_pairs={{0,4},{4,8},{8,12},{12,16},{16,20},{20,24},{24,28},{28,0},{1,5},{5... | collective-permute-start | bytes 393224 | tf_op jit(solution)/shard_map/ppermute | solution.py:203
  67.0 5.4 %collective-permute-start.7 = (bf16[64,1024]{1,0:T(8,128)(2,1)S(1)}, bf16[64,1024]{1,0:T(8,128)(2,1)S(1)}, u32[]{:S(2)}, u32[]{:S(2)}) collective-permute-start(bf16[64,1024]{1,0:T(8,128)(2,1)S(1)} %slice.38), channel_id=1, source_target_pairs={{0,28},{4,0},{8,4},{12,8},{16,12},{20,16},{24,20},{28,24},{1,29},{... | collective-permute-start | bytes 393224 | tf_op jit(solution)/shard_map/ppermute | solution.py:204
  72.3 0.1 compare_and_fusion.1
  72.4 0.6 collective-permute-done.6.refs_7_
  73.1 1.8 collective-permute-done.7.refs_8_
  74.8 1.2 copy-done.1
  76.1 0.7 shard_map.64
  76.8 1.9 %collective-permute-start.8 = (bf16[128,64]{1,0:T(8,128)(2,1)S(1)}, bf16[128,64]{1,0:T(8,128)(2,1)S(1)}, u32[]{:S(2)}, u32[]{:S(2)}) collective-permute-start(bf16[128,64]{1,0:T(8,128)(2,1)S(1)} %shard_map.64), channel_id=1, source_target_pairs={{0,1},{1,0},{2,3},{3,2},{4,5},{5,4},{6,7},{7,6},{8,9},{9,8},{10,11... | collective-permute-start | bytes 49160 | tf_op jit(solution)/shard_map/ppermute | solution.py:76
  78.7 2.2 %copy-done = bf16[8192,256]{1,0:T(8,128)(2,1)S(1)} copy-done((bf16[8192,256]{1,0:T(8,128)(2,1)S(1)}, bf16[8192,256]{1,0:T(8,128)(2,1)}, u32[]{:S(2)}) %copy-start) | copy-done | bytes 4194328
  80.9 0.8 shard_map.65
  81.8 0.2 fusion.26
  82.0 1.6 collective-permute-done.8
  83.7 0.1 pad_maximum_fusion.2
  83.8 0.7 collective-permute-start.10
  84.4 7.1 %collective-permute-start.9 = (bf16[128,128]{1,0:T(8,128)(2,1)S(1)}, bf16[128,128]{1,0:T(8,128)(2,1)S(1)}, u32[]{:S(2)}, u32[]{:S(2)}) collective-permute-start(bf16[128,128]{1,0:T(8,128)(2,1)S(1)} %pad_maximum_fusion.2), channel_id=1, source_target_pairs={{0,2},{1,3},{2,6},{3,7},{4,10},{5,11},{6,14},{7,15},{8,18},{9,19},... | collective-permute-start | bytes 98312 | tf_op jit(solution)/shard_map/ppermute | solution.py:89
  91.6 6.8 %collective-permute-done.9 = bf16[128,128]{1,0:T(8,128)(2,1)S(1)} collective-permute-done((bf16[128,128]{1,0:T(8,128)(2,1)S(1)}, bf16[128,128]{1,0:T(8,128)(2,1)S(1)}, u32[]{:S(2)}, u32[]{:S(2)}) %collective-permute-start.9) | collective-permute-done | bytes 32800 | tf_op jit(solution)/shard_map/ppermute | solution.py:89
  98.4 0.3 fusion.22
  98.7 0.3 fusion.27
  99.1 0.2 convolution_convert_fusion
  99.3 0.1 copy.15.attended_ref
  99.4 6.7 %shard_map.66 = (bf16[96,8192]{1,0:T(8,128)(2,1)}, bf16[32,32,256]{2,1,0:T(8,128)(2,1)S(1)}) custom-call(bf16[128,256]{1,0:T(8,128)(2,1)S(1)} %copy.15.attended_ref, bf16[256,8192]{1,0:T(8,128)(2,1)} %w_ref.1), custom_call_target="tpu_custom_call" | custom-call | tf_op jit(solution)/shard_map/pallas_call | solution.py:112
  106.2 22.3 %all_to_all.10 = bf16[32,32,256]{2,1,0:T(8,128)(2,1)S(1)} all-to-all(bf16[32,32,256]{2,1,0:T(8,128)(2,1)S(1)} %get-tuple-element.8), channel_id=1, replica_groups=mesh['x'=8,'yl'=2,'core'=2,'z'=8,'yh'=4] {'z','yh'}, dimensions={0} | all-to-all | bytes 1048576 | tf_op jit(solution)/shard_map/all_to_all | solution.py:215
  128.5 0.1 reduce_sum.32
  128.6 0.9 broadcast_in_dim.12
  129.5 7.8 %all-to-all-start.1 = ((bf16[32,32,256]{2,1,0:T(8,128)(2,1)}), bf16[32,32,256]{2,1,0:T(8,128)(2,1)S(1)}, u32[]{:S(2)}, u32[]{:S(2)}) async-start(bf16[32,32,256]{2,1,0:T(8,128)(2,1)} %broadcast_in_dim.12), calls=%async_computation.2 | async-start | bytes 1048576 | tf_op jit(solution)/shard_map/all_to_all | solution.py:222
  137.3 15.1 %reduce-scatter.2.cloned.1.call-done = bf16[1024,96]{0,1:T(8,128)(2,1)} async-done(((bf16[8192,96]{0,1:T(8,128)(2,1)}), bf16[1024,96]{0,1:T(8,128)(2,1)}) %reduce-scatter.2.cloned.1.call-update) | async-done | bytes 196624 | tf_op jit(solution)/shard_map/reduce_scatter | solution.py:214
  152.4 0.9 dynamic-slice_bitcast_fusion.3
  153.3 2.7 %collective-permute-start.11 = (bf16[96,512]{1,0:T(8,128)(2,1)S(1)}, bf16[96,512]{1,0:T(8,128)(2,1)S(1)}, u32[]{:S(2)}, u32[]{:S(2)}) collective-permute-start(bf16[96,512]{1,0:T(8,128)(2,1)S(1)} %pad_maximum_fusion), channel_id=1, source_target_pairs={{0,1},{1,0},{2,3},{3,2},{4,5},{5,4},{6,7},{7,6},{8,9},{9,8},{10,11... | collective-permute-start | bytes 294920 | tf_op jit(solution)/shard_map/ppermute | solution.py:141
  156.1 5.7 %collective-permute-done.11 = bf16[96,512]{1,0:T(8,128)(2,1)S(1)} collective-permute-done((bf16[96,512]{1,0:T(8,128)(2,1)S(1)}, bf16[96,512]{1,0:T(8,128)(2,1)S(1)}, u32[]{:S(2)}, u32[]{:S(2)}) %collective-permute-start.11) | collective-permute-done | bytes 98336 | tf_op jit(solution)/shard_map/ppermute | solution.py:141
  161.8 5.5 %collective-permute-start.12 = (bf16[96,256]{1,0:T(8,128)(2,1)S(1)}, bf16[96,256]{1,0:T(8,128)(2,1)S(1)}, u32[]{:S(2)}, u32[]{:S(2)}) collective-permute-start(bf16[96,256]{1,0:T(8,128)(2,1)S(1)} %slice.61), channel_id=1, source_target_pairs={{0,2},{1,3},{2,0},{3,1},{4,6},{5,7},{6,4},{7,5},{8,10},{9,11},{10,... | collective-permute-start | bytes 147464 | tf_op jit(solution)/shard_map/ppermute | solution.py:143
  167.3 0.2 convolution_convert_fusion.1
  167.5 4.2 %collective-permute-done.12 = bf16[96,256]{1,0:T(8,128)(2,1)S(1)} collective-permute-done((bf16[96,256]{1,0:T(8,128)(2,1)S(1)}, bf16[96,256]{1,0:T(8,128)(2,1)S(1)}, u32[]{:S(2)}, u32[]{:S(2)}) %collective-permute-start.12) | collective-permute-done | bytes 49184 | tf_op jit(solution)/shard_map/ppermute | solution.py:143
  171.7 0.6 pad_maximum_fusion.1
  (25 shorter events, 0.3 us)
Async XLA Ops:
  6.5 145.9 %reduce-scatter.2.cloned.1.call-start = ((), (), s32[]{:S(2)}) async-start(), calls=%async_computation.3 | async-start | bytes 1769472 | tf_op jit(solution)/shard_map/reduce_scatter | solution.py:214
  24.1 21.7 %collective-permute-start = (bf16[128,1024]{1,0:T(8,128)(2,1)S(1)}, bf16[128,1024]{1,0:T(8,128)(2,1)S(1)}, u32[]{:S(2)}, u32[]{:S(2)}) collective-permute-start(bf16[128,1024]{1,0:T(8,128)(2,1)S(1)} %all_gather.3.refs_0_), channel_id=1, source_target_pairs={{0,4},{4,8},{8,12},{12,16},{16,20},{20,24},{24,28},{28,0},{1,5},{5... | collective-permute-start | bytes 786440 | tf_op jit(solution)/shard_map/ppermute | solution.py:199
  29.3 18.4 %collective-permute-start.1 = (bf16[128,1024]{1,0:T(8,128)(2,1)S(1)}, bf16[128,1024]{1,0:T(8,128)(2,1)S(1)}, u32[]{:S(2)}, u32[]{:S(2)}) collective-permute-start(bf16[128,1024]{1,0:T(8,128)(2,1)S(1)} %all_gather.3.refs_0_), channel_id=1, source_target_pairs={{0,28},{4,0},{8,4},{12,8},{16,12},{20,16},{24,20},{28,24},{1,29},{... | collective-permute-start | bytes 786440 | tf_op jit(solution)/shard_map/ppermute | solution.py:200
  45.8 9.5 %collective-permute-start.2 = (bf16[128,1024]{1,0:T(8,128)(2,1)S(1)}, bf16[128,1024]{1,0:T(8,128)(2,1)S(1)}, u32[]{:S(2)}, u32[]{:S(2)}) collective-permute-start(bf16[128,1024]{1,0:T(8,128)(2,1)S(1)} %collective-permute-done.refs_1_), channel_id=1, source_target_pairs={{0,4},{4,8},{8,12},{12,16},{16,20},{20,24},{24,28},{28,0},{1,5},{5... | collective-permute-start | bytes 786440 | tf_op jit(solution)/shard_map/ppermute | solution.py:199
  47.7 9.5 %collective-permute-start.3 = (bf16[128,1024]{1,0:T(8,128)(2,1)S(1)}, bf16[128,1024]{1,0:T(8,128)(2,1)S(1)}, u32[]{:S(2)}, u32[]{:S(2)}) collective-permute-start(bf16[128,1024]{1,0:T(8,128)(2,1)S(1)} %collective-permute-done.1.refs_2_), channel_id=1, source_target_pairs={{0,28},{4,0},{8,4},{12,8},{16,12},{20,16},{24,20},{28,24},{1,29},{... | collective-permute-start | bytes 786440 | tf_op jit(solution)/shard_map/ppermute | solution.py:200
  55.2 9.8 %collective-permute-start.4 = (bf16[128,1024]{1,0:T(8,128)(2,1)S(1)}, bf16[128,1024]{1,0:T(8,128)(2,1)S(1)}, u32[]{:S(2)}, u32[]{:S(2)}) collective-permute-start(bf16[128,1024]{1,0:T(8,128)(2,1)S(1)} %collective-permute-done.2.refs_3_), channel_id=1, source_target_pairs={{0,4},{4,8},{8,12},{12,16},{16,20},{20,24},{24,28},{28,0},{1,5},{5... | collective-permute-start | bytes 786440 | tf_op jit(solution)/shard_map/ppermute | solution.py:199
  57.1 9.8 %collective-permute-start.5 = (bf16[128,1024]{1,0:T(8,128)(2,1)S(1)}, bf16[128,1024]{1,0:T(8,128)(2,1)S(1)}, u32[]{:S(2)}, u32[]{:S(2)}) collective-permute-start(bf16[128,1024]{1,0:T(8,128)(2,1)S(1)} %collective-permute-done.3.refs_4_), channel_id=1, source_target_pairs={{0,28},{4,0},{8,4},{12,8},{16,12},{20,16},{24,20},{28,24},{1,29},{... | collective-permute-start | bytes 786440 | tf_op jit(solution)/shard_map/ppermute | solution.py:200
  65.0 8.1 %collective-permute-start.6 = (bf16[64,1024]{1,0:T(8,128)(2,1)S(1)}, bf16[64,1024]{1,0:T(8,128)(2,1)S(1)}, u32[]{:S(2)}, u32[]{:S(2)}) collective-permute-start(bf16[64,1024]{1,0:T(8,128)(2,1)S(1)} %slice.37), channel_id=1, source_target_pairs={{0,4},{4,8},{8,12},{12,16},{16,20},{20,24},{24,28},{28,0},{1,5},{5... | collective-permute-start | bytes 393224 | tf_op jit(solution)/shard_map/ppermute | solution.py:203
  67.0 7.9 %collective-permute-start.7 = (bf16[64,1024]{1,0:T(8,128)(2,1)S(1)}, bf16[64,1024]{1,0:T(8,128)(2,1)S(1)}, u32[]{:S(2)}, u32[]{:S(2)}) collective-permute-start(bf16[64,1024]{1,0:T(8,128)(2,1)S(1)} %slice.38), channel_id=1, source_target_pairs={{0,28},{4,0},{8,4},{12,8},{16,12},{20,16},{24,20},{28,24},{1,29},{... | collective-permute-start | bytes 393224 | tf_op jit(solution)/shard_map/ppermute | solution.py:204
  74.8 1.2 copy-start.1
  76.8 6.9 %collective-permute-start.8 = (bf16[128,64]{1,0:T(8,128)(2,1)S(1)}, bf16[128,64]{1,0:T(8,128)(2,1)S(1)}, u32[]{:S(2)}, u32[]{:S(2)}) collective-permute-start(bf16[128,64]{1,0:T(8,128)(2,1)S(1)} %shard_map.64), channel_id=1, source_target_pairs={{0,1},{1,0},{2,3},{3,2},{4,5},{5,4},{6,7},{7,6},{8,9},{9,8},{10,11... | collective-permute-start | bytes 49160 | tf_op jit(solution)/shard_map/ppermute | solution.py:76
  78.7 2.2 %copy-start = (bf16[8192,256]{1,0:T(8,128)(2,1)S(1)}, bf16[8192,256]{1,0:T(8,128)(2,1)}, u32[]{:S(2)}) copy-start(bf16[8192,256]{1,0:T(8,128)(2,1)} %refs_9_.1) | copy-start | bytes 12582916
  83.8 7.8 %collective-permute-start.10 = (bf16[128,128]{1,0:T(8,128)(2,1)S(1)}, bf16[128,128]{1,0:T(8,128)(2,1)S(1)}, u32[]{:S(2)}, u32[]{:S(2)}) collective-permute-start(bf16[128,128]{1,0:T(8,128)(2,1)S(1)} %pad_maximum_fusion.2), channel_id=1, source_target_pairs={{0,0},{1,1},{2,4},{3,5},{4,8},{5,9},{6,12},{7,13},{8,16},{9,17},{1... | collective-permute-start | bytes 98312 | tf_op jit(solution)/shard_map/ppermute | solution.py:88
  84.4 14.0 %collective-permute-start.9 = (bf16[128,128]{1,0:T(8,128)(2,1)S(1)}, bf16[128,128]{1,0:T(8,128)(2,1)S(1)}, u32[]{:S(2)}, u32[]{:S(2)}) collective-permute-start(bf16[128,128]{1,0:T(8,128)(2,1)S(1)} %pad_maximum_fusion.2), channel_id=1, source_target_pairs={{0,2},{1,3},{2,6},{3,7},{4,10},{5,11},{6,14},{7,15},{8,18},{9,19},... | collective-permute-start | bytes 98312 | tf_op jit(solution)/shard_map/ppermute | solution.py:89
  99.4 56.7 %copy-start.2 = (s32[1024]{0:T(1024)S(1)}, s32[1024]{0:T(1024)}, u32[]{:S(2)}) copy-start(s32[1024]{0:T(1024)} %param.10) | copy-start | bytes 12292
  129.5 37.8 %all-to-all-start.1 = ((bf16[32,32,256]{2,1,0:T(8,128)(2,1)}), bf16[32,32,256]{2,1,0:T(8,128)(2,1)S(1)}, u32[]{:S(2)}, u32[]{:S(2)}) async-start(bf16[32,32,256]{2,1,0:T(8,128)(2,1)} %broadcast_in_dim.12), calls=%async_computation.2 | async-start | bytes 1048576 | tf_op jit(solution)/shard_map/all_to_all | solution.py:222
  153.3 8.5 %collective-permute-start.11 = (bf16[96,512]{1,0:T(8,128)(2,1)S(1)}, bf16[96,512]{1,0:T(8,128)(2,1)S(1)}, u32[]{:S(2)}, u32[]{:S(2)}) collective-permute-start(bf16[96,512]{1,0:T(8,128)(2,1)S(1)} %pad_maximum_fusion), channel_id=1, source_target_pairs={{0,1},{1,0},{2,3},{3,2},{4,5},{5,4},{6,7},{7,6},{8,9},{9,8},{10,11... | collective-permute-start | bytes 294920 | tf_op jit(solution)/shard_map/ppermute | solution.py:141
  161.8 9.9 %collective-permute-start.12 = (bf16[96,256]{1,0:T(8,128)(2,1)S(1)}, bf16[96,256]{1,0:T(8,128)(2,1)S(1)}, u32[]{:S(2)}, u32[]{:S(2)}) collective-permute-start(bf16[96,256]{1,0:T(8,128)(2,1)S(1)} %slice.61), channel_id=1, source_target_pairs={{0,2},{1,3},{2,0},{3,1},{4,6},{5,7},{6,4},{7,5},{8,10},{9,11},{10,... | collective-permute-start | bytes 147464 | tf_op jit(solution)/shard_map/ppermute | solution.py:143
Sparse Core Ops, SparseCore 0:
  106.3 46.1 reduce-scatter.1

commit v6 on v5

--- a/solution.py
+++ b/solution.py
@@ -97,49 +97,125 @@
     return jnp.sum(pieces.astype(jnp.float32), axis=0).astype(jnp.bfloat16)
 
 
-def output_kernel(attended_ref, w_ref, kept_ref, tail_ref):
-    rows = jnp.dot(attended_ref[...], w_ref[...], preferred_element_type=jnp.float32)
-    rows = rows.astype(jnp.bfloat16)
-    kept_ref[...] = rows[:KEEP]
+def output_kernel(
+    z_ref, attended_ref, w_ref, kept_ref, up_ref, down_ref, tail_ref, held, sems
+):
+    wide = kept_ref.shape[2]
     width = tail_ref.shape[2]
-    for d in range(tail_ref.shape[0]):
-        tail_ref[d] = rows[KEEP:, d * width : (d + 1) * width]
+    copies = [
+        pltpu.make_async_copy(w_ref.at[:, pl.ds(z * wide, wide)], held.at[z], sems.at[z])
+        for z in range(N_Z)
+    ]
+    for copy in copies:
+        copy.start()
+    for z in range(N_Z):
+        copies[z].wait()
+        rows = jnp.dot(attended_ref[...], held[z], preferred_element_type=jnp.float32)
+        rows = rows.astype(jnp.bfloat16)
+        kept_ref[z] = rows[:KEEP]
+        for y in range(N_Y):
+            tail_ref[z * N_Y + y] = rows[KEEP:, y * width : (y + 1) * width]
+    far = lax.rem(z_ref[0] + N_Z // 2, N_Z)
+    up_ref[...] = kept_ref[far, : KEEP // 2]
+    down_ref[...] = kept_ref[far, KEEP // 2 :]
 
 
 def output_partials(attended, w_out):
-    depth, wide = w_out.shape
+    depth, columns = w_out.shape
+    wide = columns // N_Z
     n = N_Z * N_Y
+    vmem = pl.BlockSpec(memory_space=pltpu.VMEM)
     return pl.pallas_call(
         output_kernel,
-        grid=(N_Z,),
         in_specs=[
-            pl.BlockSpec((KEEP + MOVE, depth), lambda i: (0, 0)),
-            pl.BlockSpec((depth, wide // N_Z), lambda i: (0, i)),
+            pl.BlockSpec(memory_space=pltpu.SMEM),
+            vmem,
+            pl.BlockSpec(memory_space=pl.ANY),
         ],
-        out_specs=[
-            pl.BlockSpec((KEEP, wide // N_Z), lambda i: (0, i)),
-            pl.BlockSpec((N_Y, MOVE, wide // n), lambda i: (i, 0, 0)),
+        out_specs=[vmem] * 4,
+        out_shape=[
+            jax.ShapeDtypeStruct((N_Z, KEEP, wide), jnp.bfloat16),
+            jax.ShapeDtypeStruct((KEEP // 2, wide), jnp.bfloat16),
+            jax.ShapeDtypeStruct((KEEP // 2, wide), jnp.bfloat16),
+            jax.ShapeDtypeStruct((n, MOVE, columns // n), jnp.bfloat16),
         ],
+        scratch_shapes=[
+            pltpu.VMEM((N_Z, depth, wide), jnp.bfloat16),
+            pltpu.SemaphoreType.DMA((N_Z,)),
+        ],
+        compiler_params=pltpu.CompilerParams(vmem_limit_bytes=32 * 1024 * 1024),
+    )(
+        lax.axis_index("z").reshape(1),
+        attended,
+        pltpu.with_memory_space_constraint(w_out, pltpu.HBM),
+    )
+
+
+def hop_kernel(k, z_ref, up_ref, down_ref, parts_ref, up_out, down_out):
+    above = parts_ref.at[lax.rem(z_ref[0] + k, N_Z)]
+    below = parts_ref.at[lax.rem(z_ref[0] + N_Z - k, N_Z)]
+    n, got = parts_ref.shape[1], up_ref.shape[0]
+
+    def add(a, b):
+        return (a.astype(jnp.float32) + b.astype(jnp.float32)).astype(jnp.bfloat16)
+
+    up_out[:got] = add(above[:got], up_ref[...])
+    down_out[n - got :] = add(below[n - got :], down_ref[...])
+    if got < n:
+        up_out[got:] = above[got:]
+        down_out[: n - got] = below[: n - got]
+
+
+def end_kernel(at_ref, up_ref, down_ref, parts_ref, sent_ref, held_ref, total):
+    own = parts_ref.at[at_ref[0]]
+    total[...] = (
+        own[...].astype(jnp.float32)
+        + up_ref[...].astype(jnp.float32)
+        + down_ref[...].astype(jnp.float32)
+    )
+    me = at_ref[1]
+    width = total.shape[1] // N_Y
+
+    def part(y):
+        return total[:, pl.ds(pl.multiple_of(y * width, width), width)]
+
+    sent_ref[:, :width] = part(me ^ 1).astype(jnp.bfloat16)
+    sent_ref[:, width:] = part(me ^ 3).astype(jnp.bfloat16)
+    held_ref[:, :width] = part(me)
+    held_ref[:, width:] = part(me ^ 2)
+
+
+def scatter_sum_kept(parts, up, down):
+    n, wide = parts.shape[1:]
+    z_me = lax.axis_index("z").reshape(1)
+    vmem, smem = pl.BlockSpec(memory_space=pltpu.VMEM), pl.BlockSpec(memory_space=pltpu.SMEM)
+    params = pltpu.CompilerParams(vmem_limit_bytes=16 * 1024 * 1024)
+    for k in range(N_Z // 2 - 1, -1, -1):
+        up = lax.ppermute(up, "z", ring(N_Z, 1))
+        down = lax.ppermute(down, "z", ring(N_Z, -1))
+        if k:
+            up, down = pl.pallas_call(
+                functools.partial(hop_kernel, k),
+                in_specs=[smem, vmem, vmem, vmem],
+                out_specs=[vmem] * 2,
+                out_shape=[jax.ShapeDtypeStruct((n, wide), jnp.bfloat16)] * 2,
+                compiler_params=params,
+            )(z_me, up, down, parts)
+    at = jnp.stack([lax.axis_index("z"), lax.axis_index("yh")])
+    sent, held = pl.pallas_call(
+        end_kernel,
+        in_specs=[smem, vmem, vmem, vmem],
+        out_specs=[vmem] * 2,
         out_shape=[
-            jax.ShapeDtypeStruct((KEEP, wide), jnp.bfloat16),
-            jax.ShapeDtypeStruct((n, MOVE, wide // n), jnp.bfloat16),
+            jax.ShapeDtypeStruct((n, wide // 2), jnp.bfloat16),
+            jax.ShapeDtypeStruct((n, wide // 2), jnp.float32),
         ],
-        compiler_params=pltpu.CompilerParams(vmem_limit_bytes=16 * 1024 * 1024),
-    )(attended, pltpu.with_memory_space_constraint(w_out, pltpu.HBM))
-
-
-def sum_over_y(rows):
-    me = lax.axis_index("yh")
-    width = rows.shape[1] // N_Y
-
-    def part(y):
-        return lax.dynamic_slice_in_dim(rows, y * width, width, 1)
-
-    near, far = me ^ 1, me ^ 2
-    sent = jnp.concatenate([part(near), part(near ^ 2)], axis=1)
-    held = jnp.concatenate([part(me), part(far)], axis=1)
+        scratch_shapes=[pltpu.VMEM((n, wide), jnp.float32)],
+        compiler_params=params,
+    )(at, up, down, parts)
+    width = wide // N_Y
     got = lax.ppermute(sent, "yh", [(i, i ^ 1) for i in range(N_Y)])
-    held = held.astype(jnp.float32) + got.astype(jnp.float32)
+    held = held + got.astype(jnp.float32)
     got = lax.ppermute(
         held[:, width:].astype(jnp.bfloat16), "yh", [(i, i ^ 2) for i in range(N_Y)]
     )
@@ -210,10 +286,9 @@
     key_rot = rotate(key.astype(jnp.float32), cosine, sine).astype(jnp.bfloat16)
     attended = attend(query_rot.reshape(SEQ, 1, 2, HD), key_rot, value, visible)
 
-    kept, moving = output_partials(attended, w_out)
-    kept = lax.psum_scatter(kept.T, "z", scatter_dimension=0, tiled=True)
+    kept, up, down, moving = output_partials(attended, w_out)
     moving = sum_pieces(lax.all_to_all(moving, TENSOR, 0, 0, tiled=True))
-    kept = sum_over_y(kept.T)
+    kept = scatter_sum_kept(kept, up, down)
 
     slots = lax.iota(jnp.int32, RECV)
     wanted = targets - block * RECV

time: 180 us -> 182 us (1.011)
  the two profiles are of different devices: /device:TPU:4 before, /device:TPU:2 now
where the time goes in v6:
time: 182 us; the launch traced here: 181 us
  starting transfers between devices  105 us (58%)
  waiting for transfers between devices  43.5 us (24%)
  blocking collectives  17.7 us (10%)
  Pallas kernels  6.27 us (3%)
  local copies, waits for them, and re-layouts  4.4 us (2%)
  other arithmetic  2.72 us (1%)
    ppermute x3, starting transfers between devices, shards(): down = lax.ppermute(down, 'z', ring(N_Z, -1))  24.3 us
    all_gather x1, blocking collectives, shards(): own = lax.all_gather(activations, 'yh', axis=1, tiled=True)  17.7 us
    ppermute x4, starting transfers between devices, scatter_sum_kept(): down = lax.ppermute(down, 'z', ring(N_Z, -1))  15 us
    ppermute x4, starting transfers between devices, scatter_sum_kept(): up = lax.ppermute(up, 'z', ring(N_Z, 1))  13.2 us
    ppermute x4, waiting for transfers between devices, scatter_sum_kept(): up = lax.ppermute(up, 'z', ring(N_Z, 1))  11.9 us
    ppermute x3, starting transfers between devices, shards(): up = lax.ppermute(up, 'z', ring(N_Z, 1))  9 us
    all_to_all x1, starting transfers between devices, shards(): lax.all_to_all(tails, DP, 0, 0, tiled=True).reshape(targets.shape[0], -1)  7.96 us
    all_to_all x1, starting transfers between devices, shards(): moving = sum_pieces(lax.all_to_all(moving, TENSOR, 0, 0, tiled=True))  7.89 us
  transfers between devices with their start and end apart: 23, of which 15 were waited for; matrix products, arithmetic and copies ran while one was open for 2% of the time, Pallas kernels for 1%

profile of v6, /device:TPU:2, one launch (start us, length us, event | category | flops | bytes accessed | tf_op | source)
XLA Modules:
  0.0 180.9 jit_solution(18339833769440852464)
XLA Ops:
  0.0 17.7 %all_gather.3.refs_0_ = bf16[128,1024]{1,0:T(8,128)(2,1)S(1)} all-gather(bf16[128,256]{1,0:T(8,128)(2,1)} %param.6), channel_id=1, replica_groups=mesh['x'=8,'yl'=2,'core'=2,'z'=8,'yh'=4] {'yh'}, dimensions={1}, use_global_device_ids=true | all-gather | bytes 327680 | tf_op jit(solution)/shard_map/all_gather | solution.py:271
  17.7 5.2 %collective-permute-start = (bf16[128,1024]{1,0:T(8,128)(2,1)S(1)}, bf16[128,1024]{1,0:T(8,128)(2,1)S(1)}, u32[]{:S(2)}, u32[]{:S(2)}) collective-permute-start(bf16[128,1024]{1,0:T(8,128)(2,1)S(1)} %all_gather.3.refs_0_), channel_id=1, source_target_pairs={{0,4},{4,8},{8,12},{12,16},{16,20},{20,24},{24,28},{28,0},{1,5},{5... | collective-permute-start | bytes 786440 | tf_op jit(solution)/shard_map/ppermute | solution.py:275
  22.9 14.0 %collective-permute-start.1 = (bf16[128,1024]{1,0:T(8,128)(2,1)S(1)}, bf16[128,1024]{1,0:T(8,128)(2,1)S(1)}, u32[]{:S(2)}, u32[]{:S(2)}) collective-permute-start(bf16[128,1024]{1,0:T(8,128)(2,1)S(1)} %all_gather.3.refs_0_), channel_id=1, source_target_pairs={{0,28},{4,0},{8,4},{12,8},{16,12},{20,16},{24,20},{28,24},{1,29},{... | collective-permute-start | bytes 786440 | tf_op jit(solution)/shard_map/ppermute | solution.py:276
  36.9 2.4 %collective-permute-done.refs_1_ = bf16[128,1024]{1,0:T(8,128)(2,1)S(1)} collective-permute-done((bf16[128,1024]{1,0:T(8,128)(2,1)S(1)}, bf16[128,1024]{1,0:T(8,128)(2,1)S(1)}, u32[]{:S(2)}, u32[]{:S(2)}) %collective-permute-start) | collective-permute-done | bytes 262176 | tf_op jit(solution)/shard_map/ppermute | solution.py:275
  39.3 1.9 %collective-permute-start.2 = (bf16[128,1024]{1,0:T(8,128)(2,1)S(1)}, bf16[128,1024]{1,0:T(8,128)(2,1)S(1)}, u32[]{:S(2)}, u32[]{:S(2)}) collective-permute-start(bf16[128,1024]{1,0:T(8,128)(2,1)S(1)} %collective-permute-done.refs_1_), channel_id=1, source_target_pairs={{0,4},{4,8},{8,12},{12,16},{16,20},{20,24},{24,28},{28,0},{1,5},{5... | collective-permute-start | bytes 786440 | tf_op jit(solution)/shard_map/ppermute | solution.py:275
  41.3 5.1 %collective-permute-start.3 = (bf16[128,1024]{1,0:T(8,128)(2,1)S(1)}, bf16[128,1024]{1,0:T(8,128)(2,1)S(1)}, u32[]{:S(2)}, u32[]{:S(2)}) collective-permute-start(bf16[128,1024]{1,0:T(8,128)(2,1)S(1)} %collective-permute-done.1.refs_2_), channel_id=1, source_target_pairs={{0,28},{4,0},{8,4},{12,8},{16,12},{20,16},{24,20},{28,24},{1,29},{... | collective-permute-start | bytes 786440 | tf_op jit(solution)/shard_map/ppermute | solution.py:276
  46.4 0.8 fusion.24
  47.2 0.7 slice.30
  48.0 0.8 collective-permute-done.2.refs_3_
  48.8 1.9 %collective-permute-start.4 = (bf16[128,1024]{1,0:T(8,128)(2,1)S(1)}, bf16[128,1024]{1,0:T(8,128)(2,1)S(1)}, u32[]{:S(2)}, u32[]{:S(2)}) collective-permute-start(bf16[128,1024]{1,0:T(8,128)(2,1)S(1)} %collective-permute-done.2.refs_3_), channel_id=1, source_target_pairs={{0,4},{4,8},{8,12},{12,16},{16,20},{20,24},{24,28},{28,0},{1,5},{5... | collective-permute-start | bytes 786440 | tf_op jit(solution)/shard_map/ppermute | solution.py:275
  50.7 5.1 %collective-permute-start.5 = (bf16[128,1024]{1,0:T(8,128)(2,1)S(1)}, bf16[128,1024]{1,0:T(8,128)(2,1)S(1)}, u32[]{:S(2)}, u32[]{:S(2)}) collective-permute-start(bf16[128,1024]{1,0:T(8,128)(2,1)S(1)} %collective-permute-done.3.refs_4_), channel_id=1, source_target_pairs={{0,28},{4,0},{8,4},{12,8},{16,12},{20,16},{24,20},{28,24},{1,29},{... | collective-permute-start | bytes 786440 | tf_op jit(solution)/shard_map/ppermute | solution.py:276
  56.5 2.1 %collective-permute-done.4.refs_5_ = bf16[128,1024]{1,0:T(8,128)(2,1)S(1)} collective-permute-done((bf16[128,1024]{1,0:T(8,128)(2,1)S(1)}, bf16[128,1024]{1,0:T(8,128)(2,1)S(1)}, u32[]{:S(2)}, u32[]{:S(2)}) %collective-permute-start.4) | collective-permute-done | bytes 262176 | tf_op jit(solution)/shard_map/ppermute | solution.py:275
  58.6 1.9 %collective-permute-start.6 = (bf16[64,1024]{1,0:T(8,128)(2,1)S(1)}, bf16[64,1024]{1,0:T(8,128)(2,1)S(1)}, u32[]{:S(2)}, u32[]{:S(2)}) collective-permute-start(bf16[64,1024]{1,0:T(8,128)(2,1)S(1)} %slice.37), channel_id=1, source_target_pairs={{0,4},{4,8},{8,12},{12,16},{16,20},{20,24},{24,28},{28,0},{1,5},{5... | collective-permute-start | bytes 393224 | tf_op jit(solution)/shard_map/ppermute | solution.py:279
  60.5 5.4 %collective-permute-start.7 = (bf16[64,1024]{1,0:T(8,128)(2,1)S(1)}, bf16[64,1024]{1,0:T(8,128)(2,1)S(1)}, u32[]{:S(2)}, u32[]{:S(2)}) collective-permute-start(bf16[64,1024]{1,0:T(8,128)(2,1)S(1)} %slice.38), channel_id=1, source_target_pairs={{0,28},{4,0},{8,4},{12,8},{16,12},{20,16},{24,20},{28,24},{1,29},{... | collective-permute-start | bytes 393224 | tf_op jit(solution)/shard_map/ppermute | solution.py:280
  66.0 0.6 collective-permute-done.6.refs_7_
  66.7 1.8 collective-permute-done.7.refs_8_
  68.4 2.2 %copy-done = bf16[8192,256]{1,0:T(8,128)(2,1)S(1)} copy-done((bf16[8192,256]{1,0:T(8,128)(2,1)S(1)}, bf16[8192,256]{1,0:T(8,128)(2,1)}, u32[]{:S(2)}) %copy-start) | copy-done | bytes 4194328
  70.6 0.8 shard_map.65
  71.6 0.7 shard_map.64
  72.3 1.9 %collective-permute-start.8 = (bf16[128,64]{1,0:T(8,128)(2,1)S(1)}, bf16[128,64]{1,0:T(8,128)(2,1)S(1)}, u32[]{:S(2)}, u32[]{:S(2)}) collective-permute-start(bf16[128,64]{1,0:T(8,128)(2,1)S(1)} %shard_map.64), channel_id=1, source_target_pairs={{0,1},{1,0},{2,3},{3,2},{4,5},{5,4},{6,7},{7,6},{8,9},{9,8},{10,11... | collective-permute-start | bytes 49160 | tf_op jit(solution)/shard_map/ppermute | solution.py:76
  74.4 4.9 %collective-permute-done.8 = bf16[128,64]{1,0:T(8,128)(2,1)S(1)} collective-permute-done((bf16[128,64]{1,0:T(8,128)(2,1)S(1)}, bf16[128,64]{1,0:T(8,128)(2,1)S(1)}, u32[]{:S(2)}, u32[]{:S(2)}) %collective-permute-start.8) | collective-permute-done | bytes 16416 | tf_op jit(solution)/shard_map/ppermute | solution.py:76
  79.4 0.7 collective-permute-start.10
  80.0 7.1 %collective-permute-start.9 = (bf16[128,128]{1,0:T(8,128)(2,1)S(1)}, bf16[128,128]{1,0:T(8,128)(2,1)S(1)}, u32[]{:S(2)}, u32[]{:S(2)}) collective-permute-start(bf16[128,128]{1,0:T(8,128)(2,1)S(1)} %pad_maximum_fusion.1), channel_id=1, source_target_pairs={{0,2},{1,3},{2,6},{3,7},{4,10},{5,11},{6,14},{7,15},{8,18},{9,19},... | collective-permute-start | bytes 98312 | tf_op jit(solution)/shard_map/ppermute | solution.py:89
  87.2 6.8 %collective-permute-done.9 = bf16[128,128]{1,0:T(8,128)(2,1)S(1)} collective-permute-done((bf16[128,128]{1,0:T(8,128)(2,1)S(1)}, bf16[128,128]{1,0:T(8,128)(2,1)S(1)}, u32[]{:S(2)}, u32[]{:S(2)}) %collective-permute-start.9) | collective-permute-done | bytes 32800 | tf_op jit(solution)/shard_map/ppermute | solution.py:89
  95.0 3.8 %shard_map.66 = (bf16[8,96,1024]{2,1,0:T(8,128)(2,1)S(1)}, bf16[48,1024]{1,0:T(8,128)(2,1)S(1)}, bf16[48,1024]{1,0:T(8,128)(2,1)S(1)}, bf16[32,32,256]{2,1,0:T(8,128)(2,1)}) custom-call(s32[1]{0:T(128)} %bitcast.z_ref, bf16[128,256]{1,0:T(8,128)(2,1)S(1)} %copy.15.attended_ref, bf16[256,8192]{1,0:T(8,128)(2,1)} %w_ref.1), custom_call_target="tpu_custom_call" | custom-call | tf_op jit(solution)/shard_map/pallas_call | solution.py:128
  98.9 7.9 %all-to-all-start = ((bf16[32,32,256]{2,1,0:T(8,128)(2,1)}), bf16[32,32,256]{2,1,0:T(8,128)(2,1)S(1)}, u32[]{:S(2)}, u32[]{:S(2)}) async-start(bf16[32,32,256]{2,1,0:T(8,128)(2,1)} %get-tuple-element.28), calls=%async_computation | async-start | bytes 1048576 | tf_op jit(solution)/shard_map/all_to_all | solution.py:290
  106.8 3.7 %collective-permute-start.11 = (bf16[48,1024]{1,0:T(8,128)(2,1)S(1)}, bf16[48,1024]{1,0:T(8,128)(2,1)S(1)}, u32[]{:S(2)}, u32[]{:S(2)}) collective-permute-start(bf16[48,1024]{1,0:T(8,128)(2,1)S(1)} %get-tuple-element.17), channel_id=1, source_target_pairs={{0,4},{4,8},{8,12},{12,16},{16,20},{20,24},{24,28},{28,0},{1,5},{5... | collective-permute-start | bytes 294920 | tf_op jit(solution)/shard_map/ppermute | solution.py:194
  110.5 3.4 %collective-permute-start.12 = (bf16[48,1024]{1,0:T(8,128)(2,1)S(1)}, bf16[48,1024]{1,0:T(8,128)(2,1)S(1)}, u32[]{:S(2)}, u32[]{:S(2)}) collective-permute-start(bf16[48,1024]{1,0:T(8,128)(2,1)S(1)} %get-tuple-element.18), channel_id=1, source_target_pairs={{0,28},{4,0},{8,4},{12,8},{16,12},{20,16},{24,20},{28,24},{1,29},{... | collective-permute-start | bytes 294920 | tf_op jit(solution)/shard_map/ppermute | solution.py:195
  113.8 5.5 %collective-permute-done.11.up_ref = bf16[48,1024]{1,0:T(8,128)(2,1)S(1)} collective-permute-done((bf16[48,1024]{1,0:T(8,128)(2,1)S(1)}, bf16[48,1024]{1,0:T(8,128)(2,1)S(1)}, u32[]{:S(2)}, u32[]{:S(2)}) %collective-permute-start.11) | collective-permute-done | bytes 98336 | tf_op jit(solution)/shard_map/ppermute | solution.py:194
  119.3 1.0 collective-permute-done.12.down_ref
  120.4 3.3 %collective-permute-start.13 = (bf16[96,1024]{1,0:T(8,128)(2,1)S(1)}, bf16[96,1024]{1,0:T(8,128)(2,1)S(1)}, u32[]{:S(2)}, u32[]{:S(2)}) collective-permute-start(bf16[96,1024]{1,0:T(8,128)(2,1)S(1)} %get-tuple-element.20), channel_id=1, source_target_pairs={{0,4},{4,8},{8,12},{12,16},{16,20},{20,24},{24,28},{28,0},{1,5},{5... | collective-permute-start | bytes 589832 | tf_op jit(solution)/shard_map/ppermute | solution.py:194
  123.7 3.7 %collective-permute-start.14 = (bf16[96,1024]{1,0:T(8,128)(2,1)S(1)}, bf16[96,1024]{1,0:T(8,128)(2,1)S(1)}, u32[]{:S(2)}, u32[]{:S(2)}) collective-permute-start(bf16[96,1024]{1,0:T(8,128)(2,1)S(1)} %get-tuple-element.21), channel_id=1, source_target_pairs={{0,28},{4,0},{8,4},{12,8},{16,12},{20,16},{24,20},{28,24},{1,29},{... | collective-permute-start | bytes 589832 | tf_op jit(solution)/shard_map/ppermute | solution.py:195
  127.5 3.5 %collective-permute-done.13.up_ref = bf16[96,1024]{1,0:T(8,128)(2,1)S(1)} collective-permute-done((bf16[96,1024]{1,0:T(8,128)(2,1)S(1)}, bf16[96,1024]{1,0:T(8,128)(2,1)S(1)}, u32[]{:S(2)}, u32[]{:S(2)}) %collective-permute-start.13) | collective-permute-done | bytes 196640 | tf_op jit(solution)/shard_map/ppermute | solution.py:194
  131.0 2.3 %collective-permute-done.14.down_ref = bf16[96,1024]{1,0:T(8,128)(2,1)S(1)} collective-permute-done((bf16[96,1024]{1,0:T(8,128)(2,1)S(1)}, bf16[96,1024]{1,0:T(8,128)(2,1)S(1)}, u32[]{:S(2)}, u32[]{:S(2)}) %collective-permute-start.14) | collective-permute-done | bytes 196640 | tf_op jit(solution)/shard_map/ppermute | solution.py:195
  133.4 3.8 %collective-permute-start.15 = (bf16[96,1024]{1,0:T(8,128)(2,1)S(1)}, bf16[96,1024]{1,0:T(8,128)(2,1)S(1)}, u32[]{:S(2)}, u32[]{:S(2)}) collective-permute-start(bf16[96,1024]{1,0:T(8,128)(2,1)S(1)} %get-tuple-element.22), channel_id=1, source_target_pairs={{0,4},{4,8},{8,12},{12,16},{16,20},{20,24},{24,28},{28,0},{1,5},{5... | collective-permute-start | bytes 589832 | tf_op jit(solution)/shard_map/ppermute | solution.py:194
  137.2 3.3 %collective-permute-start.16 = (bf16[96,1024]{1,0:T(8,128)(2,1)S(1)}, bf16[96,1024]{1,0:T(8,128)(2,1)S(1)}, u32[]{:S(2)}, u32[]{:S(2)}) collective-permute-start(bf16[96,1024]{1,0:T(8,128)(2,1)S(1)} %get-tuple-element.23), channel_id=1, source_target_pairs={{0,28},{4,0},{8,4},{12,8},{16,12},{20,16},{24,20},{28,24},{1,29},{... | collective-permute-start | bytes 589832 | tf_op jit(solution)/shard_map/ppermute | solution.py:195
  140.6 0.9 broadcast_in_dim.12
  141.5 8.0 %all-to-all-start.1 = ((bf16[32,32,256]{2,1,0:T(8,128)(2,1)}), bf16[32,32,256]{2,1,0:T(8,128)(2,1)S(1)}, u32[]{:S(2)}, u32[]{:S(2)}) async-start(bf16[32,32,256]{2,1,0:T(8,128)(2,1)} %broadcast_in_dim.12), calls=%async_computation.1 | async-start | bytes 1048576 | tf_op jit(solution)/shard_map/all_to_all | solution.py:297
  149.6 2.4 %collective-permute-start.17 = (bf16[96,1024]{1,0:T(8,128)(2,1)S(1)}, bf16[96,1024]{1,0:T(8,128)(2,1)S(1)}, u32[]{:S(2)}, u32[]{:S(2)}) collective-permute-start(bf16[96,1024]{1,0:T(8,128)(2,1)S(1)} %get-tuple-element.24), channel_id=1, source_target_pairs={{0,4},{4,8},{8,12},{12,16},{16,20},{20,24},{24,28},{28,0},{1,5},{5... | collective-permute-start | bytes 589832 | tf_op jit(solution)/shard_map/ppermute | solution.py:194
  152.0 4.7 %collective-permute-start.18 = (bf16[96,1024]{1,0:T(8,128)(2,1)S(1)}, bf16[96,1024]{1,0:T(8,128)(2,1)S(1)}, u32[]{:S(2)}, u32[]{:S(2)}) collective-permute-start(bf16[96,1024]{1,0:T(8,128)(2,1)S(1)} %get-tuple-element.25), channel_id=1, source_target_pairs={{0,28},{4,0},{8,4},{12,8},{16,12},{20,16},{24,20},{28,24},{1,29},{... | collective-permute-start | bytes 589832 | tf_op jit(solution)/shard_map/ppermute | solution.py:195
  156.7 2.9 %collective-permute-done.17.up_ref = bf16[96,1024]{1,0:T(8,128)(2,1)S(1)} collective-permute-done((bf16[96,1024]{1,0:T(8,128)(2,1)S(1)}, bf16[96,1024]{1,0:T(8,128)(2,1)S(1)}, u32[]{:S(2)}, u32[]{:S(2)}) %collective-permute-start.17) | collective-permute-done | bytes 196640 | tf_op jit(solution)/shard_map/ppermute | solution.py:194
  159.6 1.2 collective-permute-done.18.down_ref
  160.8 0.7 shard_map.70
  161.5 4.5 %collective-permute-start.19 = (bf16[96,512]{1,0:T(8,128)(2,1)S(1)}, bf16[96,512]{1,0:T(8,128)(2,1)S(1)}, u32[]{:S(2)}, u32[]{:S(2)}) collective-permute-start(bf16[96,512]{1,0:T(8,128)(2,1)S(1)} %get-tuple-element.27), channel_id=1, source_target_pairs={{0,1},{1,0},{2,3},{3,2},{4,5},{5,4},{6,7},{7,6},{8,9},{9,8},{10,11... | collective-permute-start | bytes 294920 | tf_op jit(solution)/shard_map/ppermute | solution.py:217
  166.0 4.1 %collective-permute-done.19 = bf16[96,512]{1,0:T(8,128)(2,1)S(1)} collective-permute-done((bf16[96,512]{1,0:T(8,128)(2,1)S(1)}, bf16[96,512]{1,0:T(8,128)(2,1)S(1)}, u32[]{:S(2)}, u32[]{:S(2)}) %collective-permute-start.19) | collective-permute-done | bytes 98336 | tf_op jit(solution)/shard_map/ppermute | solution.py:217
  170.1 6.2 %collective-permute-start.20 = (bf16[96,256]{1,0:T(8,128)(2,1)S(1)}, bf16[96,256]{1,0:T(8,128)(2,1)S(1)}, u32[]{:S(2)}, u32[]{:S(2)}) collective-permute-start(bf16[96,256]{1,0:T(8,128)(2,1)S(1)} %slice.61), channel_id=1, source_target_pairs={{0,2},{1,3},{2,0},{3,1},{4,6},{5,7},{6,4},{7,5},{8,10},{9,11},{10,... | collective-permute-start | bytes 147464 | tf_op jit(solution)/shard_map/ppermute | solution.py:219
  176.4 3.6 %collective-permute-done.20 = bf16[96,256]{1,0:T(8,128)(2,1)S(1)} collective-permute-done((bf16[96,256]{1,0:T(8,128)(2,1)S(1)}, bf16[96,256]{1,0:T(8,128)(2,1)S(1)}, u32[]{:S(2)}, u32[]{:S(2)}) %collective-permute-start.20) | collective-permute-done | bytes 49184 | tf_op jit(solution)/shard_map/ppermute | solution.py:219
  180.2 0.6 pad_maximum_fusion
  (50 shorter events, 2.9 us)
Async XLA Ops:
  0.0 71.5 %copy-start.1 = (bf16[8192,64]{0,1:T(8,128)(2,1)S(1)}, bf16[8192,64]{0,1:T(8,128)(2,1)}, u32[]{:S(2)}) copy-start(bf16[8192,64]{0,1:T(8,128)(2,1)} %param.8) | copy-start | bytes 3145732
  17.7 21.7 %collective-permute-start = (bf16[128,1024]{1,0:T(8,128)(2,1)S(1)}, bf16[128,1024]{1,0:T(8,128)(2,1)S(1)}, u32[]{:S(2)}, u32[]{:S(2)}) collective-permute-start(bf16[128,1024]{1,0:T(8,128)(2,1)S(1)} %all_gather.3.refs_0_), channel_id=1, source_target_pairs={{0,4},{4,8},{8,12},{12,16},{16,20},{20,24},{24,28},{28,0},{1,5},{5... | collective-permute-start | bytes 786440 | tf_op jit(solution)/shard_map/ppermute | solution.py:275
  22.9 18.4 %collective-permute-start.1 = (bf16[128,1024]{1,0:T(8,128)(2,1)S(1)}, bf16[128,1024]{1,0:T(8,128)(2,1)S(1)}, u32[]{:S(2)}, u32[]{:S(2)}) collective-permute-start(bf16[128,1024]{1,0:T(8,128)(2,1)S(1)} %all_gather.3.refs_0_), channel_id=1, source_target_pairs={{0,28},{4,0},{8,4},{12,8},{16,12},{20,16},{24,20},{28,24},{1,29},{... | collective-permute-start | bytes 786440 | tf_op jit(solution)/shard_map/ppermute | solution.py:276
  39.3 9.5 %collective-permute-start.2 = (bf16[128,1024]{1,0:T(8,128)(2,1)S(1)}, bf16[128,1024]{1,0:T(8,128)(2,1)S(1)}, u32[]{:S(2)}, u32[]{:S(2)}) collective-permute-start(bf16[128,1024]{1,0:T(8,128)(2,1)S(1)} %collective-permute-done.refs_1_), channel_id=1, source_target_pairs={{0,4},{4,8},{8,12},{12,16},{16,20},{20,24},{24,28},{28,0},{1,5},{5... | collective-permute-start | bytes 786440 | tf_op jit(solution)/shard_map/ppermute | solution.py:275
  41.3 9.5 %collective-permute-start.3 = (bf16[128,1024]{1,0:T(8,128)(2,1)S(1)}, bf16[128,1024]{1,0:T(8,128)(2,1)S(1)}, u32[]{:S(2)}, u32[]{:S(2)}) collective-permute-start(bf16[128,1024]{1,0:T(8,128)(2,1)S(1)} %collective-permute-done.1.refs_2_), channel_id=1, source_target_pairs={{0,28},{4,0},{8,4},{12,8},{16,12},{20,16},{24,20},{28,24},{1,29},{... | collective-permute-start | bytes 786440 | tf_op jit(solution)/shard_map/ppermute | solution.py:276
  48.8 9.8 %collective-permute-start.4 = (bf16[128,1024]{1,0:T(8,128)(2,1)S(1)}, bf16[128,1024]{1,0:T(8,128)(2,1)S(1)}, u32[]{:S(2)}, u32[]{:S(2)}) collective-permute-start(bf16[128,1024]{1,0:T(8,128)(2,1)S(1)} %collective-permute-done.2.refs_3_), channel_id=1, source_target_pairs={{0,4},{4,8},{8,12},{12,16},{16,20},{20,24},{24,28},{28,0},{1,5},{5... | collective-permute-start | bytes 786440 | tf_op jit(solution)/shard_map/ppermute | solution.py:275
  50.7 9.8 %collective-permute-start.5 = (bf16[128,1024]{1,0:T(8,128)(2,1)S(1)}, bf16[128,1024]{1,0:T(8,128)(2,1)S(1)}, u32[]{:S(2)}, u32[]{:S(2)}) collective-permute-start(bf16[128,1024]{1,0:T(8,128)(2,1)S(1)} %collective-permute-done.3.refs_4_), channel_id=1, source_target_pairs={{0,28},{4,0},{8,4},{12,8},{16,12},{20,16},{24,20},{28,24},{1,29},{... | collective-permute-start | bytes 786440 | tf_op jit(solution)/shard_map/ppermute | solution.py:276
  55.9 0.6 copy-start.3
  55.9 0.6 copy-start.5
  58.6 8.1 %collective-permute-start.6 = (bf16[64,1024]{1,0:T(8,128)(2,1)S(1)}, bf16[64,1024]{1,0:T(8,128)(2,1)S(1)}, u32[]{:S(2)}, u32[]{:S(2)}) collective-permute-start(bf16[64,1024]{1,0:T(8,128)(2,1)S(1)} %slice.37), channel_id=1, source_target_pairs={{0,4},{4,8},{8,12},{12,16},{16,20},{20,24},{24,28},{28,0},{1,5},{5... | collective-permute-start | bytes 393224 | tf_op jit(solution)/shard_map/ppermute | solution.py:279
  60.5 7.9 %collective-permute-start.7 = (bf16[64,1024]{1,0:T(8,128)(2,1)S(1)}, bf16[64,1024]{1,0:T(8,128)(2,1)S(1)}, u32[]{:S(2)}, u32[]{:S(2)}) collective-permute-start(bf16[64,1024]{1,0:T(8,128)(2,1)S(1)} %slice.38), channel_id=1, source_target_pairs={{0,28},{4,0},{8,4},{12,8},{16,12},{20,16},{24,20},{28,24},{1,29},{... | collective-permute-start | bytes 393224 | tf_op jit(solution)/shard_map/ppermute | solution.py:280
  68.4 2.2 %copy-start = (bf16[8192,256]{1,0:T(8,128)(2,1)S(1)}, bf16[8192,256]{1,0:T(8,128)(2,1)}, u32[]{:S(2)}) copy-start(bf16[8192,256]{1,0:T(8,128)(2,1)} %refs_9_.1) | copy-start | bytes 12582916
  71.5 22.5 %copy-start.4 = (f32[64]{0:T(128)S(1)}, f32[64]{0:T(128)}, u32[]{:S(2)}) copy-start(f32[64]{0:T(128)} %copy-done.3) | copy-start | bytes 772
  71.5 22.5 %copy-start.6 = (f32[128]{0:T(128)S(1)}, f32[128]{0:T(128)}, u32[]{:S(2)}) copy-start(f32[128]{0:T(128)} %copy-done.5) | copy-start | bytes 1540
  72.3 7.0 %collective-permute-start.8 = (bf16[128,64]{1,0:T(8,128)(2,1)S(1)}, bf16[128,64]{1,0:T(8,128)(2,1)S(1)}, u32[]{:S(2)}, u32[]{:S(2)}) collective-permute-start(bf16[128,64]{1,0:T(8,128)(2,1)S(1)} %shard_map.64), channel_id=1, source_target_pairs={{0,1},{1,0},{2,3},{3,2},{4,5},{5,4},{6,7},{7,6},{8,9},{9,8},{10,11... | collective-permute-start | bytes 49160 | tf_op jit(solution)/shard_map/ppermute | solution.py:76
  79.4 7.8 %collective-permute-start.10 = (bf16[128,128]{1,0:T(8,128)(2,1)S(1)}, bf16[128,128]{1,0:T(8,128)(2,1)S(1)}, u32[]{:S(2)}, u32[]{:S(2)}) collective-permute-start(bf16[128,128]{1,0:T(8,128)(2,1)S(1)} %pad_maximum_fusion.1), channel_id=1, source_target_pairs={{0,0},{1,1},{2,4},{3,5},{4,8},{5,9},{6,12},{7,13},{8,16},{9,17},{1... | collective-permute-start | bytes 98312 | tf_op jit(solution)/shard_map/ppermute | solution.py:88
  80.0 14.0 %collective-permute-start.9 = (bf16[128,128]{1,0:T(8,128)(2,1)S(1)}, bf16[128,128]{1,0:T(8,128)(2,1)S(1)}, u32[]{:S(2)}, u32[]{:S(2)}) collective-permute-start(bf16[128,128]{1,0:T(8,128)(2,1)S(1)} %pad_maximum_fusion.1), channel_id=1, source_target_pairs={{0,2},{1,3},{2,6},{3,7},{4,10},{5,11},{6,14},{7,15},{8,18},{9,19},... | collective-permute-start | bytes 98312 | tf_op jit(solution)/shard_map/ppermute | solution.py:89
  98.9 41.6 %all-to-all-start = ((bf16[32,32,256]{2,1,0:T(8,128)(2,1)}), bf16[32,32,256]{2,1,0:T(8,128)(2,1)S(1)}, u32[]{:S(2)}, u32[]{:S(2)}) async-start(bf16[32,32,256]{2,1,0:T(8,128)(2,1)} %get-tuple-element.28), calls=%async_computation | async-start | bytes 1048576 | tf_op jit(solution)/shard_map/all_to_all | solution.py:290
  106.8 12.6 %collective-permute-start.11 = (bf16[48,1024]{1,0:T(8,128)(2,1)S(1)}, bf16[48,1024]{1,0:T(8,128)(2,1)S(1)}, u32[]{:S(2)}, u32[]{:S(2)}) collective-permute-start(bf16[48,1024]{1,0:T(8,128)(2,1)S(1)} %get-tuple-element.17), channel_id=1, source_target_pairs={{0,4},{4,8},{8,12},{12,16},{16,20},{20,24},{24,28},{28,0},{1,5},{5... | collective-permute-start | bytes 294920 | tf_op jit(solution)/shard_map/ppermute | solution.py:194
  110.5 9.9 %collective-permute-start.12 = (bf16[48,1024]{1,0:T(8,128)(2,1)S(1)}, bf16[48,1024]{1,0:T(8,128)(2,1)S(1)}, u32[]{:S(2)}, u32[]{:S(2)}) collective-permute-start(bf16[48,1024]{1,0:T(8,128)(2,1)S(1)} %get-tuple-element.18), channel_id=1, source_target_pairs={{0,28},{4,0},{8,4},{12,8},{16,12},{20,16},{24,20},{28,24},{1,29},{... | collective-permute-start | bytes 294920 | tf_op jit(solution)/shard_map/ppermute | solution.py:195
  120.4 10.6 %collective-permute-start.13 = (bf16[96,1024]{1,0:T(8,128)(2,1)S(1)}, bf16[96,1024]{1,0:T(8,128)(2,1)S(1)}, u32[]{:S(2)}, u32[]{:S(2)}) collective-permute-start(bf16[96,1024]{1,0:T(8,128)(2,1)S(1)} %get-tuple-element.20), channel_id=1, source_target_pairs={{0,4},{4,8},{8,12},{12,16},{16,20},{20,24},{24,28},{28,0},{1,5},{5... | collective-permute-start | bytes 589832 | tf_op jit(solution)/shard_map/ppermute | solution.py:194
  123.7 52.6 %copy-start.2 = (s32[1024]{0:T(1024)S(1)}, s32[1024]{0:T(1024)}, u32[]{:S(2)}) copy-start(s32[1024]{0:T(1024)} %param.10) | copy-start | bytes 12292
  123.7 9.6 %collective-permute-start.14 = (bf16[96,1024]{1,0:T(8,128)(2,1)S(1)}, bf16[96,1024]{1,0:T(8,128)(2,1)S(1)}, u32[]{:S(2)}, u32[]{:S(2)}) collective-permute-start(bf16[96,1024]{1,0:T(8,128)(2,1)S(1)} %get-tuple-element.21), channel_id=1, source_target_pairs={{0,28},{4,0},{8,4},{12,8},{16,12},{20,16},{24,20},{28,24},{1,29},{... | collective-permute-start | bytes 589832 | tf_op jit(solution)/shard_map/ppermute | solution.py:195
  133.4 16.0 %collective-permute-start.15 = (bf16[96,1024]{1,0:T(8,128)(2,1)S(1)}, bf16[96,1024]{1,0:T(8,128)(2,1)S(1)}, u32[]{:S(2)}, u32[]{:S(2)}) collective-permute-start(bf16[96,1024]{1,0:T(8,128)(2,1)S(1)} %get-tuple-element.22), channel_id=1, source_target_pairs={{0,4},{4,8},{8,12},{12,16},{16,20},{20,24},{24,28},{28,0},{1,5},{5... | collective-permute-start | bytes 589832 | tf_op jit(solution)/shard_map/ppermute | solution.py:194
  137.2 12.2 %collective-permute-start.16 = (bf16[96,1024]{1,0:T(8,128)(2,1)S(1)}, bf16[96,1024]{1,0:T(8,128)(2,1)S(1)}, u32[]{:S(2)}, u32[]{:S(2)}) collective-permute-start(bf16[96,1024]{1,0:T(8,128)(2,1)S(1)} %get-tuple-element.23), channel_id=1, source_target_pairs={{0,28},{4,0},{8,4},{12,8},{16,12},{20,16},{24,20},{28,24},{1,29},{... | collective-permute-start | bytes 589832 | tf_op jit(solution)/shard_map/ppermute | solution.py:195
  141.5 38.6 %all-to-all-start.1 = ((bf16[32,32,256]{2,1,0:T(8,128)(2,1)}), bf16[32,32,256]{2,1,0:T(8,128)(2,1)S(1)}, u32[]{:S(2)}, u32[]{:S(2)}) async-start(bf16[32,32,256]{2,1,0:T(8,128)(2,1)} %broadcast_in_dim.12), calls=%async_computation.1 | async-start | bytes 1048576 | tf_op jit(solution)/shard_map/all_to_all | solution.py:297
  149.6 10.1 %collective-permute-start.17 = (bf16[96,1024]{1,0:T(8,128)(2,1)S(1)}, bf16[96,1024]{1,0:T(8,128)(2,1)S(1)}, u32[]{:S(2)}, u32[]{:S(2)}) collective-permute-start(bf16[96,1024]{1,0:T(8,128)(2,1)S(1)} %get-tuple-element.24), channel_id=1, source_target_pairs={{0,4},{4,8},{8,12},{12,16},{16,20},{20,24},{24,28},{28,0},{1,5},{5... | collective-permute-start | bytes 589832 | tf_op jit(solution)/shard_map/ppermute | solution.py:194
  152.0 8.8 %collective-permute-start.18 = (bf16[96,1024]{1,0:T(8,128)(2,1)S(1)}, bf16[96,1024]{1,0:T(8,128)(2,1)S(1)}, u32[]{:S(2)}, u32[]{:S(2)}) collective-permute-start(bf16[96,1024]{1,0:T(8,128)(2,1)S(1)} %get-tuple-element.25), channel_id=1, source_target_pairs={{0,28},{4,0},{8,4},{12,8},{16,12},{20,16},{24,20},{28,24},{1,29},{... | collective-permute-start | bytes 589832 | tf_op jit(solution)/shard_map/ppermute | solution.py:195
  161.5 8.6 %collective-permute-start.19 = (bf16[96,512]{1,0:T(8,128)(2,1)S(1)}, bf16[96,512]{1,0:T(8,128)(2,1)S(1)}, u32[]{:S(2)}, u32[]{:S(2)}) collective-permute-start(bf16[96,512]{1,0:T(8,128)(2,1)S(1)} %get-tuple-element.27), channel_id=1, source_target_pairs={{0,1},{1,0},{2,3},{3,2},{4,5},{5,4},{6,7},{7,6},{8,9},{9,8},{10,11... | collective-permute-start | bytes 294920 | tf_op jit(solution)/shard_map/ppermute | solution.py:217
  170.1 9.9 %collective-permute-start.20 = (bf16[96,256]{1,0:T(8,128)(2,1)S(1)}, bf16[96,256]{1,0:T(8,128)(2,1)S(1)}, u32[]{:S(2)}, u32[]{:S(2)}) collective-permute-start(bf16[96,256]{1,0:T(8,128)(2,1)S(1)} %slice.61), channel_id=1, source_target_pairs={{0,2},{1,3},{2,0},{3,1},{4,6},{5,7},{6,4},{7,5},{8,10},{9,11},{10,... | collective-permute-start | bytes 147464 | tf_op jit(solution)/shard_map/ppermute | solution.py:219

commit v7 on v6

--- a/solution.py
+++ b/solution.py
@@ -90,7 +90,7 @@
     first = y_me < 2
     key = jnp.where(first, straight, crossed)
     value = jnp.where(first, crossed, straight)
-    return key.reshape(rows, 1, HD), value.reshape(rows, 1, HD)
+    return key.reshape(rows, 1, HD), value.reshape(rows, 1, HD), whole
 
 
 def sum_pieces(pieces):
@@ -151,7 +151,7 @@
     )
 
 
-def hop_kernel(k, z_ref, up_ref, down_ref, parts_ref, up_out, down_out):
+def hop_kernel(k, z_ref, after_ref, up_ref, down_ref, parts_ref, up_out, down_out):
     above = parts_ref.at[lax.rem(z_ref[0] + k, N_Z)]
     below = parts_ref.at[lax.rem(z_ref[0] + N_Z - k, N_Z)]
     n, got = parts_ref.shape[1], up_ref.shape[0]
@@ -166,63 +166,68 @@
         down_out[: n - got] = below[: n - got]
 
 
-def end_kernel(at_ref, up_ref, down_ref, parts_ref, sent_ref, held_ref, total):
-    own = parts_ref.at[at_ref[0]]
-    total[...] = (
+def end_kernel(z_ref, after_ref, up_ref, down_ref, parts_ref, out_ref):
+    own = parts_ref.at[z_ref[0]]
+    total = (
         own[...].astype(jnp.float32)
         + up_ref[...].astype(jnp.float32)
         + down_ref[...].astype(jnp.float32)
-    )
-    me = at_ref[1]
-    width = total.shape[1] // N_Y
-
-    def part(y):
-        return total[:, pl.ds(pl.multiple_of(y * width, width), width)]
-
-    sent_ref[:, :width] = part(me ^ 1).astype(jnp.bfloat16)
-    sent_ref[:, width:] = part(me ^ 3).astype(jnp.bfloat16)
-    held_ref[:, :width] = part(me)
-    held_ref[:, width:] = part(me ^ 2)
-
-
-def scatter_sum_kept(parts, up, down):
+    ).astype(jnp.bfloat16)
+    width = out_ref.shape[2]
+    for y in range(N_Y):
+        out_ref[y] = total[:, y * width : (y + 1) * width]
+
+
+def spread_kernel(after_ref, pieces_ref, out_ref):
+    total = jnp.sum(pieces_ref[...].astype(jnp.float32), axis=0).astype(jnp.bfloat16)
+    for d in range(out_ref.shape[0]):
+        out_ref[d] = total
+
+
+def spread_sum(pieces, copies, after):
+    vmem = pl.BlockSpec(memory_space=pltpu.VMEM)
+    return pl.pallas_call(
+        spread_kernel,
+        in_specs=[pl.BlockSpec(memory_space=pl.ANY), vmem],
+        out_specs=vmem,
+        out_shape=jax.ShapeDtypeStruct((copies,) + pieces.shape[1:], jnp.bfloat16),
+        compiler_params=pltpu.CompilerParams(vmem_limit_bytes=16 * 1024 * 1024),
+    )(after, pieces)
+
+
+def scatter_sums(parts, up, down, moving, n_dp):
     n, wide = parts.shape[1:]
     z_me = lax.axis_index("z").reshape(1)
     vmem, smem = pl.BlockSpec(memory_space=pltpu.VMEM), pl.BlockSpec(memory_space=pltpu.SMEM)
     params = pltpu.CompilerParams(vmem_limit_bytes=16 * 1024 * 1024)
+    anywhere = pl.BlockSpec(memory_space=pl.ANY)
+    moving = lax.all_to_all(moving, TENSOR, 0, 0, tiled=True)
+    tails = z_me
     for k in range(N_Z // 2 - 1, -1, -1):
         up = lax.ppermute(up, "z", ring(N_Z, 1))
         down = lax.ppermute(down, "z", ring(N_Z, -1))
         if k:
             up, down = pl.pallas_call(
                 functools.partial(hop_kernel, k),
-                in_specs=[smem, vmem, vmem, vmem],
+                in_specs=[smem, anywhere, vmem, vmem, vmem],
                 out_specs=[vmem] * 2,
                 out_shape=[jax.ShapeDtypeStruct((n, wide), jnp.bfloat16)] * 2,
                 compiler_params=params,
-            )(z_me, up, down, parts)
-    at = jnp.stack([lax.axis_index("z"), lax.axis_index("yh")])
-    sent, held = pl.pallas_call(
+            )(z_me, moving if k == N_Z // 2 - 2 else z_me, up, down, parts)
+        if k == N_Z // 2 - 1:
+            moving = spread_sum(moving, n_dp, up)
+            tails = lax.all_to_all(moving, DP, 0, 0, tiled=True)
+    parts = pl.pallas_call(
         end_kernel,
-        in_specs=[smem, vmem, vmem, vmem],
-        out_specs=[vmem] * 2,
-        out_shape=[
-            jax.ShapeDtypeStruct((n, wide // 2), jnp.bfloat16),
-            jax.ShapeDtypeStruct((n, wide // 2), jnp.float32),
-        ],
-        scratch_shapes=[pltpu.VMEM((n, wide), jnp.float32)],
+        in_specs=[smem, anywhere, vmem, vmem, vmem],
+        out_specs=vmem,
+        out_shape=jax.ShapeDtypeStruct((N_Y, n, wide // N_Y), jnp.bfloat16),
         compiler_params=params,
-    )(at, up, down, parts)
-    width = wide // N_Y
-    got = lax.ppermute(sent, "yh", [(i, i ^ 1) for i in range(N_Y)])
-    held = held + got.astype(jnp.float32)
-    got = lax.ppermute(
-        held[:, width:].astype(jnp.bfloat16), "yh", [(i, i ^ 2) for i in range(N_Y)]
-    )
-    return (held[:, :width] + got.astype(jnp.float32)).astype(jnp.bfloat16)
-
-
-def product_kernel(transposed, z_ref, *refs):
+    )(z_me, tails, up, down, parts)
+    return sum_pieces(lax.all_to_all(parts, "yh", 0, 0, tiled=True)), tails
+
+
+def product_kernel(transposed, z_ref, after_ref, *refs):
     *piece_refs, w_ref, out_ref = refs
     depth = piece_refs[0].shape[1]
 
@@ -247,18 +252,18 @@
     out_ref[...] = total.astype(out_ref.dtype)
 
 
-def product(pieces, weight, transposed, dtype):
+def product(pieces, weight, transposed, dtype, after):
     rows = pieces[0].shape[0]
     columns = weight.shape[0] if transposed else weight.shape[1]
     z_me = lax.axis_index("z").reshape(1)
     return pl.pallas_call(
         functools.partial(product_kernel, transposed),
-        in_specs=[pl.BlockSpec(memory_space=pltpu.SMEM)]
+        in_specs=[pl.BlockSpec(memory_space=pltpu.SMEM), pl.BlockSpec(memory_space=pl.ANY)]
         + [pl.BlockSpec(memory_space=pltpu.VMEM)] * (len(pieces) + 1),
         out_specs=pl.BlockSpec(memory_space=pltpu.VMEM),
         out_shape=jax.ShapeDtypeStruct((rows, columns), dtype),
         compiler_params=pltpu.CompilerParams(vmem_limit_bytes=24 * 1024 * 1024),
-    )(z_me, *pieces, weight)
+    )(z_me, after, *pieces, weight)
 
 
 def shards(activations, w_query, w_keyval, w_out, targets, segments):
@@ -278,23 +283,21 @@
     half = SEQ // 2
     pieces.append(lax.ppermute(up[:half], "z", ring(N_Z, 1)))
     pieces.append(lax.ppermute(down[half:], "z", ring(N_Z, -1)))
-    keyval = product(pieces, w_keyval.T, True, jnp.bfloat16)
-    key, value = move_keyval(keyval)
-    query = product(pieces, w_query, False, jnp.float32)
+    keyval = product(pieces, w_keyval.T, True, jnp.bfloat16, lax.axis_index("z").reshape(1))
+    key, value, whole = move_keyval(keyval)
+    query = product(pieces, w_query, False, jnp.float32, whole)
 
     query_rot = rotate(query.reshape(SEQ, 2, HD), cosine, sine).astype(jnp.bfloat16)
     key_rot = rotate(key.astype(jnp.float32), cosine, sine).astype(jnp.bfloat16)
     attended = attend(query_rot.reshape(SEQ, 1, 2, HD), key_rot, value, visible)
 
     kept, up, down, moving = output_partials(attended, w_out)
-    moving = sum_pieces(lax.all_to_all(moving, TENSOR, 0, 0, tiled=True))
-    kept = scatter_sum_kept(kept, up, down)
+    kept, tails = scatter_sums(kept, up, down, moving, targets.shape[0] // MOVE)
 
     slots = lax.iota(jnp.int32, RECV)
     wanted = targets - block * RECV
     select = (slots[:, None] == wanted[None, :]).astype(jnp.bfloat16)
-    tails = jnp.broadcast_to(moving[None], (targets.shape[0] // MOVE,) + moving.shape)
-    tails = lax.all_to_all(tails, DP, 0, 0, tiled=True).reshape(targets.shape[0], -1)
+    tails = tails.reshape(targets.shape[0], -1)
     arrived = jnp.dot(select, tails, preferred_element_type=jnp.float32).astype(jnp.bfloat16)
     return jnp.concatenate([kept, arrived], axis=0)
 

time: 182 us -> 179 us (0.984)
  starting transfers between devices: 105 us -> 99.8 us
    all_to_all x2 -> x3, waiting for transfers between devices: 0.01 us -> 10.6 us  [the longest x1 8.83 us: scatter_sums(): return (sum_pieces(lax.all_to_all(parts, 'yh', 0, 0, tiled=True)), tails)]
    ppermute x10 -> x8, starting transfers between devices: 39 us -> 28.7 us  [the longest x4 15.7 us: scatter_sums(): down = lax.ppermute(down, 'z', ring(N_Z, -1))]
    ppermute x10 -> x8, waiting for transfers between devices: 24.1 us -> 17.7 us  [the longest x4 10.1 us: scatter_sums(): down = lax.ppermute(down, 'z', ring(N_Z, -1))]
    all_to_all x2 -> x3, starting transfers between devices: 15.9 us -> 20.5 us  [the longest x1 8.08 us: scatter_sums(): moving = lax.all_to_all(moving, TENSOR, 0, 0, tiled=True)]
    ppermute x1, waiting for transfers between devices: 6.82 us -> 3.75 us  [move_keyval(): crossed = lax.ppermute(whole, TENSOR, routes(1))]
  transfers between devices with their start and end apart: 23 -> 22, of which waited for: 15 -> 17; matrix products, arithmetic and copies ran while one was open for 2% -> 1% of each run, Pallas kernels for 1% -> 1%
where the time goes in v7:
time: 179 us; the launch traced here: 178 us
  starting transfers between devices  99.8 us (56%)
  waiting for transfers between devices  45.2 us (25%)
  blocking collectives  17.6 us (10%)
  Pallas kernels  7.33 us (4%)
  local copies, waits for them, and re-layouts  4.5 us (3%)
  other arithmetic  2.53 us (1%)
    ppermute x3, starting transfers between devices, shards(): down = lax.ppermute(down, 'z', ring(N_Z, -1))  24.7 us
    all_gather x1, blocking collectives, shards(): own = lax.all_gather(activations, 'yh', axis=1, tiled=True)  17.6 us
    ppermute x4, starting transfers between devices, scatter_sums(): down = lax.ppermute(down, 'z', ring(N_Z, -1))  15.7 us
    ppermute x4, starting transfers between devices, scatter_sums(): up = lax.ppermute(up, 'z', ring(N_Z, 1))  13 us
    ppermute x4, waiting for transfers between devices, scatter_sums(): down = lax.ppermute(down, 'z', ring(N_Z, -1))  10.1 us
    ppermute x3, starting transfers between devices, shards(): up = lax.ppermute(up, 'z', ring(N_Z, 1))  9 us
    all_to_all x1, waiting for transfers between devices, scatter_sums(): return (sum_pieces(lax.all_to_all(parts, 'yh', 0, 0, tiled=True)), tails)  8.83 us
    all_to_all x1, starting transfers between devices, scatter_sums(): moving = lax.all_to_all(moving, TENSOR, 0, 0, tiled=True)  8.08 us
  transfers between devices with their start and end apart: 22, of which 17 were waited for; matrix products, arithmetic and copies ran while one was open for 1% of the time, Pallas kernels for 1%

profile of v7, /device:TPU:2, one launch (start us, length us, event | category | flops | bytes accessed | tf_op | source)
XLA Modules:
  0.0 178.0 jit_solution(12977204286238209152)
XLA Ops:
  0.0 17.6 %all_gather.3.refs_0_ = bf16[128,1024]{1,0:T(8,128)(2,1)S(1)} all-gather(bf16[128,256]{1,0:T(8,128)(2,1)} %param.6), channel_id=1, replica_groups=mesh['x'=8,'yl'=2,'core'=2,'z'=8,'yh'=4] {'yh'}, dimensions={1}, use_global_device_ids=true | all-gather | bytes 327680 | tf_op jit(solution)/shard_map/all_gather | solution.py:276
  17.6 5.2 %collective-permute-start = (bf16[128,1024]{1,0:T(8,128)(2,1)S(1)}, bf16[128,1024]{1,0:T(8,128)(2,1)S(1)}, u32[]{:S(2)}, u32[]{:S(2)}) collective-permute-start(bf16[128,1024]{1,0:T(8,128)(2,1)S(1)} %all_gather.3.refs_0_), channel_id=1, source_target_pairs={{0,4},{4,8},{8,12},{12,16},{16,20},{20,24},{24,28},{28,0},{1,5},{5... | collective-permute-start | bytes 786440 | tf_op jit(solution)/shard_map/ppermute | solution.py:280
  22.7 14.4 %collective-permute-start.1 = (bf16[128,1024]{1,0:T(8,128)(2,1)S(1)}, bf16[128,1024]{1,0:T(8,128)(2,1)S(1)}, u32[]{:S(2)}, u32[]{:S(2)}) collective-permute-start(bf16[128,1024]{1,0:T(8,128)(2,1)S(1)} %all_gather.3.refs_0_), channel_id=1, source_target_pairs={{0,28},{4,0},{8,4},{12,8},{16,12},{20,16},{24,20},{28,24},{1,29},{... | collective-permute-start | bytes 786440 | tf_op jit(solution)/shard_map/ppermute | solution.py:281
  37.2 2.4 %collective-permute-done.refs_1_ = bf16[128,1024]{1,0:T(8,128)(2,1)S(1)} collective-permute-done((bf16[128,1024]{1,0:T(8,128)(2,1)S(1)}, bf16[128,1024]{1,0:T(8,128)(2,1)S(1)}, u32[]{:S(2)}, u32[]{:S(2)}) %collective-permute-start) | collective-permute-done | bytes 262176 | tf_op jit(solution)/shard_map/ppermute | solution.py:280
  39.6 1.9 %collective-permute-start.2 = (bf16[128,1024]{1,0:T(8,128)(2,1)S(1)}, bf16[128,1024]{1,0:T(8,128)(2,1)S(1)}, u32[]{:S(2)}, u32[]{:S(2)}) collective-permute-start(bf16[128,1024]{1,0:T(8,128)(2,1)S(1)} %collective-permute-done.refs_1_), channel_id=1, source_target_pairs={{0,4},{4,8},{8,12},{12,16},{16,20},{20,24},{24,28},{28,0},{1,5},{5... | collective-permute-start | bytes 786440 | tf_op jit(solution)/shard_map/ppermute | solution.py:280
  41.5 5.1 %collective-permute-start.3 = (bf16[128,1024]{1,0:T(8,128)(2,1)S(1)}, bf16[128,1024]{1,0:T(8,128)(2,1)S(1)}, u32[]{:S(2)}, u32[]{:S(2)}) collective-permute-start(bf16[128,1024]{1,0:T(8,128)(2,1)S(1)} %collective-permute-done.1.refs_2_), channel_id=1, source_target_pairs={{0,28},{4,0},{8,4},{12,8},{16,12},{20,16},{24,20},{28,24},{1,29},{... | collective-permute-start | bytes 786440 | tf_op jit(solution)/shard_map/ppermute | solution.py:281
  46.6 0.7 slice.23
  47.3 0.8 fusion.23
  48.1 0.9 collective-permute-done.2.refs_3_
  49.0 1.9 %collective-permute-start.4 = (bf16[128,1024]{1,0:T(8,128)(2,1)S(1)}, bf16[128,1024]{1,0:T(8,128)(2,1)S(1)}, u32[]{:S(2)}, u32[]{:S(2)}) collective-permute-start(bf16[128,1024]{1,0:T(8,128)(2,1)S(1)} %collective-permute-done.2.refs_3_), channel_id=1, source_target_pairs={{0,4},{4,8},{8,12},{12,16},{16,20},{20,24},{24,28},{28,0},{1,5},{5... | collective-permute-start | bytes 786440 | tf_op jit(solution)/shard_map/ppermute | solution.py:280
  51.0 5.1 %collective-permute-start.5 = (bf16[128,1024]{1,0:T(8,128)(2,1)S(1)}, bf16[128,1024]{1,0:T(8,128)(2,1)S(1)}, u32[]{:S(2)}, u32[]{:S(2)}) collective-permute-start(bf16[128,1024]{1,0:T(8,128)(2,1)S(1)} %collective-permute-done.3.refs_4_), channel_id=1, source_target_pairs={{0,28},{4,0},{8,4},{12,8},{16,12},{20,16},{24,20},{28,24},{1,29},{... | collective-permute-start | bytes 786440 | tf_op jit(solution)/shard_map/ppermute | solution.py:281
  56.3 2.9 %collective-permute-done.4.refs_5_ = bf16[128,1024]{1,0:T(8,128)(2,1)S(1)} collective-permute-done((bf16[128,1024]{1,0:T(8,128)(2,1)S(1)}, bf16[128,1024]{1,0:T(8,128)(2,1)S(1)}, u32[]{:S(2)}, u32[]{:S(2)}) %collective-permute-start.4) | collective-permute-done | bytes 262176 | tf_op jit(solution)/shard_map/ppermute | solution.py:280
  59.2 1.9 %collective-permute-start.6 = (bf16[64,1024]{1,0:T(8,128)(2,1)S(1)}, bf16[64,1024]{1,0:T(8,128)(2,1)S(1)}, u32[]{:S(2)}, u32[]{:S(2)}) collective-permute-start(bf16[64,1024]{1,0:T(8,128)(2,1)S(1)} %slice.28), channel_id=1, source_target_pairs={{0,4},{4,8},{8,12},{12,16},{16,20},{20,24},{24,28},{28,0},{1,5},{5... | collective-permute-start | bytes 393224 | tf_op jit(solution)/shard_map/ppermute | solution.py:284
  61.1 5.4 %collective-permute-start.7 = (bf16[64,1024]{1,0:T(8,128)(2,1)S(1)}, bf16[64,1024]{1,0:T(8,128)(2,1)S(1)}, u32[]{:S(2)}, u32[]{:S(2)}) collective-permute-start(bf16[64,1024]{1,0:T(8,128)(2,1)S(1)} %slice.29), channel_id=1, source_target_pairs={{0,28},{4,0},{8,4},{12,8},{16,12},{20,16},{24,20},{28,24},{1,29},{... | collective-permute-start | bytes 393224 | tf_op jit(solution)/shard_map/ppermute | solution.py:285
  67.2 1.8 collective-permute-done.7.refs_8_
  69.0 1.2 copy-done.1
  70.2 0.7 shard_map.64
  70.9 1.9 %collective-permute-start.8 = (bf16[128,64]{1,0:T(8,128)(2,1)S(1)}, bf16[128,64]{1,0:T(8,128)(2,1)S(1)}, u32[]{:S(2)}, u32[]{:S(2)}) collective-permute-start(bf16[128,64]{1,0:T(8,128)(2,1)S(1)} %shard_map.64), channel_id=1, source_target_pairs={{0,1},{1,0},{2,3},{3,2},{4,5},{5,4},{6,7},{7,6},{8,9},{9,8},{10,11... | collective-permute-start | bytes 49160 | tf_op jit(solution)/shard_map/ppermute | solution.py:76
  73.0 4.7 %collective-permute-done.8 = bf16[128,64]{1,0:T(8,128)(2,1)S(1)} collective-permute-done((bf16[128,64]{1,0:T(8,128)(2,1)S(1)}, bf16[128,64]{1,0:T(8,128)(2,1)S(1)}, u32[]{:S(2)}, u32[]{:S(2)}) %collective-permute-start.8) | collective-permute-done | bytes 16416 | tf_op jit(solution)/shard_map/ppermute | solution.py:76
  77.7 0.7 collective-permute-start.10
  78.4 7.1 %collective-permute-start.9 = (bf16[128,128]{1,0:T(8,128)(2,1)S(1)}, bf16[128,128]{1,0:T(8,128)(2,1)S(1)}, u32[]{:S(2)}, u32[]{:S(2)}) collective-permute-start(bf16[128,128]{1,0:T(8,128)(2,1)S(1)} %pad_maximum_fusion.1.after_ref), channel_id=1, source_target_pairs={{0,2},{1,3},{2,6},{3,7},{4,10},{5,11},{6,14},{7,15},{8,18},{9,19},... | collective-permute-start | bytes 98312 | tf_op jit(solution)/shard_map/ppermute | solution.py:89
  85.5 2.2 %copy-done = bf16[8192,256]{1,0:T(8,128)(2,1)S(1)} copy-done((bf16[8192,256]{1,0:T(8,128)(2,1)S(1)}, bf16[8192,256]{1,0:T(8,128)(2,1)}, u32[]{:S(2)}) %copy-start) | copy-done | bytes 4194328
  87.7 0.9 shard_map.65
  88.9 3.8 %collective-permute-done.9 = bf16[128,128]{1,0:T(8,128)(2,1)S(1)} collective-permute-done((bf16[128,128]{1,0:T(8,128)(2,1)S(1)}, bf16[128,128]{1,0:T(8,128)(2,1)S(1)}, u32[]{:S(2)}, u32[]{:S(2)}) %collective-permute-start.9) | collective-permute-done | bytes 32800 | tf_op jit(solution)/shard_map/ppermute | solution.py:89
  93.7 3.8 %shard_map.66 = (bf16[8,96,1024]{2,1,0:T(8,128)(2,1)S(1)}, bf16[48,1024]{1,0:T(8,128)(2,1)S(1)}, bf16[48,1024]{1,0:T(8,128)(2,1)S(1)}, bf16[32,32,256]{2,1,0:T(8,128)(2,1)}) custom-call(s32[1]{0:T(128)} %bitcast.z_ref.after_ref, bf16[128,256]{1,0:T(8,128)(2,1)S(1)} %copy.15.attended_ref, bf16[256,8192]{1,0:T(8,128)(2,1)} %w_ref.1), custom_call_target="tpu_custom_call" | custom-call | tf_op jit(solution)/shard_map/pallas_call | solution.py:128
  97.5 8.1 %all-to-all-start = ((bf16[32,32,256]{2,1,0:T(8,128)(2,1)}), bf16[32,32,256]{2,1,0:T(8,128)(2,1)S(1)}, u32[]{:S(2)}, u32[]{:S(2)}) async-start(bf16[32,32,256]{2,1,0:T(8,128)(2,1)} %get-tuple-element.19), calls=%async_computation | async-start | bytes 1048576 | tf_op jit(solution)/shard_map/all_to_all | solution.py:204
  105.6 3.7 %collective-permute-start.11 = (bf16[48,1024]{1,0:T(8,128)(2,1)S(1)}, bf16[48,1024]{1,0:T(8,128)(2,1)S(1)}, u32[]{:S(2)}, u32[]{:S(2)}) collective-permute-start(bf16[48,1024]{1,0:T(8,128)(2,1)S(1)} %get-tuple-element.15), channel_id=1, source_target_pairs={{0,4},{4,8},{8,12},{12,16},{16,20},{20,24},{24,28},{28,0},{1,5},{5... | collective-permute-start | bytes 294920 | tf_op jit(solution)/shard_map/ppermute | solution.py:207
  109.3 3.4 %collective-permute-start.12 = (bf16[48,1024]{1,0:T(8,128)(2,1)S(1)}, bf16[48,1024]{1,0:T(8,128)(2,1)S(1)}, u32[]{:S(2)}, u32[]{:S(2)}) collective-permute-start(bf16[48,1024]{1,0:T(8,128)(2,1)S(1)} %get-tuple-element.16), channel_id=1, source_target_pairs={{0,28},{4,0},{8,4},{12,8},{16,12},{20,16},{24,20},{28,24},{1,29},{... | collective-permute-start | bytes 294920 | tf_op jit(solution)/shard_map/ppermute | solution.py:208
  112.6 0.9 collective-permute-done.11.up_ref
  113.6 5.4 %collective-permute-done.12.down_ref = bf16[48,1024]{1,0:T(8,128)(2,1)S(1)} collective-permute-done((bf16[48,1024]{1,0:T(8,128)(2,1)S(1)}, bf16[48,1024]{1,0:T(8,128)(2,1)S(1)}, u32[]{:S(2)}, u32[]{:S(2)}) %collective-permute-start.12) | collective-permute-done | bytes 98336 | tf_op jit(solution)/shard_map/ppermute | solution.py:208
  119.1 1.8 %all-to-all-done.pieces_ref = bf16[32,32,256]{2,1,0:T(8,128)(2,1)S(1)} async-done(((bf16[32,32,256]{2,1,0:T(8,128)(2,1)}), bf16[32,32,256]{2,1,0:T(8,128)(2,1)S(1)}, u32[]{:S(2)}, u32[]{:S(2)}) %all-to-all-start) | async-done | bytes 524320 | tf_op jit(solution)/shard_map/all_to_all | solution.py:204
  120.8 0.9 shard_map.68.after_ref
  121.8 7.6 %all-to-all-start.1 = ((bf16[32,32,256]{2,1,0:T(8,128)(2,1)}), bf16[32,32,256]{2,1,0:T(8,128)(2,1)S(1)}, u32[]{:S(2)}, u32[]{:S(2)}) async-start(bf16[32,32,256]{2,1,0:T(8,128)(2,1)} %shard_map.68.after_ref), calls=%async_computation.1 | async-start | bytes 1048576 | tf_op jit(solution)/shard_map/all_to_all | solution.py:219
  129.4 3.2 %collective-permute-start.13 = (bf16[96,1024]{1,0:T(8,128)(2,1)S(1)}, bf16[96,1024]{1,0:T(8,128)(2,1)S(1)}, u32[]{:S(2)}, u32[]{:S(2)}) collective-permute-start(bf16[96,1024]{1,0:T(8,128)(2,1)S(1)} %get-tuple-element.18.after_ref), channel_id=1, source_target_pairs={{0,4},{4,8},{8,12},{12,16},{16,20},{20,24},{24,28},{28,0},{1,5},{5... | collective-permute-start | bytes 589832 | tf_op jit(solution)/shard_map/ppermute | solution.py:207
  132.6 3.8 %collective-permute-start.14 = (bf16[96,1024]{1,0:T(8,128)(2,1)S(1)}, bf16[96,1024]{1,0:T(8,128)(2,1)S(1)}, u32[]{:S(2)}, u32[]{:S(2)}) collective-permute-start(bf16[96,1024]{1,0:T(8,128)(2,1)S(1)} %get-tuple-element.20), channel_id=1, source_target_pairs={{0,28},{4,0},{8,4},{12,8},{16,12},{20,16},{24,20},{28,24},{1,29},{... | collective-permute-start | bytes 589832 | tf_op jit(solution)/shard_map/ppermute | solution.py:208
  136.4 3.0 %collective-permute-done.13.up_ref = bf16[96,1024]{1,0:T(8,128)(2,1)S(1)} collective-permute-done((bf16[96,1024]{1,0:T(8,128)(2,1)S(1)}, bf16[96,1024]{1,0:T(8,128)(2,1)S(1)}, u32[]{:S(2)}, u32[]{:S(2)}) %collective-permute-start.13) | collective-permute-done | bytes 196640 | tf_op jit(solution)/shard_map/ppermute | solution.py:207
  139.4 1.7 collective-permute-done.14.down_ref
  141.3 2.7 %collective-permute-start.15 = (bf16[96,1024]{1,0:T(8,128)(2,1)S(1)}, bf16[96,1024]{1,0:T(8,128)(2,1)S(1)}, u32[]{:S(2)}, u32[]{:S(2)}) collective-permute-start(bf16[96,1024]{1,0:T(8,128)(2,1)S(1)} %get-tuple-element.21), channel_id=1, source_target_pairs={{0,4},{4,8},{8,12},{12,16},{16,20},{20,24},{24,28},{28,0},{1,5},{5... | collective-permute-start | bytes 589832 | tf_op jit(solution)/shard_map/ppermute | solution.py:207
  143.9 4.4 %collective-permute-start.16 = (bf16[96,1024]{1,0:T(8,128)(2,1)S(1)}, bf16[96,1024]{1,0:T(8,128)(2,1)S(1)}, u32[]{:S(2)}, u32[]{:S(2)}) collective-permute-start(bf16[96,1024]{1,0:T(8,128)(2,1)S(1)} %get-tuple-element.22), channel_id=1, source_target_pairs={{0,28},{4,0},{8,4},{12,8},{16,12},{20,16},{24,20},{28,24},{1,29},{... | collective-permute-start | bytes 589832 | tf_op jit(solution)/shard_map/ppermute | solution.py:208
  148.3 2.0 %collective-permute-done.15.up_ref = bf16[96,1024]{1,0:T(8,128)(2,1)S(1)} collective-permute-done((bf16[96,1024]{1,0:T(8,128)(2,1)S(1)}, bf16[96,1024]{1,0:T(8,128)(2,1)S(1)}, u32[]{:S(2)}, u32[]{:S(2)}) %collective-permute-start.15) | collective-permute-done | bytes 196640 | tf_op jit(solution)/shard_map/ppermute | solution.py:207
  150.4 1.2 collective-permute-done.16.down_ref
  151.7 3.4 %collective-permute-start.17 = (bf16[96,1024]{1,0:T(8,128)(2,1)S(1)}, bf16[96,1024]{1,0:T(8,128)(2,1)S(1)}, u32[]{:S(2)}, u32[]{:S(2)}) collective-permute-start(bf16[96,1024]{1,0:T(8,128)(2,1)S(1)} %get-tuple-element.23), channel_id=1, source_target_pairs={{0,4},{4,8},{8,12},{12,16},{16,20},{20,24},{24,28},{28,0},{1,5},{5... | collective-permute-start | bytes 589832 | tf_op jit(solution)/shard_map/ppermute | solution.py:207
  155.1 4.1 %collective-permute-start.18 = (bf16[96,1024]{1,0:T(8,128)(2,1)S(1)}, bf16[96,1024]{1,0:T(8,128)(2,1)S(1)}, u32[]{:S(2)}, u32[]{:S(2)}) collective-permute-start(bf16[96,1024]{1,0:T(8,128)(2,1)S(1)} %get-tuple-element.24), channel_id=1, source_target_pairs={{0,28},{4,0},{8,4},{12,8},{16,12},{20,16},{24,20},{28,24},{1,29},{... | collective-permute-start | bytes 589832 | tf_op jit(solution)/shard_map/ppermute | solution.py:208
  159.2 1.7 collective-permute-done.17.up_ref
  160.9 1.7 collective-permute-done.18.down_ref
  162.6 0.8 shard_map.71
  163.4 4.9 %all-to-all-start.2 = ((bf16[4,96,256]{2,1,0:T(8,128)(2,1)}), bf16[4,96,256]{2,1,0:T(8,128)(2,1)S(1)}, u32[]{:S(2)}, u32[]{:S(2)}) async-start(bf16[4,96,256]{2,1,0:T(8,128)(2,1)} %shard_map.71), calls=%async_computation.2 | async-start | bytes 393216 | tf_op jit(solution)/shard_map/all_to_all | solution.py:227
  168.5 8.8 %all-to-all-done.2 = bf16[4,96,256]{2,1,0:T(8,128)(2,1)S(1)} async-done(((bf16[4,96,256]{2,1,0:T(8,128)(2,1)}), bf16[4,96,256]{2,1,0:T(8,128)(2,1)S(1)}, u32[]{:S(2)}, u32[]{:S(2)}) %all-to-all-start.2) | async-done | bytes 196640 | tf_op jit(solution)/shard_map/all_to_all | solution.py:227
  (36 shorter events, 3.5 us)
Async XLA Ops:
  17.6 22.0 %collective-permute-start = (bf16[128,1024]{1,0:T(8,128)(2,1)S(1)}, bf16[128,1024]{1,0:T(8,128)(2,1)S(1)}, u32[]{:S(2)}, u32[]{:S(2)}) collective-permute-start(bf16[128,1024]{1,0:T(8,128)(2,1)S(1)} %all_gather.3.refs_0_), channel_id=1, source_target_pairs={{0,4},{4,8},{8,12},{12,16},{16,20},{20,24},{24,28},{28,0},{1,5},{5... | collective-permute-start | bytes 786440 | tf_op jit(solution)/shard_map/ppermute | solution.py:280
  22.7 18.7 %collective-permute-start.1 = (bf16[128,1024]{1,0:T(8,128)(2,1)S(1)}, bf16[128,1024]{1,0:T(8,128)(2,1)S(1)}, u32[]{:S(2)}, u32[]{:S(2)}) collective-permute-start(bf16[128,1024]{1,0:T(8,128)(2,1)S(1)} %all_gather.3.refs_0_), channel_id=1, source_target_pairs={{0,28},{4,0},{8,4},{12,8},{16,12},{20,16},{24,20},{28,24},{1,29},{... | collective-permute-start | bytes 786440 | tf_op jit(solution)/shard_map/ppermute | solution.py:281
  39.6 9.5 %collective-permute-start.2 = (bf16[128,1024]{1,0:T(8,128)(2,1)S(1)}, bf16[128,1024]{1,0:T(8,128)(2,1)S(1)}, u32[]{:S(2)}, u32[]{:S(2)}) collective-permute-start(bf16[128,1024]{1,0:T(8,128)(2,1)S(1)} %collective-permute-done.refs_1_), channel_id=1, source_target_pairs={{0,4},{4,8},{8,12},{12,16},{16,20},{20,24},{24,28},{28,0},{1,5},{5... | collective-permute-start | bytes 786440 | tf_op jit(solution)/shard_map/ppermute | solution.py:280
  41.5 9.5 %collective-permute-start.3 = (bf16[128,1024]{1,0:T(8,128)(2,1)S(1)}, bf16[128,1024]{1,0:T(8,128)(2,1)S(1)}, u32[]{:S(2)}, u32[]{:S(2)}) collective-permute-start(bf16[128,1024]{1,0:T(8,128)(2,1)S(1)} %collective-permute-done.1.refs_2_), channel_id=1, source_target_pairs={{0,28},{4,0},{8,4},{12,8},{16,12},{20,16},{24,20},{28,24},{1,29},{... | collective-permute-start | bytes 786440 | tf_op jit(solution)/shard_map/ppermute | solution.py:281
  49.0 10.1 %collective-permute-start.4 = (bf16[128,1024]{1,0:T(8,128)(2,1)S(1)}, bf16[128,1024]{1,0:T(8,128)(2,1)S(1)}, u32[]{:S(2)}, u32[]{:S(2)}) collective-permute-start(bf16[128,1024]{1,0:T(8,128)(2,1)S(1)} %collective-permute-done.2.refs_3_), channel_id=1, source_target_pairs={{0,4},{4,8},{8,12},{12,16},{16,20},{20,24},{24,28},{28,0},{1,5},{5... | collective-permute-start | bytes 786440 | tf_op jit(solution)/shard_map/ppermute | solution.py:280
  51.0 10.1 %collective-permute-start.5 = (bf16[128,1024]{1,0:T(8,128)(2,1)S(1)}, bf16[128,1024]{1,0:T(8,128)(2,1)S(1)}, u32[]{:S(2)}, u32[]{:S(2)}) collective-permute-start(bf16[128,1024]{1,0:T(8,128)(2,1)S(1)} %collective-permute-done.3.refs_4_), channel_id=1, source_target_pairs={{0,28},{4,0},{8,4},{12,8},{16,12},{20,16},{24,20},{28,24},{1,29},{... | collective-permute-start | bytes 786440 | tf_op jit(solution)/shard_map/ppermute | solution.py:281
  59.2 8.1 %collective-permute-start.6 = (bf16[64,1024]{1,0:T(8,128)(2,1)S(1)}, bf16[64,1024]{1,0:T(8,128)(2,1)S(1)}, u32[]{:S(2)}, u32[]{:S(2)}) collective-permute-start(bf16[64,1024]{1,0:T(8,128)(2,1)S(1)} %slice.28), channel_id=1, source_target_pairs={{0,4},{4,8},{8,12},{12,16},{16,20},{20,24},{24,28},{28,0},{1,5},{5... | collective-permute-start | bytes 393224 | tf_op jit(solution)/shard_map/ppermute | solution.py:284
  61.1 7.9 %collective-permute-start.7 = (bf16[64,1024]{1,0:T(8,128)(2,1)S(1)}, bf16[64,1024]{1,0:T(8,128)(2,1)S(1)}, u32[]{:S(2)}, u32[]{:S(2)}) collective-permute-start(bf16[64,1024]{1,0:T(8,128)(2,1)S(1)} %slice.29), channel_id=1, source_target_pairs={{0,28},{4,0},{8,4},{12,8},{16,12},{20,16},{24,20},{28,24},{1,29},{... | collective-permute-start | bytes 393224 | tf_op jit(solution)/shard_map/ppermute | solution.py:285
  69.0 1.2 copy-start.1
  70.9 6.7 %collective-permute-start.8 = (bf16[128,64]{1,0:T(8,128)(2,1)S(1)}, bf16[128,64]{1,0:T(8,128)(2,1)S(1)}, u32[]{:S(2)}, u32[]{:S(2)}) collective-permute-start(bf16[128,64]{1,0:T(8,128)(2,1)S(1)} %shard_map.64), channel_id=1, source_target_pairs={{0,1},{1,0},{2,3},{3,2},{4,5},{5,4},{6,7},{7,6},{8,9},{9,8},{10,11... | collective-permute-start | bytes 49160 | tf_op jit(solution)/shard_map/ppermute | solution.py:76
  77.7 11.2 %collective-permute-start.10 = (bf16[128,128]{1,0:T(8,128)(2,1)S(1)}, bf16[128,128]{1,0:T(8,128)(2,1)S(1)}, u32[]{:S(2)}, u32[]{:S(2)}) collective-permute-start(bf16[128,128]{1,0:T(8,128)(2,1)S(1)} %pad_maximum_fusion.1.after_ref), channel_id=1, source_target_pairs={{0,0},{1,1},{2,4},{3,5},{4,8},{5,9},{6,12},{7,13},{8,16},{9,17},{1... | collective-permute-start | bytes 98312 | tf_op jit(solution)/shard_map/ppermute | solution.py:88
  78.4 14.3 %collective-permute-start.9 = (bf16[128,128]{1,0:T(8,128)(2,1)S(1)}, bf16[128,128]{1,0:T(8,128)(2,1)S(1)}, u32[]{:S(2)}, u32[]{:S(2)}) collective-permute-start(bf16[128,128]{1,0:T(8,128)(2,1)S(1)} %pad_maximum_fusion.1.after_ref), channel_id=1, source_target_pairs={{0,2},{1,3},{2,6},{3,7},{4,10},{5,11},{6,14},{7,15},{8,18},{9,19},... | collective-permute-start | bytes 98312 | tf_op jit(solution)/shard_map/ppermute | solution.py:89
  85.5 2.2 %copy-start = (bf16[8192,256]{1,0:T(8,128)(2,1)S(1)}, bf16[8192,256]{1,0:T(8,128)(2,1)}, u32[]{:S(2)}) copy-start(bf16[8192,256]{1,0:T(8,128)(2,1)} %refs_9_.1) | copy-start | bytes 12582916
  97.5 23.4 %all-to-all-start = ((bf16[32,32,256]{2,1,0:T(8,128)(2,1)}), bf16[32,32,256]{2,1,0:T(8,128)(2,1)S(1)}, u32[]{:S(2)}, u32[]{:S(2)}) async-start(bf16[32,32,256]{2,1,0:T(8,128)(2,1)} %get-tuple-element.19), calls=%async_computation | async-start | bytes 1048576 | tf_op jit(solution)/shard_map/all_to_all | solution.py:204
  105.6 8.0 %collective-permute-start.11 = (bf16[48,1024]{1,0:T(8,128)(2,1)S(1)}, bf16[48,1024]{1,0:T(8,128)(2,1)S(1)}, u32[]{:S(2)}, u32[]{:S(2)}) collective-permute-start(bf16[48,1024]{1,0:T(8,128)(2,1)S(1)} %get-tuple-element.15), channel_id=1, source_target_pairs={{0,4},{4,8},{8,12},{12,16},{16,20},{20,24},{24,28},{28,0},{1,5},{5... | collective-permute-start | bytes 294920 | tf_op jit(solution)/shard_map/ppermute | solution.py:207
  109.3 9.7 %collective-permute-start.12 = (bf16[48,1024]{1,0:T(8,128)(2,1)S(1)}, bf16[48,1024]{1,0:T(8,128)(2,1)S(1)}, u32[]{:S(2)}, u32[]{:S(2)}) collective-permute-start(bf16[48,1024]{1,0:T(8,128)(2,1)S(1)} %get-tuple-element.16), channel_id=1, source_target_pairs={{0,28},{4,0},{8,4},{12,8},{16,12},{20,16},{24,20},{28,24},{1,29},{... | collective-permute-start | bytes 294920 | tf_op jit(solution)/shard_map/ppermute | solution.py:208
  121.8 46.5 %copy-start.2 = (s32[1024]{0:T(1024)S(1)}, s32[1024]{0:T(1024)}, u32[]{:S(2)}) copy-start(s32[1024]{0:T(1024)} %param.10) | copy-start | bytes 12292
  121.8 40.9 %all-to-all-start.1 = ((bf16[32,32,256]{2,1,0:T(8,128)(2,1)}), bf16[32,32,256]{2,1,0:T(8,128)(2,1)S(1)}, u32[]{:S(2)}, u32[]{:S(2)}) async-start(bf16[32,32,256]{2,1,0:T(8,128)(2,1)} %shard_map.68.after_ref), calls=%async_computation.1 | async-start | bytes 1048576 | tf_op jit(solution)/shard_map/all_to_all | solution.py:219
  129.4 10.1 %collective-permute-start.13 = (bf16[96,1024]{1,0:T(8,128)(2,1)S(1)}, bf16[96,1024]{1,0:T(8,128)(2,1)S(1)}, u32[]{:S(2)}, u32[]{:S(2)}) collective-permute-start(bf16[96,1024]{1,0:T(8,128)(2,1)S(1)} %get-tuple-element.18.after_ref), channel_id=1, source_target_pairs={{0,4},{4,8},{8,12},{12,16},{16,20},{20,24},{24,28},{28,0},{1,5},{5... | collective-permute-start | bytes 589832 | tf_op jit(solution)/shard_map/ppermute | solution.py:207
  132.6 8.6 %collective-permute-start.14 = (bf16[96,1024]{1,0:T(8,128)(2,1)S(1)}, bf16[96,1024]{1,0:T(8,128)(2,1)S(1)}, u32[]{:S(2)}, u32[]{:S(2)}) collective-permute-start(bf16[96,1024]{1,0:T(8,128)(2,1)S(1)} %get-tuple-element.20), channel_id=1, source_target_pairs={{0,28},{4,0},{8,4},{12,8},{16,12},{20,16},{24,20},{28,24},{1,29},{... | collective-permute-start | bytes 589832 | tf_op jit(solution)/shard_map/ppermute | solution.py:208
  141.3 9.1 %collective-permute-start.15 = (bf16[96,1024]{1,0:T(8,128)(2,1)S(1)}, bf16[96,1024]{1,0:T(8,128)(2,1)S(1)}, u32[]{:S(2)}, u32[]{:S(2)}) collective-permute-start(bf16[96,1024]{1,0:T(8,128)(2,1)S(1)} %get-tuple-element.21), channel_id=1, source_target_pairs={{0,4},{4,8},{8,12},{12,16},{16,20},{20,24},{24,28},{28,0},{1,5},{5... | collective-permute-start | bytes 589832 | tf_op jit(solution)/shard_map/ppermute | solution.py:207
  143.9 7.6 %collective-permute-start.16 = (bf16[96,1024]{1,0:T(8,128)(2,1)S(1)}, bf16[96,1024]{1,0:T(8,128)(2,1)S(1)}, u32[]{:S(2)}, u32[]{:S(2)}) collective-permute-start(bf16[96,1024]{1,0:T(8,128)(2,1)S(1)} %get-tuple-element.22), channel_id=1, source_target_pairs={{0,28},{4,0},{8,4},{12,8},{16,12},{20,16},{24,20},{28,24},{1,29},{... | collective-permute-start | bytes 589832 | tf_op jit(solution)/shard_map/ppermute | solution.py:208
  151.7 9.2 %collective-permute-start.17 = (bf16[96,1024]{1,0:T(8,128)(2,1)S(1)}, bf16[96,1024]{1,0:T(8,128)(2,1)S(1)}, u32[]{:S(2)}, u32[]{:S(2)}) collective-permute-start(bf16[96,1024]{1,0:T(8,128)(2,1)S(1)} %get-tuple-element.23), channel_id=1, source_target_pairs={{0,4},{4,8},{8,12},{12,16},{16,20},{20,24},{24,28},{28,0},{1,5},{5... | collective-permute-start | bytes 589832 | tf_op jit(solution)/shard_map/ppermute | solution.py:207
  155.1 7.6 %collective-permute-start.18 = (bf16[96,1024]{1,0:T(8,128)(2,1)S(1)}, bf16[96,1024]{1,0:T(8,128)(2,1)S(1)}, u32[]{:S(2)}, u32[]{:S(2)}) collective-permute-start(bf16[96,1024]{1,0:T(8,128)(2,1)S(1)} %get-tuple-element.24), channel_id=1, source_target_pairs={{0,28},{4,0},{8,4},{12,8},{16,12},{20,16},{24,20},{28,24},{1,29},{... | collective-permute-start | bytes 589832 | tf_op jit(solution)/shard_map/ppermute | solution.py:208
  163.4 13.9 %all-to-all-start.2 = ((bf16[4,96,256]{2,1,0:T(8,128)(2,1)}), bf16[4,96,256]{2,1,0:T(8,128)(2,1)S(1)}, u32[]{:S(2)}, u32[]{:S(2)}) async-start(bf16[4,96,256]{2,1,0:T(8,128)(2,1)} %shard_map.71), calls=%async_computation.2 | async-start | bytes 393216 | tf_op jit(solution)/shard_map/all_to_all | solution.py:227

commit v8 on v7

--- a/solution.py
+++ b/solution.py
@@ -97,13 +97,17 @@
     return jnp.sum(pieces.astype(jnp.float32), axis=0).astype(jnp.bfloat16)
 
 
-def output_kernel(
-    z_ref, attended_ref, w_ref, kept_ref, up_ref, down_ref, tail_ref, held, sems
-):
-    wide = kept_ref.shape[2]
+def output_kernel(attended_ref, w_ref, kept_ref, tail_ref, held, rows_held, sems, out_sems):
+    wide = held.shape[2]
     width = tail_ref.shape[2]
     copies = [
         pltpu.make_async_copy(w_ref.at[:, pl.ds(z * wide, wide)], held.at[z], sems.at[z])
+        for z in range(N_Z)
+    ]
+    outs = [
+        pltpu.make_async_copy(
+            rows_held.at[z], kept_ref.at[:, pl.ds(z * wide, wide)], out_sems.at[z]
+        )
         for z in range(N_Z)
     ]
     for copy in copies:
@@ -112,119 +116,52 @@
         copies[z].wait()
         rows = jnp.dot(attended_ref[...], held[z], preferred_element_type=jnp.float32)
         rows = rows.astype(jnp.bfloat16)
-        kept_ref[z] = rows[:KEEP]
+        rows_held[z] = rows[:KEEP]
+        outs[z].start()
         for y in range(N_Y):
             tail_ref[z * N_Y + y] = rows[KEEP:, y * width : (y + 1) * width]
-    far = lax.rem(z_ref[0] + N_Z // 2, N_Z)
-    up_ref[...] = kept_ref[far, : KEEP // 2]
-    down_ref[...] = kept_ref[far, KEEP // 2 :]
+    for copy in outs:
+        copy.wait()
 
 
 def output_partials(attended, w_out):
     depth, columns = w_out.shape
     wide = columns // N_Z
     n = N_Z * N_Y
-    vmem = pl.BlockSpec(memory_space=pltpu.VMEM)
+    vmem, anywhere = pl.BlockSpec(memory_space=pltpu.VMEM), pl.BlockSpec(memory_space=pl.ANY)
     return pl.pallas_call(
         output_kernel,
-        in_specs=[
-            pl.BlockSpec(memory_space=pltpu.SMEM),
-            vmem,
-            pl.BlockSpec(memory_space=pl.ANY),
-        ],
-        out_specs=[vmem] * 4,
+        in_specs=[vmem, anywhere],
+        out_specs=[pl.BlockSpec(memory_space=pltpu.HBM), vmem],
         out_shape=[
-            jax.ShapeDtypeStruct((N_Z, KEEP, wide), jnp.bfloat16),
-            jax.ShapeDtypeStruct((KEEP // 2, wide), jnp.bfloat16),
-            jax.ShapeDtypeStruct((KEEP // 2, wide), jnp.bfloat16),
+            jax.ShapeDtypeStruct((KEEP, columns), jnp.bfloat16),
             jax.ShapeDtypeStruct((n, MOVE, columns // n), jnp.bfloat16),
         ],
         scratch_shapes=[
             pltpu.VMEM((N_Z, depth, wide), jnp.bfloat16),
+            pltpu.VMEM((N_Z, KEEP, wide), jnp.bfloat16),
+            pltpu.SemaphoreType.DMA((N_Z,)),
             pltpu.SemaphoreType.DMA((N_Z,)),
         ],
         compiler_params=pltpu.CompilerParams(vmem_limit_bytes=32 * 1024 * 1024),
-    )(
-        lax.axis_index("z").reshape(1),
-        attended,
-        pltpu.with_memory_space_constraint(w_out, pltpu.HBM),
-    )
-
-
-def hop_kernel(k, z_ref, after_ref, up_ref, down_ref, parts_ref, up_out, down_out):
-    above = parts_ref.at[lax.rem(z_ref[0] + k, N_Z)]
-    below = parts_ref.at[lax.rem(z_ref[0] + N_Z - k, N_Z)]
-    n, got = parts_ref.shape[1], up_ref.shape[0]
-
-    def add(a, b):
-        return (a.astype(jnp.float32) + b.astype(jnp.float32)).astype(jnp.bfloat16)
-
-    up_out[:got] = add(above[:got], up_ref[...])
-    down_out[n - got :] = add(below[n - got :], down_ref[...])
-    if got < n:
-        up_out[got:] = above[got:]
-        down_out[: n - got] = below[: n - got]
-
-
-def end_kernel(z_ref, after_ref, up_ref, down_ref, parts_ref, out_ref):
-    own = parts_ref.at[z_ref[0]]
-    total = (
-        own[...].astype(jnp.float32)
-        + up_ref[...].astype(jnp.float32)
-        + down_ref[...].astype(jnp.float32)
-    ).astype(jnp.bfloat16)
-    width = out_ref.shape[2]
-    for y in range(N_Y):
-        out_ref[y] = total[:, y * width : (y + 1) * width]
-
-
-def spread_kernel(after_ref, pieces_ref, out_ref):
+    )(attended, pltpu.with_memory_space_constraint(w_out, pltpu.HBM))
+
+
+def spread_kernel(pieces_ref, out_ref):
     total = jnp.sum(pieces_ref[...].astype(jnp.float32), axis=0).astype(jnp.bfloat16)
     for d in range(out_ref.shape[0]):
         out_ref[d] = total
 
 
-def spread_sum(pieces, copies, after):
+def spread_sum(pieces, copies):
     vmem = pl.BlockSpec(memory_space=pltpu.VMEM)
     return pl.pallas_call(
         spread_kernel,
-        in_specs=[pl.BlockSpec(memory_space=pl.ANY), vmem],
+        in_specs=[vmem],
         out_specs=vmem,
         out_shape=jax.ShapeDtypeStruct((copies,) + pieces.shape[1:], jnp.bfloat16),
         compiler_params=pltpu.CompilerParams(vmem_limit_bytes=16 * 1024 * 1024),
-    )(after, pieces)
-
-
-def scatter_sums(parts, up, down, moving, n_dp):
-    n, wide = parts.shape[1:]
-    z_me = lax.axis_index("z").reshape(1)
-    vmem, smem = pl.BlockSpec(memory_space=pltpu.VMEM), pl.BlockSpec(memory_space=pltpu.SMEM)
-    params = pltpu.CompilerParams(vmem_limit_bytes=16 * 1024 * 1024)
-    anywhere = pl.BlockSpec(memory_space=pl.ANY)
-    moving = lax.all_to_all(moving, TENSOR, 0, 0, tiled=True)
-    tails = z_me
-    for k in range(N_Z // 2 - 1, -1, -1):
-        up = lax.ppermute(up, "z", ring(N_Z, 1))
-        down = lax.ppermute(down, "z", ring(N_Z, -1))
-        if k:
-            up, down = pl.pallas_call(
-                functools.partial(hop_kernel, k),
-                in_specs=[smem, anywhere, vmem, vmem, vmem],
-                out_specs=[vmem] * 2,
-                out_shape=[jax.ShapeDtypeStruct((n, wide), jnp.bfloat16)] * 2,
-                compiler_params=params,
-            )(z_me, moving if k == N_Z // 2 - 2 else z_me, up, down, parts)
-        if k == N_Z // 2 - 1:
-            moving = spread_sum(moving, n_dp, up)
-            tails = lax.all_to_all(moving, DP, 0, 0, tiled=True)
-    parts = pl.pallas_call(
-        end_kernel,
-        in_specs=[smem, anywhere, vmem, vmem, vmem],
-        out_specs=vmem,
-        out_shape=jax.ShapeDtypeStruct((N_Y, n, wide // N_Y), jnp.bfloat16),
-        compiler_params=params,
-    )(z_me, tails, up, down, parts)
-    return sum_pieces(lax.all_to_all(parts, "yh", 0, 0, tiled=True)), tails
+    )(pieces)
 
 
 def product_kernel(transposed, z_ref, after_ref, *refs):
@@ -291,8 +228,13 @@
     key_rot = rotate(key.astype(jnp.float32), cosine, sine).astype(jnp.bfloat16)
     attended = attend(query_rot.reshape(SEQ, 1, 2, HD), key_rot, value, visible)
 
-    kept, up, down, moving = output_partials(attended, w_out)
-    kept, tails = scatter_sums(kept, up, down, moving, targets.shape[0] // MOVE)
+    kept, moving = output_partials(attended, w_out)
+    kept = lax.psum_scatter(kept.T, "z", scatter_dimension=0, tiled=True).T
+    moving = lax.all_to_all(moving, TENSOR, 0, 0, tiled=True)
+    moving = spread_sum(moving, targets.shape[0] // MOVE)
+    tails = lax.all_to_all(moving, DP, 0, 0, tiled=True)
+    kept = kept.reshape(KEEP, N_Y, -1).transpose(1, 0, 2)
+    kept = sum_pieces(lax.all_to_all(kept, "yh", 0, 0, tiled=True))
 
     slots = lax.iota(jnp.int32, RECV)
     wanted = targets - block * RECV

time: 179 us -> 178 us (level)
  the two profiles are of different devices: /device:TPU:2 before, /device:TPU:1 now
where the time goes in v8:
time: 178 us; the launch traced here: 177 us
  starting transfers between devices  74.1 us (42%)
  waiting for transfers between devices  37.3 us (21%)
  blocking collectives  36 us (20%)
  between operations  13.7 us (8%)
  Pallas kernels  6.28 us (4%)
  local copies, waits for them, and re-layouts  6.11 us (3%)
  other arithmetic  2.54 us (1%)
    ppermute x3, starting transfers between devices, shards(): down = lax.ppermute(down, 'z', ring(N_Z, -1))  27.1 us
    all_to_all x1, starting transfers between devices, shards(): tails = lax.all_to_all(moving, DP, 0, 0, tiled=True)  21.3 us
    all_to_all x1, blocking collectives, shards(): moving = lax.all_to_all(moving, TENSOR, 0, 0, tiled=True)  20.5 us
    all_gather x1, blocking collectives, shards(): own = lax.all_gather(activations, 'yh', axis=1, tiled=True)  15.5 us
    reduce_scatter x1, waiting for transfers between devices, shards(): kept = lax.psum_scatter(kept.T, 'z', scatter_dimension=0, tiled=True).T  8.59 us
    all_to_all x1, waiting for transfers between devices, shards(): kept = sum_pieces(lax.all_to_all(kept, 'yh', 0, 0, tiled=True))  7.92 us
    ppermute x1, starting transfers between devices, move_keyval(): crossed = lax.ppermute(whole, TENSOR, routes(1))  6.77 us
    all_to_all x1, waiting for transfers between devices, shards(): tails = lax.all_to_all(moving, DP, 0, 0, tiled=True)  6.5 us
  transfers between devices with their start and end apart: 14, of which 9 were waited for; matrix products, arithmetic and copies ran while one was open for 2% of the time, Pallas kernels for 1%

profile of v8, /device:TPU:1, one launch (start us, length us, event | category | flops | bytes accessed | tf_op | source)
XLA Modules:
  0.0 176.6 jit_solution(7297361935127235224)
XLA Ops:
  6.5 15.5 %all_gather.3.refs_0_ = bf16[128,1024]{1,0:T(8,128)(2,1)S(1)} all-gather(bf16[128,256]{1,0:T(8,128)(2,1)} %param.6), channel_id=1, replica_groups=mesh['x'=8,'yl'=2,'core'=2,'z'=8,'yh'=4] {'yh'}, dimensions={1}, use_global_device_ids=true | all-gather | bytes 327680 | tf_op jit(solution)/shard_map/all_gather | solution.py:213
  22.0 17.2 %collective-permute-start.1 = (bf16[128,1024]{1,0:T(8,128)(2,1)S(1)}, bf16[128,1024]{1,0:T(8,128)(2,1)S(1)}, u32[]{:S(2)}, u32[]{:S(2)}) collective-permute-start(bf16[128,1024]{1,0:T(8,128)(2,1)S(1)} %all_gather.3.refs_0_), channel_id=1, source_target_pairs={{0,28},{4,0},{8,4},{12,8},{16,12},{20,16},{24,20},{28,24},{1,29},{... | collective-permute-start | bytes 786440 | tf_op jit(solution)/shard_map/ppermute | solution.py:218
  39.2 1.9 %collective-permute-start = (bf16[128,1024]{1,0:T(8,128)(2,1)S(1)}, bf16[128,1024]{1,0:T(8,128)(2,1)S(1)}, u32[]{:S(2)}, u32[]{:S(2)}) collective-permute-start(bf16[128,1024]{1,0:T(8,128)(2,1)S(1)} %all_gather.3.refs_0_), channel_id=1, source_target_pairs={{0,4},{4,8},{8,12},{12,16},{16,20},{20,24},{24,28},{28,0},{1,5},{5... | collective-permute-start | bytes 786440 | tf_op jit(solution)/shard_map/ppermute | solution.py:217
  41.1 1.4 collective-permute-done.1.refs_2_
  42.5 5.0 %collective-permute-start.3 = (bf16[128,1024]{1,0:T(8,128)(2,1)S(1)}, bf16[128,1024]{1,0:T(8,128)(2,1)S(1)}, u32[]{:S(2)}, u32[]{:S(2)}) collective-permute-start(bf16[128,1024]{1,0:T(8,128)(2,1)S(1)} %collective-permute-done.1.refs_2_), channel_id=1, source_target_pairs={{0,28},{4,0},{8,4},{12,8},{16,12},{20,16},{24,20},{28,24},{1,29},{... | collective-permute-start | bytes 786440 | tf_op jit(solution)/shard_map/ppermute | solution.py:218
  47.5 1.9 %collective-permute-start.2 = (bf16[128,1024]{1,0:T(8,128)(2,1)S(1)}, bf16[128,1024]{1,0:T(8,128)(2,1)S(1)}, u32[]{:S(2)}, u32[]{:S(2)}) collective-permute-start(bf16[128,1024]{1,0:T(8,128)(2,1)S(1)} %collective-permute-done.refs_1_), channel_id=1, source_target_pairs={{0,4},{4,8},{8,12},{12,16},{16,20},{20,24},{24,28},{28,0},{1,5},{5... | collective-permute-start | bytes 786440 | tf_op jit(solution)/shard_map/ppermute | solution.py:217
  49.5 0.7 slice.23
  50.2 0.8 fusion.23
  50.9 4.9 %collective-permute-start.5 = (bf16[128,1024]{1,0:T(8,128)(2,1)S(1)}, bf16[128,1024]{1,0:T(8,128)(2,1)S(1)}, u32[]{:S(2)}, u32[]{:S(2)}) collective-permute-start(bf16[128,1024]{1,0:T(8,128)(2,1)S(1)} %collective-permute-done.3.refs_4_), channel_id=1, source_target_pairs={{0,28},{4,0},{8,4},{12,8},{16,12},{20,16},{24,20},{28,24},{1,29},{... | collective-permute-start | bytes 786440 | tf_op jit(solution)/shard_map/ppermute | solution.py:218
  55.8 0.0 collective-permute-done.2.refs_3_
  55.9 1.9 %collective-permute-start.4 = (bf16[128,1024]{1,0:T(8,128)(2,1)S(1)}, bf16[128,1024]{1,0:T(8,128)(2,1)S(1)}, u32[]{:S(2)}, u32[]{:S(2)}) collective-permute-start(bf16[128,1024]{1,0:T(8,128)(2,1)S(1)} %collective-permute-done.2.refs_3_), channel_id=1, source_target_pairs={{0,4},{4,8},{8,12},{12,16},{16,20},{20,24},{24,28},{28,0},{1,5},{5... | collective-permute-start | bytes 786440 | tf_op jit(solution)/shard_map/ppermute | solution.py:217
  57.8 0.1 pad_add_fusion
  57.9 0.1 convert_reduce_fusion
  58.0 1.2 collective-permute-done.5.refs_6_
  59.1 5.0 %collective-permute-start.7 = (bf16[64,1024]{1,0:T(8,128)(2,1)S(1)}, bf16[64,1024]{1,0:T(8,128)(2,1)S(1)}, u32[]{:S(2)}, u32[]{:S(2)}) collective-permute-start(bf16[64,1024]{1,0:T(8,128)(2,1)S(1)} %slice.29), channel_id=1, source_target_pairs={{0,28},{4,0},{8,4},{12,8},{16,12},{20,16},{24,20},{28,24},{1,29},{... | collective-permute-start | bytes 393224 | tf_op jit(solution)/shard_map/ppermute | solution.py:222
  64.2 1.9 %collective-permute-start.6 = (bf16[64,1024]{1,0:T(8,128)(2,1)S(1)}, bf16[64,1024]{1,0:T(8,128)(2,1)S(1)}, u32[]{:S(2)}, u32[]{:S(2)}) collective-permute-start(bf16[64,1024]{1,0:T(8,128)(2,1)S(1)} %slice.28), channel_id=1, source_target_pairs={{0,4},{4,8},{8,12},{12,16},{16,20},{20,24},{24,28},{28,0},{1,5},{5... | collective-permute-start | bytes 393224 | tf_op jit(solution)/shard_map/ppermute | solution.py:221
  66.1 0.3 multiply_cosine_fusion
  66.5 0.3 collective-permute-done.7.refs_8_
  66.7 5.3 %collective-permute-done.6.refs_7_ = bf16[64,1024]{1,0:T(8,128)(2,1)S(1)} collective-permute-done((bf16[64,1024]{1,0:T(8,128)(2,1)S(1)}, bf16[64,1024]{1,0:T(8,128)(2,1)S(1)}, u32[]{:S(2)}, u32[]{:S(2)}) %collective-permute-start.6) | collective-permute-done | bytes 131104 | tf_op jit(solution)/shard_map/ppermute | solution.py:221
  72.0 1.2 copy-done.1
  73.3 0.7 shard_map.64
  74.0 2.2 %collective-permute-start.8 = (bf16[128,64]{1,0:T(8,128)(2,1)S(1)}, bf16[128,64]{1,0:T(8,128)(2,1)S(1)}, u32[]{:S(2)}, u32[]{:S(2)}) collective-permute-start(bf16[128,64]{1,0:T(8,128)(2,1)S(1)} %shard_map.64), channel_id=1, source_target_pairs={{0,1},{1,0},{2,3},{3,2},{4,5},{5,4},{6,7},{7,6},{8,9},{9,8},{10,11... | collective-permute-start | bytes 49160 | tf_op jit(solution)/shard_map/ppermute | solution.py:76
  76.2 0.1 compare_and_fusion.1
  76.3 3.6 %collective-permute-done.8 = bf16[128,64]{1,0:T(8,128)(2,1)S(1)} collective-permute-done((bf16[128,64]{1,0:T(8,128)(2,1)S(1)}, bf16[128,64]{1,0:T(8,128)(2,1)S(1)}, u32[]{:S(2)}, u32[]{:S(2)}) %collective-permute-start.8) | collective-permute-done | bytes 16416 | tf_op jit(solution)/shard_map/ppermute | solution.py:76
  79.9 0.1 pad_maximum_fusion.1.after_ref
  80.0 0.7 collective-permute-start.10
  80.7 6.8 %collective-permute-start.9 = (bf16[128,128]{1,0:T(8,128)(2,1)S(1)}, bf16[128,128]{1,0:T(8,128)(2,1)S(1)}, u32[]{:S(2)}, u32[]{:S(2)}) collective-permute-start(bf16[128,128]{1,0:T(8,128)(2,1)S(1)} %pad_maximum_fusion.1.after_ref), channel_id=1, source_target_pairs={{0,2},{1,3},{2,6},{3,7},{4,10},{5,11},{6,14},{7,15},{8,18},{9,19},... | collective-permute-start | bytes 98312 | tf_op jit(solution)/shard_map/ppermute | solution.py:89
  87.4 2.2 %copy-done = bf16[8192,256]{1,0:T(8,128)(2,1)S(1)} copy-done((bf16[8192,256]{1,0:T(8,128)(2,1)S(1)}, bf16[8192,256]{1,0:T(8,128)(2,1)}, u32[]{:S(2)}) %copy-start) | copy-done | bytes 4194328
  89.6 0.9 shard_map.65
  90.5 0.1 reshape.209
  90.6 0.2 fusion.25
  90.8 2.5 %collective-permute-done.9 = bf16[128,128]{1,0:T(8,128)(2,1)S(1)} collective-permute-done((bf16[128,128]{1,0:T(8,128)(2,1)S(1)}, bf16[128,128]{1,0:T(8,128)(2,1)S(1)}, u32[]{:S(2)}, u32[]{:S(2)}) %collective-permute-start.9) | collective-permute-done | bytes 32800 | tf_op jit(solution)/shard_map/ppermute | solution.py:89
  93.4 0.3 fusion.21
  93.7 0.3 fusion.26
  94.0 0.2 convolution_convert_fusion
  94.2 0.1 copy.21.attended_ref
  94.4 3.8 %shard_map.66 = (bf16[96,8192]{1,0:T(8,128)(2,1)}, bf16[32,32,256]{2,1,0:T(8,128)(2,1)S(1)}) custom-call(bf16[128,256]{1,0:T(8,128)(2,1)S(1)} %copy.21.attended_ref, bf16[256,8192]{1,0:T(8,128)(2,1)} %w_ref.1), custom_call_target="tpu_custom_call" | custom-call | tf_op jit(solution)/shard_map/pallas_call | solution.py:132
  98.2 0.0 reduce-scatter.2.cloned.1.call-update
  98.2 20.5 %all_to_all.15.pieces_ref = bf16[32,32,256]{2,1,0:T(8,128)(2,1)S(1)} all-to-all(bf16[32,32,256]{2,1,0:T(8,128)(2,1)S(1)} %get-tuple-element.8), channel_id=1, replica_groups=mesh['x'=8,'yl'=2,'core'=2,'z'=8,'yh'=4] {'z','yh'}, dimensions={0} | all-to-all | bytes 1048576 | tf_op jit(solution)/shard_map/all_to_all | solution.py:233
  118.7 0.9 shard_map.67
  119.6 21.3 %all-to-all-start.2 = ((bf16[32,32,256]{2,1,0:T(8,128)(2,1)}), bf16[32,32,256]{2,1,0:T(8,128)(2,1)S(1)}, u32[]{:S(2)}, u32[]{:S(2)}) async-start(bf16[32,32,256]{2,1,0:T(8,128)(2,1)} %shard_map.67), calls=%async_computation.3 | async-start | bytes 1048576 | tf_op jit(solution)/shard_map/all_to_all | solution.py:235
  140.9 8.6 %reduce-scatter.2.cloned.1.call-done = bf16[1024,96]{0,1:T(8,128)(2,1)} async-done(((bf16[8192,96]{0,1:T(8,128)(2,1)}), bf16[1024,96]{0,1:T(8,128)(2,1)}) %reduce-scatter.2.cloned.1.call-update) | async-done | bytes 196624 | tf_op jit(solution)/shard_map/reduce_scatter | solution.py:232
  149.5 1.6 copy.30
  151.1 6.5 %all-to-all-done.2 = bf16[32,32,256]{2,1,0:T(8,128)(2,1)S(1)} async-done(((bf16[32,32,256]{2,1,0:T(8,128)(2,1)}), bf16[32,32,256]{2,1,0:T(8,128)(2,1)S(1)}, u32[]{:S(2)}, u32[]{:S(2)}) %all-to-all-start.2) | async-done | bytes 524320 | tf_op jit(solution)/shard_map/all_to_all | solution.py:235
  157.6 3.4 %all-to-all-start = ((bf16[4,96,256]{2,1,0:T(8,128)(2,1)}), bf16[4,96,256]{2,1,0:T(8,128)(2,1)S(1)}, u32[]{:S(2)}, u32[]{:S(2)}) async-start(bf16[4,96,256]{2,1,0:T(8,128)(2,1)} %bitcast.41), calls=%async_computation.1 | async-start | bytes 393216 | tf_op jit(solution)/shard_map/all_to_all | solution.py:237
  161.0 0.2 convolution_convert_fusion.1
  161.2 7.9 %all-to-all-done = bf16[4,96,256]{2,1,0:T(8,128)(2,1)S(1)} async-done(((bf16[4,96,256]{2,1,0:T(8,128)(2,1)}), bf16[4,96,256]{2,1,0:T(8,128)(2,1)S(1)}, u32[]{:S(2)}, u32[]{:S(2)}) %all-to-all-start) | async-done | bytes 196640 | tf_op jit(solution)/shard_map/all_to_all | solution.py:237
  169.2 0.6 pad_maximum_fusion
  (19 shorter events, 0.2 us)
Async XLA Ops:
  6.5 142.9 %reduce-scatter.2.cloned.1.call-start = ((), (), s32[]{:S(2)}) async-start(), calls=%async_computation.4 | async-start | bytes 1769472 | tf_op jit(solution)/shard_map/reduce_scatter | solution.py:232
  22.0 20.5 %collective-permute-start.1 = (bf16[128,1024]{1,0:T(8,128)(2,1)S(1)}, bf16[128,1024]{1,0:T(8,128)(2,1)S(1)}, u32[]{:S(2)}, u32[]{:S(2)}) collective-permute-start(bf16[128,1024]{1,0:T(8,128)(2,1)S(1)} %all_gather.3.refs_0_), channel_id=1, source_target_pairs={{0,28},{4,0},{8,4},{12,8},{16,12},{20,16},{24,20},{28,24},{1,29},{... | collective-permute-start | bytes 786440 | tf_op jit(solution)/shard_map/ppermute | solution.py:218
  39.2 8.3 %collective-permute-start = (bf16[128,1024]{1,0:T(8,128)(2,1)S(1)}, bf16[128,1024]{1,0:T(8,128)(2,1)S(1)}, u32[]{:S(2)}, u32[]{:S(2)}) collective-permute-start(bf16[128,1024]{1,0:T(8,128)(2,1)S(1)} %all_gather.3.refs_0_), channel_id=1, source_target_pairs={{0,4},{4,8},{8,12},{12,16},{16,20},{20,24},{24,28},{28,0},{1,5},{5... | collective-permute-start | bytes 786440 | tf_op jit(solution)/shard_map/ppermute | solution.py:217
  42.5 8.4 %collective-permute-start.3 = (bf16[128,1024]{1,0:T(8,128)(2,1)S(1)}, bf16[128,1024]{1,0:T(8,128)(2,1)S(1)}, u32[]{:S(2)}, u32[]{:S(2)}) collective-permute-start(bf16[128,1024]{1,0:T(8,128)(2,1)S(1)} %collective-permute-done.1.refs_2_), channel_id=1, source_target_pairs={{0,28},{4,0},{8,4},{12,8},{16,12},{20,16},{24,20},{28,24},{1,29},{... | collective-permute-start | bytes 786440 | tf_op jit(solution)/shard_map/ppermute | solution.py:218
  47.5 8.3 %collective-permute-start.2 = (bf16[128,1024]{1,0:T(8,128)(2,1)S(1)}, bf16[128,1024]{1,0:T(8,128)(2,1)S(1)}, u32[]{:S(2)}, u32[]{:S(2)}) collective-permute-start(bf16[128,1024]{1,0:T(8,128)(2,1)S(1)} %collective-permute-done.refs_1_), channel_id=1, source_target_pairs={{0,4},{4,8},{8,12},{12,16},{16,20},{20,24},{24,28},{28,0},{1,5},{5... | collective-permute-start | bytes 786440 | tf_op jit(solution)/shard_map/ppermute | solution.py:217
  50.9 8.2 %collective-permute-start.5 = (bf16[128,1024]{1,0:T(8,128)(2,1)S(1)}, bf16[128,1024]{1,0:T(8,128)(2,1)S(1)}, u32[]{:S(2)}, u32[]{:S(2)}) collective-permute-start(bf16[128,1024]{1,0:T(8,128)(2,1)S(1)} %collective-permute-done.3.refs_4_), channel_id=1, source_target_pairs={{0,28},{4,0},{8,4},{12,8},{16,12},{20,16},{24,20},{28,24},{1,29},{... | collective-permute-start | bytes 786440 | tf_op jit(solution)/shard_map/ppermute | solution.py:218
  55.9 8.3 %collective-permute-start.4 = (bf16[128,1024]{1,0:T(8,128)(2,1)S(1)}, bf16[128,1024]{1,0:T(8,128)(2,1)S(1)}, u32[]{:S(2)}, u32[]{:S(2)}) collective-permute-start(bf16[128,1024]{1,0:T(8,128)(2,1)S(1)} %collective-permute-done.2.refs_3_), channel_id=1, source_target_pairs={{0,4},{4,8},{8,12},{12,16},{16,20},{20,24},{24,28},{28,0},{1,5},{5... | collective-permute-start | bytes 786440 | tf_op jit(solution)/shard_map/ppermute | solution.py:217
  59.1 7.6 %collective-permute-start.7 = (bf16[64,1024]{1,0:T(8,128)(2,1)S(1)}, bf16[64,1024]{1,0:T(8,128)(2,1)S(1)}, u32[]{:S(2)}, u32[]{:S(2)}) collective-permute-start(bf16[64,1024]{1,0:T(8,128)(2,1)S(1)} %slice.29), channel_id=1, source_target_pairs={{0,28},{4,0},{8,4},{12,8},{16,12},{20,16},{24,20},{28,24},{1,29},{... | collective-permute-start | bytes 393224 | tf_op jit(solution)/shard_map/ppermute | solution.py:222
  64.2 7.8 %collective-permute-start.6 = (bf16[64,1024]{1,0:T(8,128)(2,1)S(1)}, bf16[64,1024]{1,0:T(8,128)(2,1)S(1)}, u32[]{:S(2)}, u32[]{:S(2)}) collective-permute-start(bf16[64,1024]{1,0:T(8,128)(2,1)S(1)} %slice.28), channel_id=1, source_target_pairs={{0,4},{4,8},{8,12},{12,16},{16,20},{20,24},{24,28},{28,0},{1,5},{5... | collective-permute-start | bytes 393224 | tf_op jit(solution)/shard_map/ppermute | solution.py:221
  72.0 1.2 copy-start.1
  74.0 5.9 %collective-permute-start.8 = (bf16[128,64]{1,0:T(8,128)(2,1)S(1)}, bf16[128,64]{1,0:T(8,128)(2,1)S(1)}, u32[]{:S(2)}, u32[]{:S(2)}) collective-permute-start(bf16[128,64]{1,0:T(8,128)(2,1)S(1)} %shard_map.64), channel_id=1, source_target_pairs={{0,1},{1,0},{2,3},{3,2},{4,5},{5,4},{6,7},{7,6},{8,9},{9,8},{10,11... | collective-permute-start | bytes 49160 | tf_op jit(solution)/shard_map/ppermute | solution.py:76
  80.0 10.9 %collective-permute-start.10 = (bf16[128,128]{1,0:T(8,128)(2,1)S(1)}, bf16[128,128]{1,0:T(8,128)(2,1)S(1)}, u32[]{:S(2)}, u32[]{:S(2)}) collective-permute-start(bf16[128,128]{1,0:T(8,128)(2,1)S(1)} %pad_maximum_fusion.1.after_ref), channel_id=1, source_target_pairs={{0,0},{1,1},{2,4},{3,5},{4,8},{5,9},{6,12},{7,13},{8,16},{9,17},{1... | collective-permute-start | bytes 98312 | tf_op jit(solution)/shard_map/ppermute | solution.py:88
  80.7 12.7 %collective-permute-start.9 = (bf16[128,128]{1,0:T(8,128)(2,1)S(1)}, bf16[128,128]{1,0:T(8,128)(2,1)S(1)}, u32[]{:S(2)}, u32[]{:S(2)}) collective-permute-start(bf16[128,128]{1,0:T(8,128)(2,1)S(1)} %pad_maximum_fusion.1.after_ref), channel_id=1, source_target_pairs={{0,2},{1,3},{2,6},{3,7},{4,10},{5,11},{6,14},{7,15},{8,18},{9,19},... | collective-permute-start | bytes 98312 | tf_op jit(solution)/shard_map/ppermute | solution.py:89
  87.4 2.2 %copy-start = (bf16[8192,256]{1,0:T(8,128)(2,1)S(1)}, bf16[8192,256]{1,0:T(8,128)(2,1)}, u32[]{:S(2)}) copy-start(bf16[8192,256]{1,0:T(8,128)(2,1)} %refs_9_.1) | copy-start | bytes 12582916
  94.4 66.6 %copy-start.2 = (s32[1024]{0:T(1024)S(1)}, s32[1024]{0:T(1024)}, u32[]{:S(2)}) copy-start(s32[1024]{0:T(1024)} %param.10) | copy-start | bytes 12292
  119.6 38.0 %all-to-all-start.2 = ((bf16[32,32,256]{2,1,0:T(8,128)(2,1)}), bf16[32,32,256]{2,1,0:T(8,128)(2,1)S(1)}, u32[]{:S(2)}, u32[]{:S(2)}) async-start(bf16[32,32,256]{2,1,0:T(8,128)(2,1)} %shard_map.67), calls=%async_computation.3 | async-start | bytes 1048576 | tf_op jit(solution)/shard_map/all_to_all | solution.py:235
  157.6 11.5 %all-to-all-start = ((bf16[4,96,256]{2,1,0:T(8,128)(2,1)}), bf16[4,96,256]{2,1,0:T(8,128)(2,1)S(1)}, u32[]{:S(2)}, u32[]{:S(2)}) async-start(bf16[4,96,256]{2,1,0:T(8,128)(2,1)} %bitcast.41), calls=%async_computation.1 | async-start | bytes 393216 | tf_op jit(solution)/shard_map/all_to_all | solution.py:237
Sparse Core Ops, SparseCore 0:
  98.3 51.1 reduce-scatter.1

commit v9 on v8

--- a/solution.py
+++ b/solution.py
@@ -203,6 +203,56 @@
     )(z_me, after, *pieces, weight)
 
 
+def early_kernel(z_ref, *refs):
+    *piece_refs, w_ref, out_ref, last_ref = refs
+    depth = piece_refs[0].shape[1]
+
+    def columns(k):
+        at = pl.multiple_of(lax.rem(z_ref[0] + k + N_Z, N_Z) * depth, depth)
+        return w_ref[:, pl.ds(at, depth)]
+
+    total = jnp.zeros(out_ref.shape, jnp.float32)
+    for piece, k in zip(piece_refs, DISTANCES, strict=True):
+        total = total + lax.dot_general(
+            piece[...], columns(k), (((1,), (1,)), ((), ())), preferred_element_type=jnp.float32
+        )
+    out_ref[...] = total
+    last_ref[...] = columns(N_Z // 2)
+
+
+def late_kernel(total_ref, up_ref, down_ref, w_ref, out_ref):
+    half = up_ref.shape[0]
+    for at, piece in ((0, up_ref), (half, down_ref)):
+        rows = lax.dot_general(
+            piece[...], w_ref[...], (((1,), (1,)), ((), ())), preferred_element_type=jnp.float32
+        )
+        out_ref[at : at + half] = (total_ref[at : at + half] + rows).astype(jnp.bfloat16)
+
+
+def keyval_product(pieces, weight):
+    rows, depth = pieces[0].shape
+    columns = weight.shape[0]
+    vmem = pl.BlockSpec(memory_space=pltpu.VMEM)
+    params = pltpu.CompilerParams(vmem_limit_bytes=16 * 1024 * 1024)
+    total, last = pl.pallas_call(
+        early_kernel,
+        in_specs=[pl.BlockSpec(memory_space=pltpu.SMEM)] + [vmem] * (len(pieces) - 1),
+        out_specs=[vmem] * 2,
+        out_shape=[
+            jax.ShapeDtypeStruct((rows, columns), jnp.float32),
+            jax.ShapeDtypeStruct((columns, depth), jnp.bfloat16),
+        ],
+        compiler_params=params,
+    )(lax.axis_index("z").reshape(1), *pieces[:-2], weight)
+    return pl.pallas_call(
+        late_kernel,
+        in_specs=[vmem] * 4,
+        out_specs=vmem,
+        out_shape=jax.ShapeDtypeStruct((rows, columns), jnp.bfloat16),
+        compiler_params=params,
+    )(total, *pieces[-2:], last)
+
+
 def shards(activations, w_query, w_keyval, w_out, targets, segments):
     block = lax.axis_index(DP)
     tail_docs = lax.dynamic_slice_in_dim(targets, block * MOVE, MOVE) // RECV
@@ -220,7 +270,7 @@
     half = SEQ // 2
     pieces.append(lax.ppermute(up[:half], "z", ring(N_Z, 1)))
     pieces.append(lax.ppermute(down[half:], "z", ring(N_Z, -1)))
-    keyval = product(pieces, w_keyval.T, True, jnp.bfloat16, lax.axis_index("z").reshape(1))
+    keyval = keyval_product(pieces, w_keyval.T)
     key, value, whole = move_keyval(keyval)
     query = product(pieces, w_query, False, jnp.float32, whole)
 

time: 178 us -> 177 us (level)
  waiting for transfers between devices: 37.3 us -> 35.4 us
  transfers between devices with their start and end apart: 14 -> 14, of which waited for: 9 -> 8; matrix products, arithmetic and copies ran while one was open for 2% -> 2% of each run, Pallas kernels for 1% -> 1%
where the time goes in v9:
time: 177 us; the launch traced here: 175 us
  starting transfers between devices  73.8 us (42%)
  blocking collectives  36.3 us (21%)
  waiting for transfers between devices  35.4 us (20%)
  between operations  13.7 us (8%)
  Pallas kernels  6.42 us (4%)
  local copies, waits for them, and re-layouts  6.12 us (3%)
  other arithmetic  2.54 us (1%)
    ppermute x3, starting transfers between devices, shards(): down = lax.ppermute(down, 'z', ring(N_Z, -1))  27.1 us
    all_to_all x1, starting transfers between devices, shards(): tails = lax.all_to_all(moving, DP, 0, 0, tiled=True)  21.3 us
    all_to_all x1, blocking collectives, shards(): moving = lax.all_to_all(moving, TENSOR, 0, 0, tiled=True)  20.8 us
    all_gather x1, blocking collectives, shards(): own = lax.all_gather(activations, 'yh', axis=1, tiled=True)  15.5 us
    reduce_scatter x1, waiting for transfers between devices, shards(): kept = lax.psum_scatter(kept.T, 'z', scatter_dimension=0, tiled=True).T  8.67 us
    all_to_all x1, waiting for transfers between devices, shards(): kept = sum_pieces(lax.all_to_all(kept, 'yh', 0, 0, tiled=True))  7.93 us
    ppermute x1, starting transfers between devices, move_keyval(): crossed = lax.ppermute(whole, TENSOR, routes(1))  6.47 us
    all_to_all x1, waiting for transfers between devices, shards(): tails = lax.all_to_all(moving, DP, 0, 0, tiled=True)  6.42 us
  transfers between devices with their start and end apart: 14, of which 8 were waited for; matrix products, arithmetic and copies ran while one was open for 2% of the time, Pallas kernels for 1%

profile of v9, /device:TPU:1, one launch (start us, length us, event | category | flops | bytes accessed | tf_op | source)
XLA Modules:
  0.0 174.9 jit_solution(9666711088875612241)
XLA Ops:
  6.5 15.5 %all_gather.3.refs_0_ = bf16[128,1024]{1,0:T(8,128)(2,1)S(1)} all-gather(bf16[128,256]{1,0:T(8,128)(2,1)} %param.6), channel_id=1, replica_groups=mesh['x'=8,'yl'=2,'core'=2,'z'=8,'yh'=4] {'yh'}, dimensions={1}, use_global_device_ids=true | all-gather | bytes 327680 | tf_op jit(solution)/shard_map/all_gather | solution.py:263
  22.0 17.2 %collective-permute-start.1 = (bf16[128,1024]{1,0:T(8,128)(2,1)S(1)}, bf16[128,1024]{1,0:T(8,128)(2,1)S(1)}, u32[]{:S(2)}, u32[]{:S(2)}) collective-permute-start(bf16[128,1024]{1,0:T(8,128)(2,1)S(1)} %all_gather.3.refs_0_), channel_id=1, source_target_pairs={{0,28},{4,0},{8,4},{12,8},{16,12},{20,16},{24,20},{28,24},{1,29},{... | collective-permute-start | bytes 786440 | tf_op jit(solution)/shard_map/ppermute | solution.py:268
  39.2 1.9 %collective-permute-start = (bf16[128,1024]{1,0:T(8,128)(2,1)S(1)}, bf16[128,1024]{1,0:T(8,128)(2,1)S(1)}, u32[]{:S(2)}, u32[]{:S(2)}) collective-permute-start(bf16[128,1024]{1,0:T(8,128)(2,1)S(1)} %all_gather.3.refs_0_), channel_id=1, source_target_pairs={{0,4},{4,8},{8,12},{12,16},{16,20},{20,24},{24,28},{28,0},{1,5},{5... | collective-permute-start | bytes 786440 | tf_op jit(solution)/shard_map/ppermute | solution.py:267
  41.1 1.4 collective-permute-done.1.refs_2_
  42.5 5.0 %collective-permute-start.3 = (bf16[128,1024]{1,0:T(8,128)(2,1)S(1)}, bf16[128,1024]{1,0:T(8,128)(2,1)S(1)}, u32[]{:S(2)}, u32[]{:S(2)}) collective-permute-start(bf16[128,1024]{1,0:T(8,128)(2,1)S(1)} %collective-permute-done.1.refs_2_), channel_id=1, source_target_pairs={{0,28},{4,0},{8,4},{12,8},{16,12},{20,16},{24,20},{28,24},{1,29},{... | collective-permute-start | bytes 786440 | tf_op jit(solution)/shard_map/ppermute | solution.py:268
  47.5 1.9 %collective-permute-start.2 = (bf16[128,1024]{1,0:T(8,128)(2,1)S(1)}, bf16[128,1024]{1,0:T(8,128)(2,1)S(1)}, u32[]{:S(2)}, u32[]{:S(2)}) collective-permute-start(bf16[128,1024]{1,0:T(8,128)(2,1)S(1)} %collective-permute-done.refs_1_), channel_id=1, source_target_pairs={{0,4},{4,8},{8,12},{12,16},{16,20},{20,24},{24,28},{28,0},{1,5},{5... | collective-permute-start | bytes 786440 | tf_op jit(solution)/shard_map/ppermute | solution.py:267
  49.5 0.7 slice.23
  50.2 0.8 fusion.23
  50.9 4.9 %collective-permute-start.5 = (bf16[128,1024]{1,0:T(8,128)(2,1)S(1)}, bf16[128,1024]{1,0:T(8,128)(2,1)S(1)}, u32[]{:S(2)}, u32[]{:S(2)}) collective-permute-start(bf16[128,1024]{1,0:T(8,128)(2,1)S(1)} %collective-permute-done.3.refs_4_), channel_id=1, source_target_pairs={{0,28},{4,0},{8,4},{12,8},{16,12},{20,16},{24,20},{28,24},{1,29},{... | collective-permute-start | bytes 786440 | tf_op jit(solution)/shard_map/ppermute | solution.py:268
  55.8 0.0 collective-permute-done.2.refs_3_
  55.9 1.9 %collective-permute-start.4 = (bf16[128,1024]{1,0:T(8,128)(2,1)S(1)}, bf16[128,1024]{1,0:T(8,128)(2,1)S(1)}, u32[]{:S(2)}, u32[]{:S(2)}) collective-permute-start(bf16[128,1024]{1,0:T(8,128)(2,1)S(1)} %collective-permute-done.2.refs_3_), channel_id=1, source_target_pairs={{0,4},{4,8},{8,12},{12,16},{16,20},{20,24},{24,28},{28,0},{1,5},{5... | collective-permute-start | bytes 786440 | tf_op jit(solution)/shard_map/ppermute | solution.py:267
  57.8 0.1 pad_add_fusion
  57.9 0.1 convert_reduce_fusion
  58.0 1.2 collective-permute-done.5.refs_6_
  59.1 5.0 %collective-permute-start.7 = (bf16[64,1024]{1,0:T(8,128)(2,1)S(1)}, bf16[64,1024]{1,0:T(8,128)(2,1)S(1)}, u32[]{:S(2)}, u32[]{:S(2)}) collective-permute-start(bf16[64,1024]{1,0:T(8,128)(2,1)S(1)} %slice.29), channel_id=1, source_target_pairs={{0,28},{4,0},{8,4},{12,8},{16,12},{20,16},{24,20},{28,24},{1,29},{... | collective-permute-start | bytes 393224 | tf_op jit(solution)/shard_map/ppermute | solution.py:272
  64.2 1.9 %collective-permute-start.6 = (bf16[64,1024]{1,0:T(8,128)(2,1)S(1)}, bf16[64,1024]{1,0:T(8,128)(2,1)S(1)}, u32[]{:S(2)}, u32[]{:S(2)}) collective-permute-start(bf16[64,1024]{1,0:T(8,128)(2,1)S(1)} %slice.28), channel_id=1, source_target_pairs={{0,4},{4,8},{8,12},{12,16},{16,20},{20,24},{24,28},{28,0},{1,5},{5... | collective-permute-start | bytes 393224 | tf_op jit(solution)/shard_map/ppermute | solution.py:271
  66.1 0.3 multiply_cosine_fusion
  66.5 1.2 copy-done.1
  67.7 0.6 shard_map.64
  68.3 3.7 %collective-permute-done.6.up_ref.refs_7_ = bf16[64,1024]{1,0:T(8,128)(2,1)S(1)} collective-permute-done((bf16[64,1024]{1,0:T(8,128)(2,1)S(1)}, bf16[64,1024]{1,0:T(8,128)(2,1)S(1)}, u32[]{:S(2)}, u32[]{:S(2)}) %collective-permute-start.6) | collective-permute-done | bytes 131104 | tf_op jit(solution)/shard_map/ppermute | solution.py:271
  72.0 0.2 shard_map.65
  72.3 2.2 %collective-permute-start.8 = (bf16[128,64]{1,0:T(8,128)(2,1)S(1)}, bf16[128,64]{1,0:T(8,128)(2,1)S(1)}, u32[]{:S(2)}, u32[]{:S(2)}) collective-permute-start(bf16[128,64]{1,0:T(8,128)(2,1)S(1)} %shard_map.65), channel_id=1, source_target_pairs={{0,1},{1,0},{2,3},{3,2},{4,5},{5,4},{6,7},{7,6},{8,9},{9,8},{10,11... | collective-permute-start | bytes 49160 | tf_op jit(solution)/shard_map/ppermute | solution.py:76
  74.5 0.1 compare_and_fusion.1
  74.6 3.9 %collective-permute-done.8 = bf16[128,64]{1,0:T(8,128)(2,1)S(1)} collective-permute-done((bf16[128,64]{1,0:T(8,128)(2,1)S(1)}, bf16[128,64]{1,0:T(8,128)(2,1)S(1)}, u32[]{:S(2)}, u32[]{:S(2)}) %collective-permute-start.8) | collective-permute-done | bytes 16416 | tf_op jit(solution)/shard_map/ppermute | solution.py:76
  78.5 0.1 pad_maximum_fusion.1.after_ref
  78.6 0.7 collective-permute-start.10
  79.2 6.5 %collective-permute-start.9 = (bf16[128,128]{1,0:T(8,128)(2,1)S(1)}, bf16[128,128]{1,0:T(8,128)(2,1)S(1)}, u32[]{:S(2)}, u32[]{:S(2)}) collective-permute-start(bf16[128,128]{1,0:T(8,128)(2,1)S(1)} %pad_maximum_fusion.1.after_ref), channel_id=1, source_target_pairs={{0,2},{1,3},{2,6},{3,7},{4,10},{5,11},{6,14},{7,15},{8,18},{9,19},... | collective-permute-start | bytes 98312 | tf_op jit(solution)/shard_map/ppermute | solution.py:89
  85.7 2.2 %copy-done = bf16[8192,256]{1,0:T(8,128)(2,1)S(1)} copy-done((bf16[8192,256]{1,0:T(8,128)(2,1)S(1)}, bf16[8192,256]{1,0:T(8,128)(2,1)}, u32[]{:S(2)}) %copy-start) | copy-done | bytes 4194328
  87.9 0.9 shard_map.66
  88.8 0.1 reshape.208
  88.9 0.2 fusion.25
  89.1 2.2 %collective-permute-done.9 = bf16[128,128]{1,0:T(8,128)(2,1)S(1)} collective-permute-done((bf16[128,128]{1,0:T(8,128)(2,1)S(1)}, bf16[128,128]{1,0:T(8,128)(2,1)S(1)}, u32[]{:S(2)}, u32[]{:S(2)}) %collective-permute-start.9) | collective-permute-done | bytes 32800 | tf_op jit(solution)/shard_map/ppermute | solution.py:89
  91.4 0.3 fusion.21
  91.7 0.3 fusion.26
  92.0 0.2 convolution_convert_fusion
  92.2 0.1 copy.21.attended_ref
  92.4 3.8 %shard_map.67 = (bf16[96,8192]{1,0:T(8,128)(2,1)}, bf16[32,32,256]{2,1,0:T(8,128)(2,1)S(1)}) custom-call(bf16[128,256]{1,0:T(8,128)(2,1)S(1)} %copy.21.attended_ref, bf16[256,8192]{1,0:T(8,128)(2,1)} %w_ref.1), custom_call_target="tpu_custom_call" | custom-call | tf_op jit(solution)/shard_map/pallas_call | solution.py:132
  96.1 0.0 reduce-scatter.2.cloned.1.call-update
  96.2 20.8 %all_to_all.15.pieces_ref = bf16[32,32,256]{2,1,0:T(8,128)(2,1)S(1)} all-to-all(bf16[32,32,256]{2,1,0:T(8,128)(2,1)S(1)} %get-tuple-element.12), channel_id=1, replica_groups=mesh['x'=8,'yl'=2,'core'=2,'z'=8,'yh'=4] {'z','yh'}, dimensions={0} | all-to-all | bytes 1048576 | tf_op jit(solution)/shard_map/all_to_all | solution.py:283
  116.9 0.9 shard_map.68
  117.9 21.3 %all-to-all-start.2 = ((bf16[32,32,256]{2,1,0:T(8,128)(2,1)}), bf16[32,32,256]{2,1,0:T(8,128)(2,1)S(1)}, u32[]{:S(2)}, u32[]{:S(2)}) async-start(bf16[32,32,256]{2,1,0:T(8,128)(2,1)} %shard_map.68), calls=%async_computation.3 | async-start | bytes 1048576 | tf_op jit(solution)/shard_map/all_to_all | solution.py:285
  139.2 8.7 %reduce-scatter.2.cloned.1.call-done = bf16[1024,96]{0,1:T(8,128)(2,1)} async-done(((bf16[8192,96]{0,1:T(8,128)(2,1)}), bf16[1024,96]{0,1:T(8,128)(2,1)}) %reduce-scatter.2.cloned.1.call-update) | async-done | bytes 196624 | tf_op jit(solution)/shard_map/reduce_scatter | solution.py:282
  147.8 1.6 copy.30
  149.4 6.4 %all-to-all-done.2 = bf16[32,32,256]{2,1,0:T(8,128)(2,1)S(1)} async-done(((bf16[32,32,256]{2,1,0:T(8,128)(2,1)}), bf16[32,32,256]{2,1,0:T(8,128)(2,1)S(1)}, u32[]{:S(2)}, u32[]{:S(2)}) %all-to-all-start.2) | async-done | bytes 524320 | tf_op jit(solution)/shard_map/all_to_all | solution.py:285
  155.9 3.4 %all-to-all-start = ((bf16[4,96,256]{2,1,0:T(8,128)(2,1)}), bf16[4,96,256]{2,1,0:T(8,128)(2,1)S(1)}, u32[]{:S(2)}, u32[]{:S(2)}) async-start(bf16[4,96,256]{2,1,0:T(8,128)(2,1)} %bitcast.41), calls=%async_computation.1 | async-start | bytes 393216 | tf_op jit(solution)/shard_map/all_to_all | solution.py:287
  159.3 0.2 convolution_convert_fusion.1
  159.5 7.9 %all-to-all-done = bf16[4,96,256]{2,1,0:T(8,128)(2,1)S(1)} async-done(((bf16[4,96,256]{2,1,0:T(8,128)(2,1)}), bf16[4,96,256]{2,1,0:T(8,128)(2,1)S(1)}, u32[]{:S(2)}, u32[]{:S(2)}) %all-to-all-start) | async-done | bytes 196640 | tf_op jit(solution)/shard_map/all_to_all | solution.py:287
  167.4 0.6 pad_maximum_fusion
  (20 shorter events, 0.2 us)
Async XLA Ops:
  6.5 141.3 %reduce-scatter.2.cloned.1.call-start = ((), (), s32[]{:S(2)}) async-start(), calls=%async_computation.4 | async-start | bytes 1769472 | tf_op jit(solution)/shard_map/reduce_scatter | solution.py:282
  22.0 20.5 %collective-permute-start.1 = (bf16[128,1024]{1,0:T(8,128)(2,1)S(1)}, bf16[128,1024]{1,0:T(8,128)(2,1)S(1)}, u32[]{:S(2)}, u32[]{:S(2)}) collective-permute-start(bf16[128,1024]{1,0:T(8,128)(2,1)S(1)} %all_gather.3.refs_0_), channel_id=1, source_target_pairs={{0,28},{4,0},{8,4},{12,8},{16,12},{20,16},{24,20},{28,24},{1,29},{... | collective-permute-start | bytes 786440 | tf_op jit(solution)/shard_map/ppermute | solution.py:268
  39.2 8.3 %collective-permute-start = (bf16[128,1024]{1,0:T(8,128)(2,1)S(1)}, bf16[128,1024]{1,0:T(8,128)(2,1)S(1)}, u32[]{:S(2)}, u32[]{:S(2)}) collective-permute-start(bf16[128,1024]{1,0:T(8,128)(2,1)S(1)} %all_gather.3.refs_0_), channel_id=1, source_target_pairs={{0,4},{4,8},{8,12},{12,16},{16,20},{20,24},{24,28},{28,0},{1,5},{5... | collective-permute-start | bytes 786440 | tf_op jit(solution)/shard_map/ppermute | solution.py:267
  42.5 8.4 %collective-permute-start.3 = (bf16[128,1024]{1,0:T(8,128)(2,1)S(1)}, bf16[128,1024]{1,0:T(8,128)(2,1)S(1)}, u32[]{:S(2)}, u32[]{:S(2)}) collective-permute-start(bf16[128,1024]{1,0:T(8,128)(2,1)S(1)} %collective-permute-done.1.refs_2_), channel_id=1, source_target_pairs={{0,28},{4,0},{8,4},{12,8},{16,12},{20,16},{24,20},{28,24},{1,29},{... | collective-permute-start | bytes 786440 | tf_op jit(solution)/shard_map/ppermute | solution.py:268
  47.5 8.3 %collective-permute-start.2 = (bf16[128,1024]{1,0:T(8,128)(2,1)S(1)}, bf16[128,1024]{1,0:T(8,128)(2,1)S(1)}, u32[]{:S(2)}, u32[]{:S(2)}) collective-permute-start(bf16[128,1024]{1,0:T(8,128)(2,1)S(1)} %collective-permute-done.refs_1_), channel_id=1, source_target_pairs={{0,4},{4,8},{8,12},{12,16},{16,20},{20,24},{24,28},{28,0},{1,5},{5... | collective-permute-start | bytes 786440 | tf_op jit(solution)/shard_map/ppermute | solution.py:267
  50.9 8.2 %collective-permute-start.5 = (bf16[128,1024]{1,0:T(8,128)(2,1)S(1)}, bf16[128,1024]{1,0:T(8,128)(2,1)S(1)}, u32[]{:S(2)}, u32[]{:S(2)}) collective-permute-start(bf16[128,1024]{1,0:T(8,128)(2,1)S(1)} %collective-permute-done.3.refs_4_), channel_id=1, source_target_pairs={{0,28},{4,0},{8,4},{12,8},{16,12},{20,16},{24,20},{28,24},{1,29},{... | collective-permute-start | bytes 786440 | tf_op jit(solution)/shard_map/ppermute | solution.py:268
  55.9 8.3 %collective-permute-start.4 = (bf16[128,1024]{1,0:T(8,128)(2,1)S(1)}, bf16[128,1024]{1,0:T(8,128)(2,1)S(1)}, u32[]{:S(2)}, u32[]{:S(2)}) collective-permute-start(bf16[128,1024]{1,0:T(8,128)(2,1)S(1)} %collective-permute-done.2.refs_3_), channel_id=1, source_target_pairs={{0,4},{4,8},{8,12},{12,16},{16,20},{20,24},{24,28},{28,0},{1,5},{5... | collective-permute-start | bytes 786440 | tf_op jit(solution)/shard_map/ppermute | solution.py:267
  59.1 9.2 %collective-permute-start.7 = (bf16[64,1024]{1,0:T(8,128)(2,1)S(1)}, bf16[64,1024]{1,0:T(8,128)(2,1)S(1)}, u32[]{:S(2)}, u32[]{:S(2)}) collective-permute-start(bf16[64,1024]{1,0:T(8,128)(2,1)S(1)} %slice.29), channel_id=1, source_target_pairs={{0,28},{4,0},{8,4},{12,8},{16,12},{20,16},{24,20},{28,24},{1,29},{... | collective-permute-start | bytes 393224 | tf_op jit(solution)/shard_map/ppermute | solution.py:272
  64.2 7.8 %collective-permute-start.6 = (bf16[64,1024]{1,0:T(8,128)(2,1)S(1)}, bf16[64,1024]{1,0:T(8,128)(2,1)S(1)}, u32[]{:S(2)}, u32[]{:S(2)}) collective-permute-start(bf16[64,1024]{1,0:T(8,128)(2,1)S(1)} %slice.28), channel_id=1, source_target_pairs={{0,4},{4,8},{8,12},{12,16},{16,20},{20,24},{24,28},{28,0},{1,5},{5... | collective-permute-start | bytes 393224 | tf_op jit(solution)/shard_map/ppermute | solution.py:271
  66.5 1.2 copy-start.1
  72.3 6.2 %collective-permute-start.8 = (bf16[128,64]{1,0:T(8,128)(2,1)S(1)}, bf16[128,64]{1,0:T(8,128)(2,1)S(1)}, u32[]{:S(2)}, u32[]{:S(2)}) collective-permute-start(bf16[128,64]{1,0:T(8,128)(2,1)S(1)} %shard_map.65), channel_id=1, source_target_pairs={{0,1},{1,0},{2,3},{3,2},{4,5},{5,4},{6,7},{7,6},{8,9},{9,8},{10,11... | collective-permute-start | bytes 49160 | tf_op jit(solution)/shard_map/ppermute | solution.py:76
  78.6 10.6 %collective-permute-start.10 = (bf16[128,128]{1,0:T(8,128)(2,1)S(1)}, bf16[128,128]{1,0:T(8,128)(2,1)S(1)}, u32[]{:S(2)}, u32[]{:S(2)}) collective-permute-start(bf16[128,128]{1,0:T(8,128)(2,1)S(1)} %pad_maximum_fusion.1.after_ref), channel_id=1, source_target_pairs={{0,0},{1,1},{2,4},{3,5},{4,8},{5,9},{6,12},{7,13},{8,16},{9,17},{1... | collective-permute-start | bytes 98312 | tf_op jit(solution)/shard_map/ppermute | solution.py:88
  79.2 12.1 %collective-permute-start.9 = (bf16[128,128]{1,0:T(8,128)(2,1)S(1)}, bf16[128,128]{1,0:T(8,128)(2,1)S(1)}, u32[]{:S(2)}, u32[]{:S(2)}) collective-permute-start(bf16[128,128]{1,0:T(8,128)(2,1)S(1)} %pad_maximum_fusion.1.after_ref), channel_id=1, source_target_pairs={{0,2},{1,3},{2,6},{3,7},{4,10},{5,11},{6,14},{7,15},{8,18},{9,19},... | collective-permute-start | bytes 98312 | tf_op jit(solution)/shard_map/ppermute | solution.py:89
  85.7 2.2 %copy-start = (bf16[8192,256]{1,0:T(8,128)(2,1)S(1)}, bf16[8192,256]{1,0:T(8,128)(2,1)}, u32[]{:S(2)}) copy-start(bf16[8192,256]{1,0:T(8,128)(2,1)} %refs_9_.1) | copy-start | bytes 12582916
  92.4 66.9 %copy-start.2 = (s32[1024]{0:T(1024)S(1)}, s32[1024]{0:T(1024)}, u32[]{:S(2)}) copy-start(s32[1024]{0:T(1024)} %param.10) | copy-start | bytes 12292
  117.9 38.0 %all-to-all-start.2 = ((bf16[32,32,256]{2,1,0:T(8,128)(2,1)}), bf16[32,32,256]{2,1,0:T(8,128)(2,1)S(1)}, u32[]{:S(2)}, u32[]{:S(2)}) async-start(bf16[32,32,256]{2,1,0:T(8,128)(2,1)} %shard_map.68), calls=%async_computation.3 | async-start | bytes 1048576 | tf_op jit(solution)/shard_map/all_to_all | solution.py:285
  155.9 11.5 %all-to-all-start = ((bf16[4,96,256]{2,1,0:T(8,128)(2,1)}), bf16[4,96,256]{2,1,0:T(8,128)(2,1)S(1)}, u32[]{:S(2)}, u32[]{:S(2)}) async-start(bf16[4,96,256]{2,1,0:T(8,128)(2,1)} %bitcast.41), calls=%async_computation.1 | async-start | bytes 393216 | tf_op jit(solution)/shard_map/all_to_all | solution.py:287
Sparse Core Ops, SparseCore 0:
  96.3 51.4 reduce-scatter.1

commit v10 on v9

--- a/solution.py
+++ b/solution.py
@@ -70,27 +70,22 @@
     return [(i, (i + k) % n) for i in range(n)]
 
 
+def keyval_routes(k):
+    half = N_Z * N_Y // 2
+    return [
+        (s, N_Y * ((s % half) // 2) + (s % 2 + 2 * (s // half) + k) % N_Y) for s in range(2 * half)
+    ]
+
+
 def move_keyval(keyval):
     rows = keyval.shape[0]
     y_me = lax.axis_index("yh")
-    other = lax.ppermute(keyval, "yh", [(i, i ^ 1) for i in range(N_Y)])
-    low = y_me % 2 == 0
-    whole = jnp.concatenate(
-        [jnp.where(low, keyval, other), jnp.where(low, other, keyval)], axis=1
-    )
-    half = N_Z * N_Y // 2
-
-    def routes(flip):
-        return [
-            (s, N_Y * ((s % half) // 2) + s % 2 + 2 * ((s // half) ^ flip)) for s in range(2 * half)
-        ]
-
-    straight = lax.ppermute(whole, TENSOR, routes(0))
-    crossed = lax.ppermute(whole, TENSOR, routes(1))
-    first = y_me < 2
-    key = jnp.where(first, straight, crossed)
-    value = jnp.where(first, crossed, straight)
-    return key.reshape(rows, 1, HD), value.reshape(rows, 1, HD), whole
+    pieces = [lax.ppermute(keyval, TENSOR, keyval_routes(k)) for k in range(N_Y)]
+    stack = jnp.stack(pieces)
+    roles = [lax.dynamic_index_in_dim(stack, (y_me - r) % N_Y, 0, False) for r in range(N_Y)]
+    key = jnp.concatenate(roles[:2], axis=1).reshape(rows, 1, HD)
+    value = jnp.concatenate(roles[2:], axis=1).reshape(rows, 1, HD)
+    return key, value
 
 
 def sum_pieces(pieces):
@@ -271,8 +266,8 @@
     pieces.append(lax.ppermute(up[:half], "z", ring(N_Z, 1)))
     pieces.append(lax.ppermute(down[half:], "z", ring(N_Z, -1)))
     keyval = keyval_product(pieces, w_keyval.T)
-    key, value, whole = move_keyval(keyval)
-    query = product(pieces, w_query, False, jnp.float32, whole)
+    key, value = move_keyval(keyval)
+    query = product(pieces, w_query, False, jnp.float32, keyval)
 
     query_rot = rotate(query.reshape(SEQ, 2, HD), cosine, sine).astype(jnp.bfloat16)
     key_rot = rotate(key.astype(jnp.float32), cosine, sine).astype(jnp.bfloat16)

time: 177 us -> 180 us (1.017)
  blocking collectives: 36.3 us -> 42.3 us
  waiting for transfers between devices: 35.4 us -> 33 us
    all_to_all x1, blocking collectives: 20.8 us -> 26.8 us  [shards(): moving = lax.all_to_all(moving, TENSOR, 0, 0, tiled=True)]
    ppermute x3 -> x4, waiting for transfers between devices: 6.13 us -> 3.72 us  [move_keyval(): lax.ppermute(keyval, TENSOR, keyval_routes(k))]
    ppermute x3 -> x4, starting transfers between devices: 9.34 us -> 10.3 us  [move_keyval(): lax.ppermute(keyval, TENSOR, keyval_routes(k))]
  transfers between devices with their start and end apart: 14 -> 15, of which waited for: 8 -> 7; matrix products, arithmetic and copies ran while one was open for 2% -> 2% of each run, Pallas kernels for 1% -> 1%
where the time goes in v10:
time: 180 us; the launch traced here: 178 us
  starting transfers between devices  73.1 us (41%)
  blocking collectives  42.3 us (24%)
  waiting for transfers between devices  33 us (18%)
  between operations  13.8 us (8%)
  Pallas kernels  6.44 us (4%)
  local copies, waits for them, and re-layouts  6.31 us (4%)
  other arithmetic  2.56 us (1%)
    ppermute x3, starting transfers between devices, shards(): down = lax.ppermute(down, 'z', ring(N_Z, -1))  26.9 us
    all_to_all x1, blocking collectives, shards(): moving = lax.all_to_all(moving, TENSOR, 0, 0, tiled=True)  26.8 us
    all_to_all x1, starting transfers between devices, shards(): tails = lax.all_to_all(moving, DP, 0, 0, tiled=True)  19.8 us
    all_gather x1, blocking collectives, shards(): own = lax.all_gather(activations, 'yh', axis=1, tiled=True)  15.5 us
    ppermute x4, starting transfers between devices, move_keyval(): lax.ppermute(keyval, TENSOR, keyval_routes(k))  10.3 us
    reduce_scatter x1, waiting for transfers between devices, shards(): kept = lax.psum_scatter(kept.T, 'z', scatter_dimension=0, tiled=True).T  9.23 us
    all_to_all x1, waiting for transfers between devices, shards(): kept = sum_pieces(lax.all_to_all(kept, 'yh', 0, 0, tiled=True))  7.93 us
    all_to_all x1, waiting for transfers between devices, shards(): tails = lax.all_to_all(moving, DP, 0, 0, tiled=True)  5.86 us
  transfers between devices with their start and end apart: 15, of which 7 were waited for; matrix products, arithmetic and copies ran while one was open for 2% of the time, Pallas kernels for 1%

profile of v10, /device:TPU:1, one launch (start us, length us, event | category | flops | bytes accessed | tf_op | source)
XLA Modules:
  0.0 178.2 jit_solution(7310489577764200382)
XLA Ops:
  6.5 15.5 %all_gather.3.refs_0_ = bf16[128,1024]{1,0:T(8,128)(2,1)S(1)} all-gather(bf16[128,256]{1,0:T(8,128)(2,1)} %param.6), channel_id=1, replica_groups=mesh['x'=8,'yl'=2,'core'=2,'z'=8,'yh'=4] {'yh'}, dimensions={1}, use_global_device_ids=true | all-gather | bytes 327680 | tf_op jit(solution)/shard_map/all_gather | solution.py:258
  22.0 17.2 %collective-permute-start.1 = (bf16[128,1024]{1,0:T(8,128)(2,1)S(1)}, bf16[128,1024]{1,0:T(8,128)(2,1)S(1)}, u32[]{:S(2)}, u32[]{:S(2)}) collective-permute-start(bf16[128,1024]{1,0:T(8,128)(2,1)S(1)} %all_gather.3.refs_0_), channel_id=1, source_target_pairs={{0,28},{4,0},{8,4},{12,8},{16,12},{20,16},{24,20},{28,24},{1,29},{... | collective-permute-start | bytes 786440 | tf_op jit(solution)/shard_map/ppermute | solution.py:263
  39.2 1.9 %collective-permute-start = (bf16[128,1024]{1,0:T(8,128)(2,1)S(1)}, bf16[128,1024]{1,0:T(8,128)(2,1)S(1)}, u32[]{:S(2)}, u32[]{:S(2)}) collective-permute-start(bf16[128,1024]{1,0:T(8,128)(2,1)S(1)} %all_gather.3.refs_0_), channel_id=1, source_target_pairs={{0,4},{4,8},{8,12},{12,16},{16,20},{20,24},{24,28},{28,0},{1,5},{5... | collective-permute-start | bytes 786440 | tf_op jit(solution)/shard_map/ppermute | solution.py:262
  41.1 1.4 collective-permute-done.1.refs_2_
  42.5 5.0 %collective-permute-start.3 = (bf16[128,1024]{1,0:T(8,128)(2,1)S(1)}, bf16[128,1024]{1,0:T(8,128)(2,1)S(1)}, u32[]{:S(2)}, u32[]{:S(2)}) collective-permute-start(bf16[128,1024]{1,0:T(8,128)(2,1)S(1)} %collective-permute-done.1.refs_2_), channel_id=1, source_target_pairs={{0,28},{4,0},{8,4},{12,8},{16,12},{20,16},{24,20},{28,24},{1,29},{... | collective-permute-start | bytes 786440 | tf_op jit(solution)/shard_map/ppermute | solution.py:263
  47.5 1.9 %collective-permute-start.2 = (bf16[128,1024]{1,0:T(8,128)(2,1)S(1)}, bf16[128,1024]{1,0:T(8,128)(2,1)S(1)}, u32[]{:S(2)}, u32[]{:S(2)}) collective-permute-start(bf16[128,1024]{1,0:T(8,128)(2,1)S(1)} %collective-permute-done.refs_1_), channel_id=1, source_target_pairs={{0,4},{4,8},{8,12},{12,16},{16,20},{20,24},{24,28},{28,0},{1,5},{5... | collective-permute-start | bytes 786440 | tf_op jit(solution)/shard_map/ppermute | solution.py:262
  49.5 0.8 fusion.22
  50.2 0.7 slice.23
  50.9 0.1 pad_add_fusion
  51.0 0.1 convert_reduce_fusion
  51.1 4.7 %collective-permute-start.5 = (bf16[128,1024]{1,0:T(8,128)(2,1)S(1)}, bf16[128,1024]{1,0:T(8,128)(2,1)S(1)}, u32[]{:S(2)}, u32[]{:S(2)}) collective-permute-start(bf16[128,1024]{1,0:T(8,128)(2,1)S(1)} %collective-permute-done.3.refs_4_), channel_id=1, source_target_pairs={{0,28},{4,0},{8,4},{12,8},{16,12},{20,16},{24,20},{28,24},{1,29},{... | collective-permute-start | bytes 786440 | tf_op jit(solution)/shard_map/ppermute | solution.py:263
  55.9 1.9 %collective-permute-start.4 = (bf16[128,1024]{1,0:T(8,128)(2,1)S(1)}, bf16[128,1024]{1,0:T(8,128)(2,1)S(1)}, u32[]{:S(2)}, u32[]{:S(2)}) collective-permute-start(bf16[128,1024]{1,0:T(8,128)(2,1)S(1)} %collective-permute-done.2.refs_3_), channel_id=1, source_target_pairs={{0,4},{4,8},{8,12},{12,16},{16,20},{20,24},{24,28},{28,0},{1,5},{5... | collective-permute-start | bytes 786440 | tf_op jit(solution)/shard_map/ppermute | solution.py:262
  57.9 0.3 multiply_cosine_fusion
  58.2 0.9 collective-permute-done.5.refs_6_
  59.1 5.0 %collective-permute-start.7 = (bf16[64,1024]{1,0:T(8,128)(2,1)S(1)}, bf16[64,1024]{1,0:T(8,128)(2,1)S(1)}, u32[]{:S(2)}, u32[]{:S(2)}) collective-permute-start(bf16[64,1024]{1,0:T(8,128)(2,1)S(1)} %slice.29), channel_id=1, source_target_pairs={{0,28},{4,0},{8,4},{12,8},{16,12},{20,16},{24,20},{28,24},{1,29},{... | collective-permute-start | bytes 393224 | tf_op jit(solution)/shard_map/ppermute | solution.py:267
  64.2 1.9 %collective-permute-start.6 = (bf16[64,1024]{1,0:T(8,128)(2,1)S(1)}, bf16[64,1024]{1,0:T(8,128)(2,1)S(1)}, u32[]{:S(2)}, u32[]{:S(2)}) collective-permute-start(bf16[64,1024]{1,0:T(8,128)(2,1)S(1)} %slice.28), channel_id=1, source_target_pairs={{0,4},{4,8},{8,12},{12,16},{16,20},{20,24},{24,28},{28,0},{1,5},{5... | collective-permute-start | bytes 393224 | tf_op jit(solution)/shard_map/ppermute | solution.py:266
  66.1 0.1 compare_and_fusion.1
  66.2 1.2 copy-done.1
  67.5 0.6 shard_map.64
  68.1 3.9 %collective-permute-done.6.up_ref.refs_7_ = bf16[64,1024]{1,0:T(8,128)(2,1)S(1)} collective-permute-done((bf16[64,1024]{1,0:T(8,128)(2,1)S(1)}, bf16[64,1024]{1,0:T(8,128)(2,1)S(1)}, u32[]{:S(2)}, u32[]{:S(2)}) %collective-permute-start.6) | collective-permute-done | bytes 131104 | tf_op jit(solution)/shard_map/ppermute | solution.py:266
  72.0 0.2 shard_map.65.after_ref
  72.3 3.3 %collective-permute-start.11 = (bf16[128,64]{1,0:T(8,128)(2,1)S(1)}, bf16[128,64]{1,0:T(8,128)(2,1)S(1)}, u32[]{:S(2)}, u32[]{:S(2)}) collective-permute-start(bf16[128,64]{1,0:T(8,128)(2,1)S(1)} %shard_map.65.after_ref), channel_id=1, source_target_pairs={{0,3},{1,0},{2,7},{3,4},{4,11},{5,8},{6,15},{7,12},{8,19},{9,16},{... | collective-permute-start | bytes 49160 | tf_op jit(solution)/shard_map/ppermute | solution.py:83
  75.6 3.8 %collective-permute-start.10 = (bf16[128,64]{1,0:T(8,128)(2,1)S(1)}, bf16[128,64]{1,0:T(8,128)(2,1)S(1)}, u32[]{:S(2)}, u32[]{:S(2)}) collective-permute-start(bf16[128,64]{1,0:T(8,128)(2,1)S(1)} %shard_map.65.after_ref), channel_id=1, source_target_pairs={{0,2},{1,3},{2,6},{3,7},{4,10},{5,11},{6,14},{7,15},{8,18},{9,19},... | collective-permute-start | bytes 49160 | tf_op jit(solution)/shard_map/ppermute | solution.py:83
  79.4 2.5 %collective-permute-start.9 = (bf16[128,64]{1,0:T(8,128)(2,1)S(1)}, bf16[128,64]{1,0:T(8,128)(2,1)S(1)}, u32[]{:S(2)}, u32[]{:S(2)}) collective-permute-start(bf16[128,64]{1,0:T(8,128)(2,1)S(1)} %shard_map.65.after_ref), channel_id=1, source_target_pairs={{0,1},{1,2},{2,5},{3,6},{4,9},{5,10},{6,13},{7,14},{8,17},{9,18},{... | collective-permute-start | bytes 49160 | tf_op jit(solution)/shard_map/ppermute | solution.py:83
  81.9 0.7 collective-permute-start.8
  82.6 2.2 %copy-done = bf16[8192,256]{1,0:T(8,128)(2,1)S(1)} copy-done((bf16[8192,256]{1,0:T(8,128)(2,1)S(1)}, bf16[8192,256]{1,0:T(8,128)(2,1)}, u32[]{:S(2)}) %copy-start) | copy-done | bytes 4194328
  84.8 0.9 shard_map.66
  85.7 0.1 reshape.238
  85.7 0.2 fusion.25
  86.0 3.7 %collective-permute-done.9 = bf16[128,64]{1,0:T(8,128)(2,1)S(1)} collective-permute-done((bf16[128,64]{1,0:T(8,128)(2,1)S(1)}, bf16[128,64]{1,0:T(8,128)(2,1)S(1)}, u32[]{:S(2)}, u32[]{:S(2)}) %collective-permute-start.9) | collective-permute-done | bytes 16416 | tf_op jit(solution)/shard_map/ppermute | solution.py:83
  89.8 0.1 copy.17
  89.9 0.1 copy.18
  90.0 0.1 maximum_convert_fusion
  90.1 0.3 fusion.21
  90.4 0.3 fusion.26
  90.7 0.2 convolution_convert_fusion
  90.9 0.1 copy.25.attended_ref
  91.0 3.8 %shard_map.67 = (bf16[96,8192]{1,0:T(8,128)(2,1)}, bf16[32,32,256]{2,1,0:T(8,128)(2,1)S(1)}) custom-call(bf16[128,256]{1,0:T(8,128)(2,1)S(1)} %copy.25.attended_ref, bf16[256,8192]{1,0:T(8,128)(2,1)} %w_ref.1), custom_call_target="tpu_custom_call" | custom-call | tf_op jit(solution)/shard_map/pallas_call | solution.py:127
  94.8 26.8 %all_to_all.15.pieces_ref = bf16[32,32,256]{2,1,0:T(8,128)(2,1)S(1)} all-to-all(bf16[32,32,256]{2,1,0:T(8,128)(2,1)S(1)} %get-tuple-element.12), channel_id=1, replica_groups=mesh['x'=8,'yl'=2,'core'=2,'z'=8,'yh'=4] {'z','yh'}, dimensions={0} | all-to-all | bytes 1048576 | tf_op jit(solution)/shard_map/all_to_all | solution.py:278
  121.7 0.9 shard_map.68
  122.6 19.8 %all-to-all-start.2 = ((bf16[32,32,256]{2,1,0:T(8,128)(2,1)}), bf16[32,32,256]{2,1,0:T(8,128)(2,1)S(1)}, u32[]{:S(2)}, u32[]{:S(2)}) async-start(bf16[32,32,256]{2,1,0:T(8,128)(2,1)} %shard_map.68), calls=%async_computation.3 | async-start | bytes 1048576 | tf_op jit(solution)/shard_map/all_to_all | solution.py:280
  142.4 9.2 %reduce-scatter.2.cloned.1.call-done = bf16[1024,96]{0,1:T(8,128)(2,1)} async-done(((bf16[8192,96]{0,1:T(8,128)(2,1)}), bf16[1024,96]{0,1:T(8,128)(2,1)}) %reduce-scatter.2.cloned.1.call-update) | async-done | bytes 196624 | tf_op jit(solution)/shard_map/reduce_scatter | solution.py:277
  151.7 1.6 copy.34
  153.3 5.9 %all-to-all-done.2 = bf16[32,32,256]{2,1,0:T(8,128)(2,1)S(1)} async-done(((bf16[32,32,256]{2,1,0:T(8,128)(2,1)}), bf16[32,32,256]{2,1,0:T(8,128)(2,1)S(1)}, u32[]{:S(2)}, u32[]{:S(2)}) %all-to-all-start.2) | async-done | bytes 524320 | tf_op jit(solution)/shard_map/all_to_all | solution.py:280
  159.1 3.4 %all-to-all-start = ((bf16[4,96,256]{2,1,0:T(8,128)(2,1)}), bf16[4,96,256]{2,1,0:T(8,128)(2,1)S(1)}, u32[]{:S(2)}, u32[]{:S(2)}) async-start(bf16[4,96,256]{2,1,0:T(8,128)(2,1)} %bitcast.48), calls=%async_computation.1 | async-start | bytes 393216 | tf_op jit(solution)/shard_map/all_to_all | solution.py:282
  162.5 0.2 convolution_convert_fusion.1
  162.7 7.9 %all-to-all-done = bf16[4,96,256]{2,1,0:T(8,128)(2,1)S(1)} async-done(((bf16[4,96,256]{2,1,0:T(8,128)(2,1)}), bf16[4,96,256]{2,1,0:T(8,128)(2,1)S(1)}, u32[]{:S(2)}, u32[]{:S(2)}) %all-to-all-start) | async-done | bytes 196640 | tf_op jit(solution)/shard_map/all_to_all | solution.py:282
  170.7 0.6 pad_maximum_fusion.1
  (24 shorter events, 0.3 us)
Async XLA Ops:
  6.5 145.1 %reduce-scatter.2.cloned.1.call-start = ((), (), s32[]{:S(2)}) async-start(), calls=%async_computation.4 | async-start | bytes 1769472 | tf_op jit(solution)/shard_map/reduce_scatter | solution.py:277
  22.0 20.5 %collective-permute-start.1 = (bf16[128,1024]{1,0:T(8,128)(2,1)S(1)}, bf16[128,1024]{1,0:T(8,128)(2,1)S(1)}, u32[]{:S(2)}, u32[]{:S(2)}) collective-permute-start(bf16[128,1024]{1,0:T(8,128)(2,1)S(1)} %all_gather.3.refs_0_), channel_id=1, source_target_pairs={{0,28},{4,0},{8,4},{12,8},{16,12},{20,16},{24,20},{28,24},{1,29},{... | collective-permute-start | bytes 786440 | tf_op jit(solution)/shard_map/ppermute | solution.py:263
  39.2 8.3 %collective-permute-start = (bf16[128,1024]{1,0:T(8,128)(2,1)S(1)}, bf16[128,1024]{1,0:T(8,128)(2,1)S(1)}, u32[]{:S(2)}, u32[]{:S(2)}) collective-permute-start(bf16[128,1024]{1,0:T(8,128)(2,1)S(1)} %all_gather.3.refs_0_), channel_id=1, source_target_pairs={{0,4},{4,8},{8,12},{12,16},{16,20},{20,24},{24,28},{28,0},{1,5},{5... | collective-permute-start | bytes 786440 | tf_op jit(solution)/shard_map/ppermute | solution.py:262
  42.5 8.6 %collective-permute-start.3 = (bf16[128,1024]{1,0:T(8,128)(2,1)S(1)}, bf16[128,1024]{1,0:T(8,128)(2,1)S(1)}, u32[]{:S(2)}, u32[]{:S(2)}) collective-permute-start(bf16[128,1024]{1,0:T(8,128)(2,1)S(1)} %collective-permute-done.1.refs_2_), channel_id=1, source_target_pairs={{0,28},{4,0},{8,4},{12,8},{16,12},{20,16},{24,20},{28,24},{1,29},{... | collective-permute-start | bytes 786440 | tf_op jit(solution)/shard_map/ppermute | solution.py:263
  47.5 8.3 %collective-permute-start.2 = (bf16[128,1024]{1,0:T(8,128)(2,1)S(1)}, bf16[128,1024]{1,0:T(8,128)(2,1)S(1)}, u32[]{:S(2)}, u32[]{:S(2)}) collective-permute-start(bf16[128,1024]{1,0:T(8,128)(2,1)S(1)} %collective-permute-done.refs_1_), channel_id=1, source_target_pairs={{0,4},{4,8},{8,12},{12,16},{16,20},{20,24},{24,28},{28,0},{1,5},{5... | collective-permute-start | bytes 786440 | tf_op jit(solution)/shard_map/ppermute | solution.py:262
  51.1 8.0 %collective-permute-start.5 = (bf16[128,1024]{1,0:T(8,128)(2,1)S(1)}, bf16[128,1024]{1,0:T(8,128)(2,1)S(1)}, u32[]{:S(2)}, u32[]{:S(2)}) collective-permute-start(bf16[128,1024]{1,0:T(8,128)(2,1)S(1)} %collective-permute-done.3.refs_4_), channel_id=1, source_target_pairs={{0,28},{4,0},{8,4},{12,8},{16,12},{20,16},{24,20},{28,24},{1,29},{... | collective-permute-start | bytes 786440 | tf_op jit(solution)/shard_map/ppermute | solution.py:263
  55.9 8.3 %collective-permute-start.4 = (bf16[128,1024]{1,0:T(8,128)(2,1)S(1)}, bf16[128,1024]{1,0:T(8,128)(2,1)S(1)}, u32[]{:S(2)}, u32[]{:S(2)}) collective-permute-start(bf16[128,1024]{1,0:T(8,128)(2,1)S(1)} %collective-permute-done.2.refs_3_), channel_id=1, source_target_pairs={{0,4},{4,8},{8,12},{12,16},{16,20},{20,24},{24,28},{28,0},{1,5},{5... | collective-permute-start | bytes 786440 | tf_op jit(solution)/shard_map/ppermute | solution.py:262
  59.1 9.0 %collective-permute-start.7 = (bf16[64,1024]{1,0:T(8,128)(2,1)S(1)}, bf16[64,1024]{1,0:T(8,128)(2,1)S(1)}, u32[]{:S(2)}, u32[]{:S(2)}) collective-permute-start(bf16[64,1024]{1,0:T(8,128)(2,1)S(1)} %slice.29), channel_id=1, source_target_pairs={{0,28},{4,0},{8,4},{12,8},{16,12},{20,16},{24,20},{28,24},{1,29},{... | collective-permute-start | bytes 393224 | tf_op jit(solution)/shard_map/ppermute | solution.py:267
  64.2 7.8 %collective-permute-start.6 = (bf16[64,1024]{1,0:T(8,128)(2,1)S(1)}, bf16[64,1024]{1,0:T(8,128)(2,1)S(1)}, u32[]{:S(2)}, u32[]{:S(2)}) collective-permute-start(bf16[64,1024]{1,0:T(8,128)(2,1)S(1)} %slice.28), channel_id=1, source_target_pairs={{0,4},{4,8},{8,12},{12,16},{16,20},{20,24},{24,28},{28,0},{1,5},{5... | collective-permute-start | bytes 393224 | tf_op jit(solution)/shard_map/ppermute | solution.py:266
  66.2 1.2 copy-start.1
  72.3 13.7 %collective-permute-start.11 = (bf16[128,64]{1,0:T(8,128)(2,1)S(1)}, bf16[128,64]{1,0:T(8,128)(2,1)S(1)}, u32[]{:S(2)}, u32[]{:S(2)}) collective-permute-start(bf16[128,64]{1,0:T(8,128)(2,1)S(1)} %shard_map.65.after_ref), channel_id=1, source_target_pairs={{0,3},{1,0},{2,7},{3,4},{4,11},{5,8},{6,15},{7,12},{8,19},{9,16},{... | collective-permute-start | bytes 49160 | tf_op jit(solution)/shard_map/ppermute | solution.py:83
  75.6 10.4 %collective-permute-start.10 = (bf16[128,64]{1,0:T(8,128)(2,1)S(1)}, bf16[128,64]{1,0:T(8,128)(2,1)S(1)}, u32[]{:S(2)}, u32[]{:S(2)}) collective-permute-start(bf16[128,64]{1,0:T(8,128)(2,1)S(1)} %shard_map.65.after_ref), channel_id=1, source_target_pairs={{0,2},{1,3},{2,6},{3,7},{4,10},{5,11},{6,14},{7,15},{8,18},{9,19},... | collective-permute-start | bytes 49160 | tf_op jit(solution)/shard_map/ppermute | solution.py:83
  79.4 10.4 %collective-permute-start.9 = (bf16[128,64]{1,0:T(8,128)(2,1)S(1)}, bf16[128,64]{1,0:T(8,128)(2,1)S(1)}, u32[]{:S(2)}, u32[]{:S(2)}) collective-permute-start(bf16[128,64]{1,0:T(8,128)(2,1)S(1)} %shard_map.65.after_ref), channel_id=1, source_target_pairs={{0,1},{1,2},{2,5},{3,6},{4,9},{5,10},{6,13},{7,14},{8,17},{9,18},{... | collective-permute-start | bytes 49160 | tf_op jit(solution)/shard_map/ppermute | solution.py:83
  81.9 7.8 %collective-permute-start.8 = (bf16[128,64]{1,0:T(8,128)(2,1)S(1)}, bf16[128,64]{1,0:T(8,128)(2,1)S(1)}, u32[]{:S(2)}, u32[]{:S(2)}) collective-permute-start(bf16[128,64]{1,0:T(8,128)(2,1)S(1)} %shard_map.65.after_ref), channel_id=1, source_target_pairs={{0,0},{1,1},{2,4},{3,5},{4,8},{5,9},{6,12},{7,13},{8,16},{9,17},{1... | collective-permute-start | bytes 49160 | tf_op jit(solution)/shard_map/ppermute | solution.py:83
  82.6 2.2 %copy-start = (bf16[8192,256]{1,0:T(8,128)(2,1)S(1)}, bf16[8192,256]{1,0:T(8,128)(2,1)}, u32[]{:S(2)}) copy-start(bf16[8192,256]{1,0:T(8,128)(2,1)} %refs_9_.1) | copy-start | bytes 12582916
  91.0 71.5 %copy-start.2 = (s32[1024]{0:T(1024)S(1)}, s32[1024]{0:T(1024)}, u32[]{:S(2)}) copy-start(s32[1024]{0:T(1024)} %param.10) | copy-start | bytes 12292
  122.6 36.6 %all-to-all-start.2 = ((bf16[32,32,256]{2,1,0:T(8,128)(2,1)}), bf16[32,32,256]{2,1,0:T(8,128)(2,1)S(1)}, u32[]{:S(2)}, u32[]{:S(2)}) async-start(bf16[32,32,256]{2,1,0:T(8,128)(2,1)} %shard_map.68), calls=%async_computation.3 | async-start | bytes 1048576 | tf_op jit(solution)/shard_map/all_to_all | solution.py:280
  159.1 11.5 %all-to-all-start = ((bf16[4,96,256]{2,1,0:T(8,128)(2,1)}), bf16[4,96,256]{2,1,0:T(8,128)(2,1)S(1)}, u32[]{:S(2)}, u32[]{:S(2)}) async-start(bf16[4,96,256]{2,1,0:T(8,128)(2,1)} %bitcast.48), calls=%async_computation.1 | async-start | bytes 393216 | tf_op jit(solution)/shard_map/all_to_all | solution.py:282
Sparse Core Ops, SparseCore 0:
  95.0 56.6 reduce-scatter.1
